TPU v7x, 512 devices: a whole 4x4x16 slice. The times are simulated.
512 devices in a mesh: wide: 64 (over x_hi, z, core), narrow: 8 (over y, x_lo).
Axes of the slice: x: 4 (x_hi: 2, x_lo: 2; x = x_hi * 2 + x_lo), y: 4, z: 16, core: 2. Of those that a mesh axis runs over, the one named last changes fastest.
Arguments:
- density: bfloat16 [1024, 24, 128, 128], P('wide', 'narrow'), may hold values from -2 to 2
- block_list: int32 [1024, 24], replicated, may hold values from -1 to 127, as said below
- product_list: int32 [256, 24], replicated, may hold values from -1 to 127, as said below
Outputs:
- square: bfloat16 [256, 24, 128, 128], P('wide', 'narrow')
- cube: bfloat16 [256, 24, 128, 128], P('wide', 'narrow')
Inputs may be any that keep to these rules, and one draw needn't show every extreme that they name: `block_list`: within one block row and one index of narrow the live entries are distinct and stand before the empty ones; each such group has at least one live entry, some group has 3 and some exactly one. The global block column of a live entry lies within cyclic distance 16 of the block row: (column - row) mod 1024 is below 16 or at least 1008. `product_list`: within one product row and one index of narrow the live entries are distinct and stand before the empty ones; each such group has at least one live entry, some group has 3 and some exactly one. The global block column of a live entry lies within cyclic distance 16 of the product row's block row, as for block_list.
All inputs are finite; a program needn't handle non-finite values.
Results may differ from a plain program's by a relative error of at most 0.0049.
Values may be sent and summed in bfloat16 or wider, within the bound.
No kernel may reach another device: no remote copies, remote signals or barrier semaphores. Data moves between devices by JAX's collectives and lax.ppermute only.
A program may use at most 64 MiB of HBM per device.

v0:
```python
import jax
import jax.numpy as jnp
from jax import lax
from jax.sharding import PartitionSpec as P


def shifted(x, axis, by):
    peers = lax.axis_size(axis)
    return lax.ppermute(x, axis, [(i, (i + by) % peers) for i in range(peers)])


def fetch_neighbours(kept):
    below = shifted(kept, "wide", 1)
    above = shifted(kept, "wide", -1)
    return jnp.concatenate([below, kept, above], axis=0)


def per_device(density, block_list, product_list):
    narrow_count = lax.axis_size("narrow")
    wide_count = lax.axis_size("wide")
    rows_dev = density.shape[0]
    capacity = density.shape[1]
    block_size = density.shape[2]
    total_rows = block_list.shape[0]
    window = product_list.shape[0] // wide_count
    out_slots = product_list.shape[1] // narrow_count
    wide_at = lax.axis_index("wide")
    narrow_at = lax.axis_index("narrow")
    kept_live = block_list >= 0
    entry_device = jnp.arange(narrow_count * capacity, dtype=jnp.int32) // capacity
    kept_cols = jnp.maximum(block_list, 0) * narrow_count + entry_device[None, :]
    own_live = lax.dynamic_slice(
        kept_live, (wide_at * rows_dev, narrow_at * capacity), (rows_dev, capacity)
    )
    kept = density * own_live[:, :, None, None].astype(jnp.bfloat16)
    local_rows = jnp.arange(window, dtype=jnp.int32) * (rows_dev // window)
    block_rows = wide_at * rows_dev + local_rows
    window_lists = lax.dynamic_slice_in_dim(product_list, wide_at * window, window, 0)
    target_live = window_lists >= 0
    target_device = jnp.arange(narrow_count * out_slots, dtype=jnp.int32) // out_slots
    target_cols = jnp.maximum(window_lists, 0) * narrow_count + target_device[None, :]
    own_target_cols = lax.dynamic_slice_in_dim(target_cols, narrow_at * out_slots, out_slots, 1)
    own_target_live = lax.dynamic_slice_in_dim(target_live, narrow_at * out_slots, out_slots, 1)
    first_row = wide_at * rows_dev - rows_dev

    def multiply(extended, left_blocks, left_cols, left_live):
        flat_blocks = extended.reshape(-1, block_size, block_size)

        def one_row(pieces):
            left_row, cols_row, live_row, goal_cols, goal_live = pieces
            safe_rows = jnp.where(live_row, cols_row, 0)
            nearby = jnp.where(live_row, jnp.mod(safe_rows - first_row, total_rows), 0)
            candidate_cols = lax.dynamic_slice_in_dim(
                kept_cols[safe_rows], narrow_at * capacity, capacity, 1
            )
            candidate_live = lax.dynamic_slice_in_dim(
                kept_live[safe_rows], narrow_at * capacity, capacity, 1
            )
            matches = (candidate_cols[:, None, :] == goal_cols[None, :, None]) & candidate_live[
                :, None, :
            ]
            matches = matches & live_row[:, None, None] & goal_live[None, :, None]
            chosen = jnp.argmax(matches, axis=2)
            present = jnp.any(matches, axis=2)
            right_blocks = flat_blocks[nearby[:, None] * capacity + chosen] * present[
                :, :, None, None
            ].astype(jnp.bfloat16)
            result_sum = jnp.einsum(
                "eab,eqbc->qac", left_row, right_blocks, preferred_element_type=jnp.float32
            )
            return (result_sum * goal_live[:, None, None].astype(jnp.float32)).astype(jnp.bfloat16)

        return lax.map(
            one_row, (left_blocks, left_cols, left_live, own_target_cols, own_target_live)
        )

    row_lists = lax.all_gather(kept[local_rows], "narrow", axis=1, tiled=True)
    extended = fetch_neighbours(kept)
    square_own = multiply(extended, row_lists, kept_cols[block_rows], kept_live[block_rows])
    square_rows = lax.all_gather(square_own, "narrow", axis=1, tiled=True)
    cube_source = fetch_neighbours(kept)
    cube_own = multiply(cube_source, square_rows, target_cols, target_live)
    return (square_own, cube_own)


def solution(mesh):
    placed = (P("wide", "narrow", None, None), P(), P())
    return jax.shard_map(
        per_device,
        mesh=mesh,
        in_specs=placed,
        out_specs=(P("wide", "narrow", None, None), P("wide", "narrow", None, None)),
        check_vma=False,
    )
```

profile of v0, /device:TPU:24, one launch (start us, length us, event | category | flops | bytes accessed | tf_op | source)
XLA Modules:
  0.0 272.7 jit_solution(4868845626367417619)
XLA Ops:
  13.5 13.3 %collective-permute-start.1 = (bf16[16,3,128,128]{3,2,1,0:T(8,128)(2,1)S(1)}, bf16[16,3,128,128]{3,2,1,0:T(8,128)(2,1)}, u32[]{:S(2)}, u32[]{:S(2)}) collective-permute-start(bf16[16,3,128,128]{3,2,1,0:T(8,128)(2,1)S(1)} %broadcast_multiply_fusion), channel_id=1, source_target_pairs={{0,504},{8,0},{16,8},{24,16},{32,24},{40,32},{48,40},{56,48},{64,5... | collective-permute-start | bytes 4718600 | tf_op jit(solution)/shard_map/ppermute | solution.py:9
  28.3 14.8 %collective-permute-done = bf16[16,3,128,128]{3,2,1,0:T(8,128)(2,1)} collective-permute-done((bf16[16,3,128,128]{3,2,1,0:T(8,128)(2,1)S(1)}, bf16[16,3,128,128]{3,2,1,0:T(8,128)(2,1)}, u32[]{:S(2)}, u32[]{:S(2)}) %collective-permute-start) | collective-permute-done | bytes 1572896 | tf_op jit(solution)/shard_map/ppermute | solution.py:9
  44.7 3.8 %pad_maximum_fusion = bf16[48,3,128,128]{3,2,1,0:T(8,128)(2,1)} fusion(bf16[16,3,128,128]{3,2,1,0:T(8,128)(2,1)} %collective-permute-done.1, bf16[16,3,128,128]{3,2,1,0:T(8,128)(2,1)S(1)} %broadcast_multiply_fusion, bf16[16,3,128,128]{3,2,1,0:T(8,128)(2,1)} %collective-permute-done), kind=kLoop, calls=%fused_computation.79 | loop fusion | flops 4718592 | bytes 9437184 | tf_op jit(solution)/shard_map/concatenate | solution.py:15
  48.6 52.4 %all-gather.6.cloned.1.call-done = bf16[4,24,128,128]{3,2,1,0:T(8,128)(2,1)} async-done(((bf16[4,3,128,128]{3,2,1,0:T(8,128)(2,1)}), bf16[4,24,128,128]{3,2,1,0:T(8,128)(2,1)}) %all-gather.6.cloned.1.call-update) | async-done | bytes 3145744 | tf_op jit(solution)/shard_map/all_gather | solution.py:77
  101.0 44.4 %while.24 = (s32[]{:T(128)}, bf16[4,3,128,128]{3,2,1,0:T(8,128)(2,1)S(1)}, pred[4,24]{1,0:T(4,128)(4,1)S(1)}, s32[4,24]{1,0:T(4,128)S(1)}, s32[]{:T(128)}, /*ind...) while((s32[]{:T(128)}, ...), condition=%wide.region_3.4_spmd, body=%wide.region_0.3_spmd.sunk | while | flops 303272736 | bytes 13095314 | solution.py:73
  103.5 3.3 %gather_fusion.2 = bf16[72,128,128]{2,1,0:T(8,128)(2,1)S(1)} fusion(bf16[144,128,128]{2,1,0:T(8,128)(2,1)} %get-tuple-element.594, s32[1024]{0:T(1024)S(1)} %pad_clamp_fusion.11), kind=kCustom, calls=%fused_computation.2.clone.1 | custom fusion | bytes 4718880 | tf_op jit(solution)/shard_map/while/body/eval_jaxpr/gather | solution.py:65
  106.8 2.5 copy.55
  109.3 2.7 fusion.85
  114.6 3.3 %gather_fusion.2 = bf16[72,128,128]{2,1,0:T(8,128)(2,1)S(1)} fusion(bf16[144,128,128]{2,1,0:T(8,128)(2,1)} %get-tuple-element.594, s32[1024]{0:T(1024)S(1)} %pad_clamp_fusion.11), kind=kCustom, calls=%fused_computation.2.clone.1 | custom fusion | bytes 4718880 | tf_op jit(solution)/shard_map/while/body/eval_jaxpr/gather | solution.py:65
  120.4 2.7 fusion.85
  125.7 3.3 %gather_fusion.2 = bf16[72,128,128]{2,1,0:T(8,128)(2,1)S(1)} fusion(bf16[144,128,128]{2,1,0:T(8,128)(2,1)} %get-tuple-element.594, s32[1024]{0:T(1024)S(1)} %pad_clamp_fusion.11), kind=kCustom, calls=%fused_computation.2.clone.1 | custom fusion | bytes 4718880 | tf_op jit(solution)/shard_map/while/body/eval_jaxpr/gather | solution.py:65
  131.5 2.7 fusion.85
  136.8 3.3 %gather_fusion.2 = bf16[72,128,128]{2,1,0:T(8,128)(2,1)S(1)} fusion(bf16[144,128,128]{2,1,0:T(8,128)(2,1)} %get-tuple-element.594, s32[1024]{0:T(1024)S(1)} %pad_clamp_fusion.11), kind=kCustom, calls=%fused_computation.2.clone.1 | custom fusion | bytes 4718880 | tf_op jit(solution)/shard_map/while/body/eval_jaxpr/gather | solution.py:65
  142.6 2.7 fusion.85
  146.2 74.4 %all-gather.4.cloned.1.call-done = bf16[4,24,128,128]{3,2,1,0:T(8,128)(2,1)} async-done(((bf16[4,3,128,128]{3,2,1,0:T(8,128)(2,1)}), bf16[4,24,128,128]{3,2,1,0:T(8,128)(2,1)}) %all-gather.4.cloned.1.call-update) | async-done | bytes 3145744 | tf_op jit(solution)/shard_map/all_gather | solution.py:80
  220.7 44.4 %while.25 = (s32[]{:T(128)}, bf16[4,3,128,128]{3,2,1,0:T(8,128)(2,1)S(1)}, pred[4,24]{1,0:T(4,128)(4,1)S(1)}, s32[4,24]{1,0:T(4,128)S(1)}, s32[]{:T(128)}, /*ind...) while((s32[]{:T(128)}, ...), condition=%wide.region_7.8_spmd, body=%wide.region_4.7_spmd.sunk | while | flops 303272736 | bytes 13095314 | solution.py:73
  223.1 3.3 %gather_fusion.5 = bf16[72,128,128]{2,1,0:T(8,128)(2,1)S(1)} fusion(bf16[144,128,128]{2,1,0:T(8,128)(2,1)} %get-tuple-element.633, s32[1024]{0:T(1024)S(1)} %pad_clamp_fusion.13), kind=kCustom, calls=%fused_computation.5.clone.1 | custom fusion | bytes 4718880 | tf_op jit(solution)/shard_map/while/body/eval_jaxpr/gather | solution.py:65
  229.0 2.7 fusion.93
  234.2 3.3 %gather_fusion.5 = bf16[72,128,128]{2,1,0:T(8,128)(2,1)S(1)} fusion(bf16[144,128,128]{2,1,0:T(8,128)(2,1)} %get-tuple-element.633, s32[1024]{0:T(1024)S(1)} %pad_clamp_fusion.13), kind=kCustom, calls=%fused_computation.5.clone.1 | custom fusion | bytes 4718880 | tf_op jit(solution)/shard_map/while/body/eval_jaxpr/gather | solution.py:65
  240.1 2.7 fusion.93
  245.3 3.3 %gather_fusion.5 = bf16[72,128,128]{2,1,0:T(8,128)(2,1)S(1)} fusion(bf16[144,128,128]{2,1,0:T(8,128)(2,1)} %get-tuple-element.633, s32[1024]{0:T(1024)S(1)} %pad_clamp_fusion.13), kind=kCustom, calls=%fused_computation.5.clone.1 | custom fusion | bytes 4718880 | tf_op jit(solution)/shard_map/while/body/eval_jaxpr/gather | solution.py:65
  251.2 2.7 fusion.93
  256.4 3.3 %gather_fusion.5 = bf16[72,128,128]{2,1,0:T(8,128)(2,1)S(1)} fusion(bf16[144,128,128]{2,1,0:T(8,128)(2,1)} %get-tuple-element.633, s32[1024]{0:T(1024)S(1)} %pad_clamp_fusion.13), kind=kCustom, calls=%fused_computation.5.clone.1 | custom fusion | bytes 4718880 | tf_op jit(solution)/shard_map/while/body/eval_jaxpr/gather | solution.py:65
  262.3 2.7 fusion.93
  (199 shorter events, 48.6 us)
Async XLA Ops:
  7.2 19.6 %copy-start = (s32[256,24]{0,1:T(8,128)S(1)}, s32[256,24]{0,1:T(8,128)}, u32[]{:S(2)}) copy-start(s32[256,24]{0,1:T(8,128)} %param.9) | copy-start | bytes 73732
  7.2 93.8 %all-gather.6.cloned.1.call-start = ((), (), s32[]{:S(2)}) async-start(), calls=%async_computation.1 | async-start | bytes 3538944 | tf_op jit(solution)/shard_map/all_gather | solution.py:77
  11.5 209.1 %all-gather.4.cloned.1.call-start = ((), (), s32[]{:S(2)}) async-start(), calls=%async_computation | async-start | bytes 3538944 | tf_op jit(solution)/shard_map/all_gather | solution.py:80
  11.5 31.6 %collective-permute-start = (bf16[16,3,128,128]{3,2,1,0:T(8,128)(2,1)S(1)}, bf16[16,3,128,128]{3,2,1,0:T(8,128)(2,1)}, u32[]{:S(2)}, u32[]{:S(2)}) collective-permute-start(bf16[16,3,128,128]{3,2,1,0:T(8,128)(2,1)S(1)} %broadcast_multiply_fusion), channel_id=1, source_target_pairs={{0,8},{8,16},{16,24},{24,32},{32,40},{40,48},{48,56},{56,64},{64,7... | collective-permute-start | bytes 4718600 | tf_op jit(solution)/shard_map/ppermute | solution.py:9
  13.5 31.3 %collective-permute-start.1 = (bf16[16,3,128,128]{3,2,1,0:T(8,128)(2,1)S(1)}, bf16[16,3,128,128]{3,2,1,0:T(8,128)(2,1)}, u32[]{:S(2)}, u32[]{:S(2)}) collective-permute-start(bf16[16,3,128,128]{3,2,1,0:T(8,128)(2,1)S(1)} %broadcast_multiply_fusion), channel_id=1, source_target_pairs={{0,504},{8,0},{16,8},{24,16},{32,24},{40,32},{48,40},{56,48},{64,5... | collective-permute-start | bytes 4718600 | tf_op jit(solution)/shard_map/ppermute | solution.py:9
  145.4 0.7 copy-start.1
  265.1 0.7 copy-start.2
Sparse Core Ops, SparseCore 0:
  11.6 89.3 all-gather.5
  146.3 74.2 all-gather.3
where the time goes:
time: 275 us; the launch traced here: 273 us
  waiting for transfers between devices  143 us (52%)
  local copies, waits for them, and re-layouts  66.8 us (24%)
  matrix products  21.3 us (8%)
  starting transfers between devices  15.3 us (6%)
  between operations  14.2 us (5%)
  other arithmetic  11.2 us (4%)
    all_gather x1, waiting for transfers between devices, per_device(): square_rows = lax.all_gather(square_own, 'narrow', axis=1, tiled=True)  74.4 us
    all_gather x1, waiting for transfers between devices, per_device(): row_lists = lax.all_gather(kept[local_rows], 'narrow', axis=1, tiled=True)  52.4 us
    gather x16, local copies, waits for them, and re-layouts, one_row(): flat_blocks[nearby[:, None] * capacity + chosen]  46.7 us
    dot_general x8, matrix products, one_row(): jnp.einsum('eab,eqbc->qac', left_row, right_blocks, preferred_element_typ...  21.3 us
    ppermute x2, waiting for transfers between devices, shifted(): return lax.ppermute(x, axis, [(i, (i + by) % peers) for i in range(peers)])  16.4 us
    ppermute x2, starting transfers between devices, shifted(): return lax.ppermute(x, axis, [(i, (i + by) % peers) for i in range(peers)])  15.2 us
  transfers between devices with their start and end apart: 4, of which 4 were waited for; matrix products, arithmetic and copies ran while one was open for 2% of the time, Pallas kernels for 0%

commit v1 on v0

v1 whole, which is shorter than its diff:
```python
import functools

import jax
import jax.numpy as jnp
from jax import lax
from jax.experimental import pallas as pl
from jax.experimental.pallas import tpu as pltpu
from jax.sharding import PartitionSpec as P

Y = 4
GROUP = 4
SOURCES = ((0, 0), (0, 1), (-1, 0), (1, 0), (2, 0), (-1, 1), (1, 1), (2, 1))
HALF = len(SOURCES) // 2


def shifted(x, axis, by):
    peers = lax.axis_size(axis)
    return lax.ppermute(x, axis, [(i, (i + by) % peers) for i in range(peers)])


def moved(a, dy, dx):
    pairs = []
    for n in range(2 * Y):
        y, x = divmod(n, 2)
        pairs.append((n, (y + dy) % Y * 2 + (x ^ dx)))
    return lax.ppermute(a, "narrow", pairs)


def gather_rows(own):
    partner = moved(own, 0, 1)
    lower = moved(own, 1, 0)
    upper = moved(own, -1, 0)
    partner_lower = moved(partner, 1, 0)
    partner_upper = moved(partner, -1, 0)
    far = moved(lower, 1, 0)
    partner_far = moved(partner_upper, -1, 0)
    return (own, partner, lower, upper), (far, partner_lower, partner_upper, partner_far)


def list_kernel(rows_dev, slots, window, total_rows, block_ref, product_ref, *rest):
    codes = rest[0:4]
    counts = rest[4:8]
    near, goals, sem = rest[8:11]
    wide_count = lax.axis_size("wide")
    narrow_count = lax.axis_size("narrow")
    wide_at = lax.axis_index("wide")
    narrow_at = lax.axis_index("narrow")
    copies = []
    for part in range(3):
        owner = lax.rem(wide_at + (part - 1 + wide_count), wide_count)
        copies.append(
            pltpu.make_async_copy(
                block_ref.at[pl.ds(owner * rows_dev, rows_dev)],
                near.at[pl.ds(part * rows_dev, rows_dev)],
                sem.at[part],
            )
        )
    copies.append(
        pltpu.make_async_copy(product_ref.at[pl.ds(wide_at * window, window)], goals, sem.at[3])
    )
    for copy in copies:
        copy.start()
    for copy in copies:
        copy.wait()
    step = rows_dev // window
    ext_rows = 3 * rows_dev - step
    capacity = HALF * slots
    left_pad = HALF * window * slots
    right_pad = ext_rows * slots
    pad = left_pad * 256 + right_pad
    y_at = narrow_at // 2
    x_at = lax.rem(narrow_at, 2)
    for which in range(4):
        stage, half = divmod(which, 2)
        code_ref, count_ref = codes[which], counts[which]

        def one_row(g, _, stage=stage, half=half, code_ref=code_ref, count_ref=count_ref):
            base = g * slots * capacity
            for i in range(slots * capacity):
                code_ref[base + i] = pad
            targets = [goals[g, narrow_at * slots + q] for q in range(slots)]
            found = [jnp.int32(0)] * slots
            for j in range(HALF):
                dy, dx = SOURCES[half * HALF + j]
                source = lax.rem(y_at + (dy + Y), Y) * 2 + lax.rem(x_at + dx, 2)
                for s in range(slots):
                    if stage == 0:
                        col = near[rows_dev + g * step, source * slots + s]
                    else:
                        col = goals[g, source * slots + s]
                    live = col >= 0
                    row = lax.rem(
                        col * narrow_count + source - wide_at * rows_dev + (rows_dev + total_rows),
                        total_rows,
                    )
                    row = jnp.where(live, jnp.minimum(row, ext_rows - 1), 0)
                    left = (j * window + g) * slots + s
                    for t in range(slots):
                        right_col = near[row, narrow_at * slots + t]
                        usable = live & (right_col >= 0)
                        code = left * 256 + row * slots + t
                        for q in range(slots):
                            hit = usable & (right_col == targets[q])

                            @pl.when(hit)
                            def _(q=q, code=code, at=found[q]):
                                code_ref[base + q * capacity + at] = code

                            found[q] = found[q] + hit.astype(jnp.int32)
            most = found[0]
            for q in range(1, slots):
                most = jnp.maximum(most, found[q])
            count_ref[g] = (most + (GROUP - 1)) // GROUP
            return 0

        lax.fori_loop(0, window, one_row, 0)


def build_lists(block_list, product_list, rows_dev, slots, window):
    total_rows = block_list.shape[0]
    capacity = HALF * slots
    codes = jax.ShapeDtypeStruct((window * slots * capacity,), jnp.int32)
    counts = jax.ShapeDtypeStruct((window,), jnp.int32)
    outs = pl.pallas_call(
        functools.partial(list_kernel, rows_dev, slots, window, total_rows),
        out_shape=[codes] * 4 + [counts] * 4,
        in_specs=[pl.BlockSpec(memory_space=pl.ANY)] * 2,
        out_specs=[pl.BlockSpec(memory_space=pltpu.SMEM)] * 8,
        scratch_shapes=[
            pltpu.SMEM((3 * rows_dev, block_list.shape[1]), jnp.int32),
            pltpu.SMEM((window, product_list.shape[1]), jnp.int32),
            pltpu.SemaphoreType.DMA((4,)),
        ],
        name="pair_lists",
        cost_estimate=pl.CostEstimate(flops=0, bytes_accessed=3_000_000, transcendentals=0),
    )(block_list, product_list)
    return [(outs[i], outs[4 + i]) for i in range(4)]


def product_kernel(window, slots, ext_rows, first, code_ref, count_ref, *rest):
    lefts = rest[:HALF]
    below, own, above = rest[HALF : HALF + 3]
    rest = rest[HALF + 3 :]
    if not first:
        start_ref, rest = rest[0], rest[1:]
    out_ref, left_buf, right_buf, total, sem = rest
    rows_dev = own.shape[0]
    step = rows_dev // window
    capacity = HALF * slots
    left_pad = HALF * window * slots
    right_pad = ext_rows * slots
    copies = []
    for j in range(HALF):
        copies.append((lefts[j], left_buf.at[pl.ds(j * window, window)]))
    copies.append((below, right_buf.at[pl.ds(0, rows_dev)]))
    copies.append((own, right_buf.at[pl.ds(rows_dev, rows_dev)]))
    tail = ext_rows - 2 * rows_dev
    copies.append((above.at[pl.ds(0, tail)], right_buf.at[pl.ds(2 * rows_dev, tail)]))
    if not first:
        copies.append((start_ref, total))
    copies = [pltpu.make_async_copy(a, b, sem.at[i]) for i, (a, b) in enumerate(copies)]
    for copy in copies:
        copy.start()
    left_buf[HALF * window] = jnp.zeros(left_buf.shape[1:], left_buf.dtype)
    right_buf[ext_rows] = jnp.zeros(right_buf.shape[1:], right_buf.dtype)
    if first:
        total[...] = jnp.zeros_like(total)
    for copy in copies:
        copy.wait()

    def one_row(g, _):
        def one_group(i, _):
            for q in range(slots):
                at = (g * slots + q) * capacity + i * GROUP
                left, right = [], []
                for m in range(GROUP):
                    code = code_ref[at + m]
                    l, r = code // 256, lax.rem(code, 256)
                    left.append(left_buf[l // slots, lax.rem(l, slots)])
                    right.append(right_buf[r // slots, lax.rem(r, slots)])
                total[g, q] += jnp.dot(
                    jnp.concatenate(left, axis=1),
                    jnp.concatenate(right, axis=0),
                    preferred_element_type=jnp.float32,
                )
            return 0

        lax.fori_loop(0, count_ref[g], one_group, 0)
        return 0

    lax.fori_loop(0, window, one_row, 0)
    out_ref[...] = total[...].astype(out_ref.dtype)


def multiply(lists, lefts, rights, start, window, slots, out_type):
    code, count = lists
    block = lefts[0].shape[2:]
    rows_dev = rights[1].shape[0]
    ext_rows = 3 * rows_dev - rows_dev // window
    first = start is None
    anywhere = pl.BlockSpec(memory_space=pl.ANY)
    scalar = pl.BlockSpec(memory_space=pltpu.SMEM)
    extra = () if first else (start,)
    return pl.pallas_call(
        functools.partial(product_kernel, window, slots, ext_rows, first),
        out_shape=jax.ShapeDtypeStruct((window, slots) + block, out_type),
        in_specs=[scalar] * 2 + [anywhere] * (HALF + 3 + len(extra)),
        out_specs=pl.BlockSpec(memory_space=pltpu.VMEM),
        scratch_shapes=[
            pltpu.VMEM((HALF * window + 1, slots) + block, jnp.bfloat16),
            pltpu.VMEM((ext_rows + 1, slots) + block, jnp.bfloat16),
            pltpu.VMEM((window, slots) + block, jnp.float32),
            pltpu.SemaphoreType.DMA((HALF + 4,)),
        ],
        compiler_params=pltpu.CompilerParams(vmem_limit_bytes=24 * 1024 * 1024),
        name="block_products",
        cost_estimate=pl.CostEstimate(
            flops=300_000_000, bytes_accessed=8_000_000, transcendentals=0
        ),
    )(code, count, *lefts, *rights, *extra)


def per_device(density, block_list, product_list):
    rows_dev, slots = density.shape[:2]
    window = product_list.shape[0] // lax.axis_size("wide")
    step = rows_dev // window
    lists = build_lists(block_list, product_list, rows_dev, slots, window)
    local = density.reshape((window, step) + density.shape[1:])[:, 0]
    early, late = gather_rows(local)
    rights = (shifted(density, "wide", 1), density, shifted(density, "wide", -1))
    part = multiply(lists[0], early, rights, None, window, slots, jnp.float32)
    square = multiply(lists[1], late, rights, part, window, slots, jnp.bfloat16)
    early, late = gather_rows(square)
    part = multiply(lists[2], early, rights, None, window, slots, jnp.float32)
    cube = multiply(lists[3], late, rights, part, window, slots, jnp.bfloat16)
    return square, cube


def solution(mesh):
    placed = P("wide", "narrow", None, None)
    return jax.shard_map(
        per_device,
        mesh=mesh,
        in_specs=(placed, P(), P()),
        out_specs=(placed, placed),
        check_vma=False,
    )
```

time: 275 us -> 127 us (0.46)
  the two profiles are of different devices: /device:TPU:24 before, /device:TPU:4 now
where the time goes in v1:
time: 127 us; the launch traced here: 126 us
  starting transfers between devices  59.4 us (47%)
  Pallas kernels  30.2 us (24%)
  waiting for transfers between devices  27.3 us (21%)
  local copies, waits for them, and re-layouts  8.48 us (7%)
    ppermute x14, starting transfers between devices, moved(): return lax.ppermute(a, 'narrow', pairs)  46.5 us
    ppermute x14, waiting for transfers between devices, moved(): return lax.ppermute(a, 'narrow', pairs)  27.3 us
    pallas_call x4, Pallas kernels, multiply(): pl.pallas_call(functools.partial(product_kernel, window, slots, ext_rows,...  21.1 us
    ppermute x2, starting transfers between devices, shifted(): return lax.ppermute(x, axis, [(i, (i + by) % peers) for i in range(peers)])  12.8 us
    pallas_call x1, Pallas kernels, build_lists(): pl.pallas_call(functools.partial(list_kernel, rows_dev, slots, window, to...  9.14 us
    unnamed x26, local copies, waits for them, and re-layouts  7.45 us
  transfers between devices with their start and end apart: 16, of which 5 were waited for; matrix products, arithmetic and copies ran while one was open for 3% of the time, Pallas kernels for 15%

profile of v1, /device:TPU:4, one launch (start us, length us, event | category | flops | bytes accessed | tf_op | source)
XLA Modules:
  0.0 126.3 jit_solution(10176443261091436210)
XLA Ops:
  0.6 2.1 %collective-permute-start.6 = (bf16[16,3,128,128]{3,2,1,0:T(8,128)(2,1)}, bf16[16,3,128,128]{3,2,1,0:T(8,128)(2,1)S(1)}, u32[]{:S(2)}, u32[]{:S(2)}) collective-permute-start(bf16[16,3,128,128]{3,2,1,0:T(8,128)(2,1)} %rest_5_.7), channel_id=1, source_target_pairs={{0,8},{8,16},{16,24},{24,32},{32,40},{40,48},{48,56},{56,64},{64,7... | collective-permute-start | bytes 4718600 | tf_op jit(solution)/shard_map/ppermute | solution.py:18
  2.7 10.8 %collective-permute-start.7 = (bf16[16,3,128,128]{3,2,1,0:T(8,128)(2,1)}, bf16[16,3,128,128]{3,2,1,0:T(8,128)(2,1)}, u32[]{:S(2)}, u32[]{:S(2)}) collective-permute-start(bf16[16,3,128,128]{3,2,1,0:T(8,128)(2,1)} %rest_5_.7), channel_id=1, source_target_pairs={{0,504},{8,0},{16,8},{24,16},{32,24},{40,32},{48,40},{56,48},{64,5... | collective-permute-start | bytes 4718600 | tf_op jit(solution)/shard_map/ppermute | solution.py:18
  14.5 4.0 %collective-permute-start.2 = (bf16[4,3,128,128]{3,2,1,0:T(8,128)(2,1)S(1)}, bf16[4,3,128,128]{3,2,1,0:T(8,128)(2,1)}, u32[]{:S(2)}, u32[]{:S(2)}) collective-permute-start(bf16[4,3,128,128]{3,2,1,0:T(8,128)(2,1)S(1)} %slice_bitcast_fusion.rest_0_), channel_id=1, source_target_pairs={{0,1},{1,0},{2,3},{3,2},{4,5},{5,4},{6,7},{7,6},{8,9},{9,8},{10,11... | collective-permute-start | bytes 1179656 | tf_op jit(solution)/shard_map/ppermute | solution.py:26
  18.5 3.5 %collective-permute-start = (bf16[4,3,128,128]{3,2,1,0:T(8,128)(2,1)S(1)}, bf16[4,3,128,128]{3,2,1,0:T(8,128)(2,1)}, u32[]{:S(2)}, u32[]{:S(2)}) collective-permute-start(bf16[4,3,128,128]{3,2,1,0:T(8,128)(2,1)S(1)} %slice_bitcast_fusion.rest_0_), channel_id=1, source_target_pairs={{0,2},{1,3},{2,4},{3,5},{4,6},{5,7},{6,0},{7,1},{8,10},{9,11},{10,... | collective-permute-start | bytes 1179656 | tf_op jit(solution)/shard_map/ppermute | solution.py:26
  22.0 3.6 %collective-permute-start.8 = (bf16[4,3,128,128]{3,2,1,0:T(8,128)(2,1)S(1)}, bf16[4,3,128,128]{3,2,1,0:T(8,128)(2,1)S(1)}, u32[]{:S(2)}, u32[]{:S(2)}) collective-permute-start(bf16[4,3,128,128]{3,2,1,0:T(8,128)(2,1)S(1)} %slice_bitcast_fusion.rest_0_), channel_id=1, source_target_pairs={{0,6},{1,7},{2,0},{3,1},{4,2},{5,3},{6,4},{7,5},{8,14},{9,15},{10,... | collective-permute-start | bytes 1179656 | tf_op jit(solution)/shard_map/ppermute | solution.py:26
  25.6 11.9 %collective-permute-done.2.rest_1_ = bf16[4,3,128,128]{3,2,1,0:T(8,128)(2,1)} collective-permute-done((bf16[4,3,128,128]{3,2,1,0:T(8,128)(2,1)S(1)}, bf16[4,3,128,128]{3,2,1,0:T(8,128)(2,1)}, u32[]{:S(2)}, u32[]{:S(2)}) %collective-permute-start.2) | collective-permute-done | bytes 393248 | tf_op jit(solution)/shard_map/ppermute | solution.py:26
  37.6 4.9 %collective-permute-start.4 = (bf16[4,3,128,128]{3,2,1,0:T(8,128)(2,1)}, bf16[4,3,128,128]{3,2,1,0:T(8,128)(2,1)}, u32[]{:S(2)}, u32[]{:S(2)}) collective-permute-start(bf16[4,3,128,128]{3,2,1,0:T(8,128)(2,1)} %collective-permute-done.2.rest_1_), channel_id=1, source_target_pairs={{0,6},{1,7},{2,0},{3,1},{4,2},{5,3},{6,4},{7,5},{8,14},{9,15},{10,... | collective-permute-start | bytes 1179656 | tf_op jit(solution)/shard_map/ppermute | solution.py:26
  42.5 1.9 %collective-permute-start.3 = (bf16[4,3,128,128]{3,2,1,0:T(8,128)(2,1)}, bf16[4,3,128,128]{3,2,1,0:T(8,128)(2,1)}, u32[]{:S(2)}, u32[]{:S(2)}) collective-permute-start(bf16[4,3,128,128]{3,2,1,0:T(8,128)(2,1)} %collective-permute-done.2.rest_1_), channel_id=1, source_target_pairs={{0,2},{1,3},{2,4},{3,5},{4,6},{5,7},{6,0},{7,1},{8,10},{9,11},{10,... | collective-permute-start | bytes 1179656 | tf_op jit(solution)/shard_map/ppermute | solution.py:26
  45.2 2.5 %collective-permute-start.1 = (bf16[4,3,128,128]{3,2,1,0:T(8,128)(2,1)}, bf16[4,3,128,128]{3,2,1,0:T(8,128)(2,1)}, u32[]{:S(2)}, u32[]{:S(2)}) collective-permute-start(bf16[4,3,128,128]{3,2,1,0:T(8,128)(2,1)} %collective-permute-done.rest_2_), channel_id=1, source_target_pairs={{0,2},{1,3},{2,4},{3,5},{4,6},{5,7},{6,0},{7,1},{8,10},{9,11},{10,... | collective-permute-start | bytes 1179656 | tf_op jit(solution)/shard_map/ppermute | solution.py:26
  47.7 2.1 %collective-permute-done.4.rest_2_ = bf16[4,3,128,128]{3,2,1,0:T(8,128)(2,1)} collective-permute-done((bf16[4,3,128,128]{3,2,1,0:T(8,128)(2,1)}, bf16[4,3,128,128]{3,2,1,0:T(8,128)(2,1)}, u32[]{:S(2)}, u32[]{:S(2)}) %collective-permute-start.4) | collective-permute-done | bytes 393248 | tf_op jit(solution)/shard_map/ppermute | solution.py:26
  49.7 5.6 %collective-permute-start.5 = (bf16[4,3,128,128]{3,2,1,0:T(8,128)(2,1)}, bf16[4,3,128,128]{3,2,1,0:T(8,128)(2,1)}, u32[]{:S(2)}, u32[]{:S(2)}) collective-permute-start(bf16[4,3,128,128]{3,2,1,0:T(8,128)(2,1)} %collective-permute-done.4.rest_2_), channel_id=1, source_target_pairs={{0,6},{1,7},{2,0},{3,1},{4,2},{5,3},{6,4},{7,5},{8,14},{9,15},{10,... | collective-permute-start | bytes 1179656 | tf_op jit(solution)/shard_map/ppermute | solution.py:26
  58.7 9.1 %pair_lists.1 = (s32[144]{0:T(256)}, s32[144]{0:T(256)}, s32[144]{0:T(256)}, s32[144]{0:T(256)}, s32[4]{0:T(128)}, /*index=5*/s32[4]{0:T(128)}, s32[4]{0:T(128)}, s32[4]{0:T(128)}) custom-call(s32[1024,24]{1,0:T(8,128)} %copy.7.block_ref, s32[256,24]{1,0:T(8,128)} %copy.8.product_ref), custom_call_target="tpu_custom_call" | custom-call | bytes 3000000 | tf_op jit(solution)/shard_map/pair_lists/pallas_call | solution.py:124
  70.2 5.0 %block_products.4.rest_7_ = f32[4,3,128,128]{3,2,1,0:T(8,128)S(1)} custom-call(s32[144]{0:T(256)S(1)} %copy-done.7, s32[4]{0:T(128)S(1)} %copy-done.11, bf16[4,3,128,128]{3,2,1,0:T(8,128)(2,1)S(1)} %slice_bitcast_fusion.rest_0_, bf16[4,3,128,128]{3,2,1,0:T(8,128)(2,1)} %collective-permute-done.2.rest_1_, ...), custom_call_target="tpu_custom_call" | custom-call | flops 300000000 | bytes 8000000 | tf_op jit(solution)/shard_map/block_products/pallas_call | solution.py:204
  75.2 4.8 %block_products.5.rest_0_ = bf16[4,3,128,128]{3,2,1,0:T(8,128)(2,1)} custom-call(s32[144]{0:T(256)S(1)} %copy-done.5, s32[4]{0:T(128)S(1)} %copy-done.10, bf16[4,3,128,128]{3,2,1,0:T(8,128)(2,1)} %collective-permute-done.1.rest_0_, bf16[4,3,128,128]{3,2,1,0:T(8,128)(2,1)} %collective-permute-done.3.rest_1_, ...), custom_call_target="tpu_custom_call" | custom-call | flops 300000000 | bytes 8000000 | tf_op jit(solution)/shard_map/block_products/pallas_call | solution.py:204
  80.1 3.9 %collective-permute-start.11 = (bf16[4,3,128,128]{3,2,1,0:T(8,128)(2,1)}, bf16[4,3,128,128]{3,2,1,0:T(8,128)(2,1)S(1)}, u32[]{:S(2)}, u32[]{:S(2)}) collective-permute-start(bf16[4,3,128,128]{3,2,1,0:T(8,128)(2,1)} %block_products.5.rest_0_), channel_id=1, source_target_pairs={{0,1},{1,0},{2,3},{3,2},{4,5},{5,4},{6,7},{7,6},{8,9},{9,8},{10,11... | collective-permute-start | bytes 1179656 | tf_op jit(solution)/shard_map/ppermute | solution.py:26
  83.9 1.9 %collective-permute-start.9 = (bf16[4,3,128,128]{3,2,1,0:T(8,128)(2,1)}, bf16[4,3,128,128]{3,2,1,0:T(8,128)(2,1)S(1)}, u32[]{:S(2)}, u32[]{:S(2)}) collective-permute-start(bf16[4,3,128,128]{3,2,1,0:T(8,128)(2,1)} %block_products.5.rest_0_), channel_id=1, source_target_pairs={{0,2},{1,3},{2,4},{3,5},{4,6},{5,7},{6,0},{7,1},{8,10},{9,11},{10,... | collective-permute-start | bytes 1179656 | tf_op jit(solution)/shard_map/ppermute | solution.py:26
  85.9 5.7 %collective-permute-done.11.rest_1_ = bf16[4,3,128,128]{3,2,1,0:T(8,128)(2,1)S(1)} collective-permute-done((bf16[4,3,128,128]{3,2,1,0:T(8,128)(2,1)}, bf16[4,3,128,128]{3,2,1,0:T(8,128)(2,1)S(1)}, u32[]{:S(2)}, u32[]{:S(2)}) %collective-permute-start.11) | collective-permute-done | bytes 393248 | tf_op jit(solution)/shard_map/ppermute | solution.py:26
  95.4 3.9 %collective-permute-start.12 = (bf16[4,3,128,128]{3,2,1,0:T(8,128)(2,1)S(1)}, bf16[4,3,128,128]{3,2,1,0:T(8,128)(2,1)S(1)}, u32[]{:S(2)}, u32[]{:S(2)}) collective-permute-start(bf16[4,3,128,128]{3,2,1,0:T(8,128)(2,1)S(1)} %collective-permute-done.11.rest_1_), channel_id=1, source_target_pairs={{0,2},{1,3},{2,4},{3,5},{4,6},{5,7},{6,0},{7,1},{8,10},{9,11},{10,... | collective-permute-start | bytes 1179656 | tf_op jit(solution)/shard_map/ppermute | solution.py:26
  99.4 3.9 %collective-permute-start.10 = (bf16[4,3,128,128]{3,2,1,0:T(8,128)(2,1)S(1)}, bf16[4,3,128,128]{3,2,1,0:T(8,128)(2,1)S(1)}, u32[]{:S(2)}, u32[]{:S(2)}) collective-permute-start(bf16[4,3,128,128]{3,2,1,0:T(8,128)(2,1)S(1)} %collective-permute-done.9.rest_2_), channel_id=1, source_target_pairs={{0,2},{1,3},{2,4},{3,5},{4,6},{5,7},{6,0},{7,1},{8,10},{9,11},{10,... | collective-permute-start | bytes 1179656 | tf_op jit(solution)/shard_map/ppermute | solution.py:26
  103.3 2.2 %collective-permute-done.13.rest_2_ = bf16[4,3,128,128]{3,2,1,0:T(8,128)(2,1)S(1)} collective-permute-done((bf16[4,3,128,128]{3,2,1,0:T(8,128)(2,1)S(1)}, bf16[4,3,128,128]{3,2,1,0:T(8,128)(2,1)S(1)}, u32[]{:S(2)}, u32[]{:S(2)}) %collective-permute-start.13) | collective-permute-done | bytes 393248 | tf_op jit(solution)/shard_map/ppermute | solution.py:26
  105.5 3.1 %collective-permute-start.14 = (bf16[4,3,128,128]{3,2,1,0:T(8,128)(2,1)S(1)}, bf16[4,3,128,128]{3,2,1,0:T(8,128)(2,1)S(1)}, u32[]{:S(2)}, u32[]{:S(2)}) collective-permute-start(bf16[4,3,128,128]{3,2,1,0:T(8,128)(2,1)S(1)} %collective-permute-done.13.rest_2_), channel_id=1, source_target_pairs={{0,6},{1,7},{2,0},{3,1},{4,2},{5,3},{6,4},{7,5},{8,14},{9,15},{10,... | collective-permute-start | bytes 1179656 | tf_op jit(solution)/shard_map/ppermute | solution.py:26
  108.7 5.3 %collective-permute-done.15.rest_3_ = bf16[4,3,128,128]{3,2,1,0:T(8,128)(2,1)S(1)} collective-permute-done((bf16[4,3,128,128]{3,2,1,0:T(8,128)(2,1)}, bf16[4,3,128,128]{3,2,1,0:T(8,128)(2,1)S(1)}, u32[]{:S(2)}, u32[]{:S(2)}) %collective-permute-start.15) | collective-permute-done | bytes 393248 | tf_op jit(solution)/shard_map/ppermute | solution.py:26
  115.0 5.3 %block_products.6.rest_7_ = f32[4,3,128,128]{3,2,1,0:T(8,128)S(1)} custom-call(s32[144]{0:T(256)S(1)} %copy-done.6, s32[4]{0:T(128)S(1)} %copy-done.9, bf16[4,3,128,128]{3,2,1,0:T(8,128)(2,1)S(1)} %copy-done.1, bf16[4,3,128,128]{3,2,1,0:T(8,128)(2,1)S(1)} %collective-permute-done.11.rest_1_, bf16[4,3,128,128]{3,2,1,0:T(8,128)(2,1)S(1)} %collective-permute-done.9.rest_2_, ...), custom_call_target="tpu_custom_call" | custom-call | flops 300000000 | bytes 8000000 | tf_op jit(solution)/shard_map/block_products/pallas_call | solution.py:204
  120.3 6.0 %block_products.7 = bf16[4,3,128,128]{3,2,1,0:T(8,128)(2,1)} custom-call(s32[144]{0:T(256)S(1)} %copy-done.4, s32[4]{0:T(128)S(1)} %copy-done.8, bf16[4,3,128,128]{3,2,1,0:T(8,128)(2,1)S(1)} %collective-permute-done.10.rest_0_, bf16[4,3,128,128]{3,2,1,0:T(8,128)(2,1)S(1)} %collective-permute-done.12.rest_1_, ...), custom_call_target="tpu_custom_call" | custom-call | flops 300000000 | bytes 8000000 | tf_op jit(solution)/shard_map/block_products/pallas_call | solution.py:204
  (40 shorter events, 12.3 us)
Async XLA Ops:
  0.6 67.2 %copy-start = (bf16[16,3,128,128]{3,2,1,0:T(8,128)(2,1)S(1)}, bf16[16,3,128,128]{3,2,1,0:T(8,128)(2,1)}, u32[]{:S(2)}) copy-start(bf16[16,3,128,128]{3,2,1,0:T(8,128)(2,1)} %rest_5_.7) | copy-start | bytes 4718596
  0.6 67.2 %collective-permute-start.6 = (bf16[16,3,128,128]{3,2,1,0:T(8,128)(2,1)}, bf16[16,3,128,128]{3,2,1,0:T(8,128)(2,1)S(1)}, u32[]{:S(2)}, u32[]{:S(2)}) collective-permute-start(bf16[16,3,128,128]{3,2,1,0:T(8,128)(2,1)} %rest_5_.7), channel_id=1, source_target_pairs={{0,8},{8,16},{16,24},{24,32},{32,40},{40,48},{48,56},{56,64},{64,7... | collective-permute-start | bytes 4718600 | tf_op jit(solution)/shard_map/ppermute | solution.py:18
  2.7 65.2 %collective-permute-start.7 = (bf16[16,3,128,128]{3,2,1,0:T(8,128)(2,1)}, bf16[16,3,128,128]{3,2,1,0:T(8,128)(2,1)}, u32[]{:S(2)}, u32[]{:S(2)}) collective-permute-start(bf16[16,3,128,128]{3,2,1,0:T(8,128)(2,1)} %rest_5_.7), channel_id=1, source_target_pairs={{0,504},{8,0},{16,8},{24,16},{32,24},{40,32},{48,40},{56,48},{64,5... | collective-permute-start | bytes 4718600 | tf_op jit(solution)/shard_map/ppermute | solution.py:18
  14.5 23.0 %collective-permute-start.2 = (bf16[4,3,128,128]{3,2,1,0:T(8,128)(2,1)S(1)}, bf16[4,3,128,128]{3,2,1,0:T(8,128)(2,1)}, u32[]{:S(2)}, u32[]{:S(2)}) collective-permute-start(bf16[4,3,128,128]{3,2,1,0:T(8,128)(2,1)S(1)} %slice_bitcast_fusion.rest_0_), channel_id=1, source_target_pairs={{0,1},{1,0},{2,3},{3,2},{4,5},{5,4},{6,7},{7,6},{8,9},{9,8},{10,11... | collective-permute-start | bytes 1179656 | tf_op jit(solution)/shard_map/ppermute | solution.py:26
  18.5 23.9 %collective-permute-start = (bf16[4,3,128,128]{3,2,1,0:T(8,128)(2,1)S(1)}, bf16[4,3,128,128]{3,2,1,0:T(8,128)(2,1)}, u32[]{:S(2)}, u32[]{:S(2)}) collective-permute-start(bf16[4,3,128,128]{3,2,1,0:T(8,128)(2,1)S(1)} %slice_bitcast_fusion.rest_0_), channel_id=1, source_target_pairs={{0,2},{1,3},{2,4},{3,5},{4,6},{5,7},{6,0},{7,1},{8,10},{9,11},{10,... | collective-permute-start | bytes 1179656 | tf_op jit(solution)/shard_map/ppermute | solution.py:26
  22.0 22.4 %collective-permute-start.8 = (bf16[4,3,128,128]{3,2,1,0:T(8,128)(2,1)S(1)}, bf16[4,3,128,128]{3,2,1,0:T(8,128)(2,1)S(1)}, u32[]{:S(2)}, u32[]{:S(2)}) collective-permute-start(bf16[4,3,128,128]{3,2,1,0:T(8,128)(2,1)S(1)} %slice_bitcast_fusion.rest_0_), channel_id=1, source_target_pairs={{0,6},{1,7},{2,0},{3,1},{4,2},{5,3},{6,4},{7,5},{8,14},{9,15},{10,... | collective-permute-start | bytes 1179656 | tf_op jit(solution)/shard_map/ppermute | solution.py:26
  37.6 12.2 %collective-permute-start.4 = (bf16[4,3,128,128]{3,2,1,0:T(8,128)(2,1)}, bf16[4,3,128,128]{3,2,1,0:T(8,128)(2,1)}, u32[]{:S(2)}, u32[]{:S(2)}) collective-permute-start(bf16[4,3,128,128]{3,2,1,0:T(8,128)(2,1)} %collective-permute-done.2.rest_1_), channel_id=1, source_target_pairs={{0,6},{1,7},{2,0},{3,1},{4,2},{5,3},{6,4},{7,5},{8,14},{9,15},{10,... | collective-permute-start | bytes 1179656 | tf_op jit(solution)/shard_map/ppermute | solution.py:26
  42.5 32.7 %collective-permute-start.3 = (bf16[4,3,128,128]{3,2,1,0:T(8,128)(2,1)}, bf16[4,3,128,128]{3,2,1,0:T(8,128)(2,1)}, u32[]{:S(2)}, u32[]{:S(2)}) collective-permute-start(bf16[4,3,128,128]{3,2,1,0:T(8,128)(2,1)} %collective-permute-done.2.rest_1_), channel_id=1, source_target_pairs={{0,2},{1,3},{2,4},{3,5},{4,6},{5,7},{6,0},{7,1},{8,10},{9,11},{10,... | collective-permute-start | bytes 1179656 | tf_op jit(solution)/shard_map/ppermute | solution.py:26
  45.2 30.0 %collective-permute-start.1 = (bf16[4,3,128,128]{3,2,1,0:T(8,128)(2,1)}, bf16[4,3,128,128]{3,2,1,0:T(8,128)(2,1)}, u32[]{:S(2)}, u32[]{:S(2)}) collective-permute-start(bf16[4,3,128,128]{3,2,1,0:T(8,128)(2,1)} %collective-permute-done.rest_2_), channel_id=1, source_target_pairs={{0,2},{1,3},{2,4},{3,5},{4,6},{5,7},{6,0},{7,1},{8,10},{9,11},{10,... | collective-permute-start | bytes 1179656 | tf_op jit(solution)/shard_map/ppermute | solution.py:26
  49.7 25.5 %collective-permute-start.5 = (bf16[4,3,128,128]{3,2,1,0:T(8,128)(2,1)}, bf16[4,3,128,128]{3,2,1,0:T(8,128)(2,1)}, u32[]{:S(2)}, u32[]{:S(2)}) collective-permute-start(bf16[4,3,128,128]{3,2,1,0:T(8,128)(2,1)} %collective-permute-done.4.rest_2_), channel_id=1, source_target_pairs={{0,6},{1,7},{2,0},{3,1},{4,2},{5,3},{6,4},{7,5},{8,14},{9,15},{10,... | collective-permute-start | bytes 1179656 | tf_op jit(solution)/shard_map/ppermute | solution.py:26
  67.9 1.0 copy-start.3
  70.2 5.0 %copy-start.5 = (s32[144]{0:T(256)S(1)}, s32[144]{0:T(256)}, u32[]{:S(2)}) copy-start(s32[144]{0:T(256)} %get-tuple-element.10.code_ref) | copy-start | bytes 1732
  70.2 5.0 %copy-start.10 = (s32[4]{0:T(128)S(1)}, s32[4]{0:T(128)}, u32[]{:S(2)}) copy-start(s32[4]{0:T(128)} %get-tuple-element.11.count_ref) | copy-start | bytes 52
  75.2 38.7 %copy-start.6 = (s32[144]{0:T(256)S(1)}, s32[144]{0:T(256)}, u32[]{:S(2)}) copy-start(s32[144]{0:T(256)} %get-tuple-element.16.code_ref) | copy-start | bytes 1732
  75.2 38.7 %copy-start.9 = (s32[4]{0:T(128)S(1)}, s32[4]{0:T(128)}, u32[]{:S(2)}) copy-start(s32[4]{0:T(128)} %get-tuple-element.17.count_ref) | copy-start | bytes 52
  80.1 11.5 %collective-permute-start.11 = (bf16[4,3,128,128]{3,2,1,0:T(8,128)(2,1)}, bf16[4,3,128,128]{3,2,1,0:T(8,128)(2,1)S(1)}, u32[]{:S(2)}, u32[]{:S(2)}) collective-permute-start(bf16[4,3,128,128]{3,2,1,0:T(8,128)(2,1)} %block_products.5.rest_0_), channel_id=1, source_target_pairs={{0,1},{1,0},{2,3},{3,2},{4,5},{5,4},{6,7},{7,6},{8,9},{9,8},{10,11... | collective-permute-start | bytes 1179656 | tf_op jit(solution)/shard_map/ppermute | solution.py:26
  83.9 15.4 %collective-permute-start.9 = (bf16[4,3,128,128]{3,2,1,0:T(8,128)(2,1)}, bf16[4,3,128,128]{3,2,1,0:T(8,128)(2,1)S(1)}, u32[]{:S(2)}, u32[]{:S(2)}) collective-permute-start(bf16[4,3,128,128]{3,2,1,0:T(8,128)(2,1)} %block_products.5.rest_0_), channel_id=1, source_target_pairs={{0,2},{1,3},{2,4},{3,5},{4,6},{5,7},{6,0},{7,1},{8,10},{9,11},{10,... | collective-permute-start | bytes 1179656 | tf_op jit(solution)/shard_map/ppermute | solution.py:26
  91.6 13.9 %collective-permute-start.13 = (bf16[4,3,128,128]{3,2,1,0:T(8,128)(2,1)S(1)}, bf16[4,3,128,128]{3,2,1,0:T(8,128)(2,1)S(1)}, u32[]{:S(2)}, u32[]{:S(2)}) collective-permute-start(bf16[4,3,128,128]{3,2,1,0:T(8,128)(2,1)S(1)} %collective-permute-done.11.rest_1_), channel_id=1, source_target_pairs={{0,6},{1,7},{2,0},{3,1},{4,2},{5,3},{6,4},{7,5},{8,14},{9,15},{10,... | collective-permute-start | bytes 1179656 | tf_op jit(solution)/shard_map/ppermute | solution.py:26
  93.5 20.4 %collective-permute-start.15 = (bf16[4,3,128,128]{3,2,1,0:T(8,128)(2,1)}, bf16[4,3,128,128]{3,2,1,0:T(8,128)(2,1)S(1)}, u32[]{:S(2)}, u32[]{:S(2)}) collective-permute-start(bf16[4,3,128,128]{3,2,1,0:T(8,128)(2,1)} %block_products.5.rest_0_), channel_id=1, source_target_pairs={{0,6},{1,7},{2,0},{3,1},{4,2},{5,3},{6,4},{7,5},{8,14},{9,15},{10,... | collective-permute-start | bytes 1179656 | tf_op jit(solution)/shard_map/ppermute | solution.py:26
  95.4 24.8 %collective-permute-start.12 = (bf16[4,3,128,128]{3,2,1,0:T(8,128)(2,1)S(1)}, bf16[4,3,128,128]{3,2,1,0:T(8,128)(2,1)S(1)}, u32[]{:S(2)}, u32[]{:S(2)}) collective-permute-start(bf16[4,3,128,128]{3,2,1,0:T(8,128)(2,1)S(1)} %collective-permute-done.11.rest_1_), channel_id=1, source_target_pairs={{0,2},{1,3},{2,4},{3,5},{4,6},{5,7},{6,0},{7,1},{8,10},{9,11},{10,... | collective-permute-start | bytes 1179656 | tf_op jit(solution)/shard_map/ppermute | solution.py:26
  99.4 20.9 %collective-permute-start.10 = (bf16[4,3,128,128]{3,2,1,0:T(8,128)(2,1)S(1)}, bf16[4,3,128,128]{3,2,1,0:T(8,128)(2,1)S(1)}, u32[]{:S(2)}, u32[]{:S(2)}) collective-permute-start(bf16[4,3,128,128]{3,2,1,0:T(8,128)(2,1)S(1)} %collective-permute-done.9.rest_2_), channel_id=1, source_target_pairs={{0,2},{1,3},{2,4},{3,5},{4,6},{5,7},{6,0},{7,1},{8,10},{9,11},{10,... | collective-permute-start | bytes 1179656 | tf_op jit(solution)/shard_map/ppermute | solution.py:26
  105.5 14.7 %collective-permute-start.14 = (bf16[4,3,128,128]{3,2,1,0:T(8,128)(2,1)S(1)}, bf16[4,3,128,128]{3,2,1,0:T(8,128)(2,1)S(1)}, u32[]{:S(2)}, u32[]{:S(2)}) collective-permute-start(bf16[4,3,128,128]{3,2,1,0:T(8,128)(2,1)S(1)} %collective-permute-done.13.rest_2_), channel_id=1, source_target_pairs={{0,6},{1,7},{2,0},{3,1},{4,2},{5,3},{6,4},{7,5},{8,14},{9,15},{10,... | collective-permute-start | bytes 1179656 | tf_op jit(solution)/shard_map/ppermute | solution.py:26
  115.0 5.3 %copy-start.4 = (s32[144]{0:T(256)S(1)}, s32[144]{0:T(256)}, u32[]{:S(2)}) copy-start(s32[144]{0:T(256)} %get-tuple-element.14.code_ref) | copy-start | bytes 1732
  115.0 5.3 %copy-start.8 = (s32[4]{0:T(128)S(1)}, s32[4]{0:T(128)}, u32[]{:S(2)}) copy-start(s32[4]{0:T(128)} %get-tuple-element.15.count_ref) | copy-start | bytes 52
  (4 other events, 3.1 us)

commit v2 on v0

v2 whole, which is shorter than its diff:
```python
import functools

import jax
import jax.numpy as jnp
from jax import lax
from jax.experimental import pallas as pl
from jax.experimental.pallas import tpu as pltpu
from jax.sharding import PartitionSpec as P

Y = 4
LANES = 128
SOURCES = ((0, 0), (0, 1), (-1, 0), (1, 0), (2, 0), (-1, 1), (1, 1), (2, 1))
HALF = len(SOURCES) // 2


def shifted(x, axis, by):
    peers = lax.axis_size(axis)
    return lax.ppermute(x, axis, [(i, (i + by) % peers) for i in range(peers)])


def moved(a, dy, dx):
    pairs = []
    for n in range(2 * Y):
        y, x = divmod(n, 2)
        pairs.append((n, (y + dy) % Y * 2 + (x ^ dx)))
    return lax.ppermute(a, "narrow", pairs)


def gather_rows(own, make_tables):
    partner = moved(own, 0, 1)
    lower = moved(own, 1, 0)
    upper = moved(own, -1, 0)
    partner, tables = lax.optimization_barrier((partner, make_tables()))
    partner_lower = moved(partner, 1, 0)
    partner_upper = moved(partner, -1, 0)
    far = moved(lower, 1, 0)
    partner_far = moved(partner_upper, -1, 0)
    return (own, partner, lower, upper), (far, partner_lower, partner_upper, partner_far), tables


def table_kernel(stage, rows_dev, slots, window, total_rows, block_ref, product_ref, *rest):
    tables = rest[0:2]
    near, goals, sem = rest[2:5]
    wide_count = lax.axis_size("wide")
    narrow_count = lax.axis_size("narrow")
    wide_at = lax.axis_index("wide")
    narrow_at = lax.axis_index("narrow")

    def tile(row):
        return pl.ds(pl.multiple_of(row // LANES * LANES, LANES), LANES)

    copies = []
    for part in range(3):
        owner = lax.rem(wide_at + (part - 1 + wide_count), wide_count)
        copies.append((block_ref.at[:, tile(owner * rows_dev)], near.at[part]))
    copies.append((product_ref.at[:, tile(wide_at * window)], goals))
    copies = [pltpu.make_async_copy(a, b, sem.at[i]) for i, (a, b) in enumerate(copies)]
    for copy in copies:
        copy.start()
    for copy in copies:
        copy.wait()
    step = rows_dev // window
    ext_rows = 3 * rows_dev - step
    pad = ext_rows * slots
    y_at = narrow_at // 2
    x_at = lax.rem(narrow_at, 2)
    first_row = wide_at * rows_dev

    def one_row(g, _):
        lane = lax.rem(wide_at * window + g, LANES)
        own_lane = lax.rem(first_row + g * step, LANES)
        targets = [goals[narrow_at * slots + q, lane] for q in range(slots)]
        targets = [jnp.where(t < 0, -2, t) for t in targets]
        for j, (dy, dx) in enumerate(SOURCES):
            source = lax.rem(y_at + (dy + Y), Y) * 2 + lax.rem(x_at + dx, 2)
            half, at = divmod(j, HALF)
            for s in range(slots):
                if stage == 0:
                    col = near[1, source * slots + s, own_lane]
                else:
                    col = goals[source * slots + s, lane]
                row = lax.rem(
                    col * narrow_count + source - first_row + (rows_dev + total_rows), total_rows
                )
                row = jnp.where(col >= 0, jnp.minimum(row, ext_rows - 1), 0)
                part = row // rows_dev
                right_lane = lax.rem(first_row + row + (total_rows - rows_dev), LANES)
                right = [near[part, narrow_at * slots + t, right_lane] for t in range(slots)]
                right = [jnp.where(col >= 0, r, -1) for r in right]
                for q in range(slots):
                    found = jnp.int32(pad)
                    for t in range(slots):
                        found = jnp.where(right[t] == targets[q], row * slots + t, found)
                    tables[half][(g * slots + q) * HALF * slots + at * slots + s] = found
        return 0

    lax.fori_loop(0, window, one_row, 0)


def build_tables(stage, block_list, product_list, rows_dev, slots, window):
    table = jax.ShapeDtypeStruct((window * slots * HALF * slots,), jnp.int32)
    return pl.pallas_call(
        functools.partial(table_kernel, stage, rows_dev, slots, window, block_list.shape[0]),
        out_shape=[table] * 2,
        in_specs=[pl.BlockSpec(memory_space=pl.ANY)] * 2,
        out_specs=[pl.BlockSpec(memory_space=pltpu.SMEM)] * 2,
        scratch_shapes=[
            pltpu.SMEM((3, block_list.shape[1], LANES), jnp.int32),
            pltpu.SMEM((product_list.shape[1], LANES), jnp.int32),
            pltpu.SemaphoreType.DMA((4,)),
        ],
        name="square_tables" if stage == 0 else "cube_tables",
        cost_estimate=pl.CostEstimate(flops=0, bytes_accessed=6_000_000, transcendentals=0),
    )(block_list.T, product_list.T)


def add_products(window, slots, table, lefts, ext, start, out_ref):
    capacity = HALF * slots
    size = out_ref.shape[2]
    pair = 2
    for g in range(window):
        total = [None if start is None else start[g, q] for q in range(slots)]
        for e in range(0, capacity, pair):
            near = range(e, e + pair)
            left = jnp.concatenate([lefts[i // slots][g, i % slots] for i in near], axis=1)
            right = jnp.concatenate(
                [
                    jnp.concatenate(
                        [ext[table[(g * slots + q) * capacity + i]] for i in near], axis=0
                    )
                    for q in range(slots)
                ],
                axis=1,
            )
            term = jnp.dot(left, right, preferred_element_type=jnp.float32)
            for q in range(slots):
                piece = term[:, q * size : (q + 1) * size]
                total[q] = piece if total[q] is None else total[q] + piece
        for q in range(slots):
            out_ref[g, q] = total[q].astype(out_ref.dtype)


def first_kernel(window, slots, table, *rest):
    lefts, (below, own, above, out_ref, ext, sem) = rest[:HALF], rest[HALF:]
    rows = own.shape[0]
    tail = ext.shape[0] - slots - 2 * rows
    copies = [
        (below, ext.at[pl.ds(0, rows)]),
        (own, ext.at[pl.ds(rows, rows)]),
        (above.at[pl.ds(0, tail)], ext.at[pl.ds(2 * rows, tail)]),
    ]
    copies = [pltpu.make_async_copy(a, b, sem.at[i]) for i, (a, b) in enumerate(copies)]
    for copy in copies:
        copy.start()
    for s in range(slots):
        ext[ext.shape[0] - slots + s] = jnp.zeros(ext.shape[1:], ext.dtype)
    for copy in copies:
        copy.wait()
    add_products(window, slots, table, lefts, ext, None, out_ref)


def next_kernel(window, slots, table, *rest):
    lefts, rest = rest[:HALF], rest[HALF:]
    if len(rest) == 3:
        ext, start, out_ref = rest
    else:
        (ext, out_ref), start = rest, None
    add_products(window, slots, table, lefts, ext, start, out_ref)


LOCAL = pl.BlockSpec(memory_space=pltpu.VMEM)
SCALAR = pl.BlockSpec(memory_space=pltpu.SMEM)
PARAMS = pltpu.CompilerParams(vmem_limit_bytes=16 * 1024 * 1024)
COST = pl.CostEstimate(flops=600_000_000, bytes_accessed=6_000_000, transcendentals=0)


def multiply_first(table, lefts, rights, window, slots):
    block = lefts[0].shape[2:]
    rows = rights[0].shape[0]
    ext_blocks = 3 * rows - rows // window + slots
    return pl.pallas_call(
        functools.partial(first_kernel, window, slots),
        out_shape=(
            jax.ShapeDtypeStruct((window, slots) + block, jnp.float32),
            jax.ShapeDtypeStruct((ext_blocks,) + block, jnp.bfloat16),
        ),
        in_specs=[SCALAR] + [LOCAL] * (HALF + 3),
        out_specs=(LOCAL, LOCAL),
        scratch_shapes=[pltpu.SemaphoreType.DMA((3,))],
        compiler_params=PARAMS,
        name="first_products",
        cost_estimate=COST,
    )(table, *lefts, *rights)


def multiply(table, lefts, ext, start, window, slots, out_type):
    block = lefts[0].shape[2:]
    extra = () if start is None else (start,)
    return pl.pallas_call(
        functools.partial(next_kernel, window, slots),
        out_shape=jax.ShapeDtypeStruct((window, slots) + block, out_type),
        in_specs=[SCALAR] + [LOCAL] * (HALF + 1 + len(extra)),
        out_specs=LOCAL,
        compiler_params=PARAMS,
        name="next_products",
        cost_estimate=COST,
    )(table, *lefts, ext, *extra)


def per_device(density, block_list, product_list):
    rows_dev, slots = density.shape[:2]
    window = product_list.shape[0] // lax.axis_size("wide")
    step = rows_dev // window
    local = density.reshape((window, step) + density.shape[1:])[:, 0]
    density, local = lax.optimization_barrier((density, local))
    early, late, tables = gather_rows(
        local, lambda: build_tables(0, block_list, product_list, rows_dev, slots, window)
    )
    blocks = density.reshape((rows_dev * slots,) + density.shape[2:])
    rights = (shifted(blocks, "wide", 1), blocks, shifted(blocks, "wide", -1))
    part, ext = multiply_first(tables[0], early, rights, window, slots)
    square = multiply(tables[1], late, ext, part, window, slots, jnp.bfloat16)
    square, block_list, product_list = lax.optimization_barrier((square, block_list, product_list))
    early, late, tables = gather_rows(
        square, lambda: build_tables(1, block_list, product_list, rows_dev, slots, window)
    )
    part = multiply(tables[0], early, ext, None, window, slots, jnp.float32)
    cube = multiply(tables[1], late, ext, part, window, slots, jnp.bfloat16)
    return square, cube


def solution(mesh):
    placed = P("wide", "narrow", None, None)
    return jax.shard_map(
        per_device,
        mesh=mesh,
        in_specs=(placed, P(), P()),
        out_specs=(placed, placed),
        check_vma=False,
    )
```

time: 275 us -> 112 us (0.41)
  waiting for transfers between devices: 143 us -> 28.2 us
  local copies, waits for them, and re-layouts: 66.8 us -> 7.05 us
  starting transfers between devices: 15.3 us -> 56.1 us
  matrix products: 21.3 us -> 0 us
  Pallas kernels: 0 us -> 18.6 us
  between operations: 14.2 us -> 0.89 us
  other arithmetic: 11.2 us -> 0 us
    all_gather x2 -> x0, waiting for transfers between devices: 127 us -> none  [the longest x1 74.4 us: per_device(): square_rows = lax.all_gather(square_own, 'narrow', axis=1, tiled=True)]
    gather x35 -> x0, local copies, waits for them, and re-layouts: 58.4 us -> none  [the longest x16 46.7 us: one_row(): flat_blocks[nearby[:, None] * capacity + chosen]]
    ppermute x0 -> x14, starting transfers between devices: none -> 40.8 us  [moved(): return lax.ppermute(a, 'narrow', pairs)]
    ppermute x0 -> x14, waiting for transfers between devices: none -> 28.2 us  [moved(): return lax.ppermute(a, 'narrow', pairs)]
    dot_general x8 -> x0, matrix products: 21.3 us -> none  [one_row(): jnp.einsum('eab,eqbc->qac', left_row, right_blocks, preferred_element_typ...]
    pallas_call x0 -> x6, Pallas kernels: none -> 18.6 us  [the longest x2 9.67 us: build_tables(): pl.pallas_call(functools.partial(table_kernel, stage, rows_dev, slots, wi...]
    ppermute x2, waiting for transfers between devices: 16.4 us -> 0.01 us  [shifted(): return lax.ppermute(x, axis, [(i, (i + by) % peers) for i in range(peers)])]
    another operation x8 -> x0, other arithmetic: 4.29 us -> none  [one_row(): chosen = jnp.argmax(matches, axis=2)]
  transfers between devices with their start and end apart: 4 -> 16, of which waited for: 4 -> 7; matrix products, arithmetic and copies ran while one was open for 2% -> 0% of each run, Pallas kernels for 0% -> 13%
where the time goes in v2:
time: 112 us; the launch traced here: 111 us
  starting transfers between devices  56.1 us (50%)
  waiting for transfers between devices  28.2 us (25%)
  Pallas kernels  18.6 us (17%)
  local copies, waits for them, and re-layouts  7.05 us (6%)
    ppermute x14, starting transfers between devices, moved(): return lax.ppermute(a, 'narrow', pairs)  40.8 us
    ppermute x14, waiting for transfers between devices, moved(): return lax.ppermute(a, 'narrow', pairs)  28.2 us
    ppermute x2, starting transfers between devices, shifted(): return lax.ppermute(x, axis, [(i, (i + by) % peers) for i in range(peers)])  15.2 us
    pallas_call x2, Pallas kernels, build_tables(): pl.pallas_call(functools.partial(table_kernel, stage, rows_dev, slots, wi...  9.67 us
    pallas_call x3, Pallas kernels, multiply(): pl.pallas_call(functools.partial(next_kernel, window, slots), out_shape=j...  6.19 us
    unnamed x16, local copies, waits for them, and re-layouts  6.02 us
    pallas_call x1, Pallas kernels, multiply_first(): pl.pallas_call(functools.partial(first_kernel, window, slots), out_shape=...  2.73 us
  transfers between devices with their start and end apart: 16, of which 7 were waited for; matrix products, arithmetic and copies ran while one was open for 0% of the time, Pallas kernels for 13%

profile of v2, /device:TPU:24, one launch (start us, length us, event | category | flops | bytes accessed | tf_op | source)
XLA Modules:
  0.0 110.8 jit_solution(11254276070967002559)
XLA Ops:
  3.6 13.3 %collective-permute-start.8 = (bf16[48,128,128]{2,1,0:T(8,128)(2,1)}, bf16[48,128,128]{2,1,0:T(8,128)(2,1)S(1)}, u32[]{:S(2)}, u32[]{:S(2)}) collective-permute-start(bf16[48,128,128]{2,1,0:T(8,128)(2,1)} %bitcast.12), channel_id=1, source_target_pairs={{0,504},{8,0},{16,8},{24,16},{32,24},{40,32},{48,40},{56,48},{64,5... | collective-permute-start | bytes 4718600 | tf_op jit(solution)/shard_map/ppermute | solution.py:18
  16.9 2.5 %collective-permute-start = (bf16[4,3,128,128]{3,2,1,0:T(8,128)(2,1)S(1)}, bf16[4,3,128,128]{3,2,1,0:T(8,128)(2,1)}, u32[]{:S(2)}, u32[]{:S(2)}) collective-permute-start(bf16[4,3,128,128]{3,2,1,0:T(8,128)(2,1)S(1)} %slice_bitcast_fusion.rest_0_), channel_id=1, source_target_pairs={{0,1},{1,0},{2,3},{3,2},{4,5},{5,4},{6,7},{7,6},{8,9},{9,8},{10,11... | collective-permute-start | bytes 1179656 | tf_op jit(solution)/shard_map/ppermute | solution.py:26
  19.4 2.1 %collective-permute-start.1 = (bf16[4,3,128,128]{3,2,1,0:T(8,128)(2,1)S(1)}, bf16[4,3,128,128]{3,2,1,0:T(8,128)(2,1)}, u32[]{:S(2)}, u32[]{:S(2)}) collective-permute-start(bf16[4,3,128,128]{3,2,1,0:T(8,128)(2,1)S(1)} %slice_bitcast_fusion.rest_0_), channel_id=1, source_target_pairs={{0,2},{1,3},{2,4},{3,5},{4,6},{5,7},{6,0},{7,1},{8,10},{9,11},{10,... | collective-permute-start | bytes 1179656 | tf_op jit(solution)/shard_map/ppermute | solution.py:26
  21.6 3.7 %collective-permute-start.6 = (bf16[4,3,128,128]{3,2,1,0:T(8,128)(2,1)S(1)}, bf16[4,3,128,128]{3,2,1,0:T(8,128)(2,1)}, u32[]{:S(2)}, u32[]{:S(2)}) collective-permute-start(bf16[4,3,128,128]{3,2,1,0:T(8,128)(2,1)S(1)} %slice_bitcast_fusion.rest_0_), channel_id=1, source_target_pairs={{0,6},{1,7},{2,0},{3,1},{4,2},{5,3},{6,4},{7,5},{8,14},{9,15},{10,... | collective-permute-start | bytes 1179656 | tf_op jit(solution)/shard_map/ppermute | solution.py:26
  25.3 4.8 %square_tables.1 = (s32[144]{0:T(256)}, s32[144]{0:T(256)}) custom-call(s32[24,1024]{1,0:T(8,128)} %bitcast.14, s32[24,256]{1,0:T(8,128)} %bitcast.16), custom_call_target="tpu_custom_call" | custom-call | bytes 6000000 | tf_op jit(solution)/shard_map/square_tables/pallas_call | solution.py:102
  30.1 7.3 %collective-permute-done.rest_1_ = bf16[4,3,128,128]{3,2,1,0:T(8,128)(2,1)} collective-permute-done((bf16[4,3,128,128]{3,2,1,0:T(8,128)(2,1)S(1)}, bf16[4,3,128,128]{3,2,1,0:T(8,128)(2,1)}, u32[]{:S(2)}, u32[]{:S(2)}) %collective-permute-start) | collective-permute-done | bytes 393248 | tf_op jit(solution)/shard_map/ppermute | solution.py:26
  37.4 2.8 %collective-permute-start.4 = (bf16[4,3,128,128]{3,2,1,0:T(8,128)(2,1)}, bf16[4,3,128,128]{3,2,1,0:T(8,128)(2,1)S(1)}, u32[]{:S(2)}, u32[]{:S(2)}) collective-permute-start(bf16[4,3,128,128]{3,2,1,0:T(8,128)(2,1)} %collective-permute-done.rest_1_), channel_id=1, source_target_pairs={{0,6},{1,7},{2,0},{3,1},{4,2},{5,3},{6,4},{7,5},{8,14},{9,15},{10,... | collective-permute-start | bytes 1179656 | tf_op jit(solution)/shard_map/ppermute | solution.py:26
  40.2 4.4 %collective-permute-start.3 = (bf16[4,3,128,128]{3,2,1,0:T(8,128)(2,1)}, bf16[4,3,128,128]{3,2,1,0:T(8,128)(2,1)S(1)}, u32[]{:S(2)}, u32[]{:S(2)}) collective-permute-start(bf16[4,3,128,128]{3,2,1,0:T(8,128)(2,1)} %collective-permute-done.rest_1_), channel_id=1, source_target_pairs={{0,2},{1,3},{2,4},{3,5},{4,6},{5,7},{6,0},{7,1},{8,10},{9,11},{10,... | collective-permute-start | bytes 1179656 | tf_op jit(solution)/shard_map/ppermute | solution.py:26
  44.6 3.8 %collective-permute-start.2 = (bf16[4,3,128,128]{3,2,1,0:T(8,128)(2,1)}, bf16[4,3,128,128]{3,2,1,0:T(8,128)(2,1)S(1)}, u32[]{:S(2)}, u32[]{:S(2)}) collective-permute-start(bf16[4,3,128,128]{3,2,1,0:T(8,128)(2,1)} %collective-permute-done.1.rest_2_), channel_id=1, source_target_pairs={{0,2},{1,3},{2,4},{3,5},{4,6},{5,7},{6,0},{7,1},{8,10},{9,11},{10,... | collective-permute-start | bytes 1179656 | tf_op jit(solution)/shard_map/ppermute | solution.py:26
  48.4 3.6 %collective-permute-done.4.rest_2_ = bf16[4,3,128,128]{3,2,1,0:T(8,128)(2,1)S(1)} collective-permute-done((bf16[4,3,128,128]{3,2,1,0:T(8,128)(2,1)}, bf16[4,3,128,128]{3,2,1,0:T(8,128)(2,1)S(1)}, u32[]{:S(2)}, u32[]{:S(2)}) %collective-permute-start.4) | collective-permute-done | bytes 393248 | tf_op jit(solution)/shard_map/ppermute | solution.py:26
  56.0 2.7 %first_products.1 = (f32[4,3,128,128]{3,2,1,0:T(8,128)S(1)}, bf16[135,128,128]{2,1,0:T(8,128)(2,1)S(1)}) custom-call(s32[144]{0:T(256)S(1)} %copy-done.4, bf16[4,3,128,128]{3,2,1,0:T(8,128)(2,1)S(1)} %slice_bitcast_fusion.rest_0_, bf16[4,3,128,128]{3,2,1,0:T(8,128)(2,1)} %collective-permute-done.rest_1_, ...), custom_call_target="tpu_custom_call" | custom-call | flops 600000000 | bytes 6000000 | tf_op jit(solution)/shard_map/first_products/pallas_call | solution.py:181
  58.8 2.9 %collective-permute-done.2.rest_0_ = bf16[4,3,128,128]{3,2,1,0:T(8,128)(2,1)S(1)} collective-permute-done((bf16[4,3,128,128]{3,2,1,0:T(8,128)(2,1)}, bf16[4,3,128,128]{3,2,1,0:T(8,128)(2,1)S(1)}, u32[]{:S(2)}, u32[]{:S(2)}) %collective-permute-start.2) | collective-permute-done | bytes 393248 | tf_op jit(solution)/shard_map/ppermute | solution.py:26
  61.7 3.7 %collective-permute-done.5.rest_3_ = bf16[4,3,128,128]{3,2,1,0:T(8,128)(2,1)S(1)} collective-permute-done((bf16[4,3,128,128]{3,2,1,0:T(8,128)(2,1)S(1)}, bf16[4,3,128,128]{3,2,1,0:T(8,128)(2,1)S(1)}, u32[]{:S(2)}, u32[]{:S(2)}) %collective-permute-start.5) | collective-permute-done | bytes 393248 | tf_op jit(solution)/shard_map/ppermute | solution.py:26
  65.4 2.3 %next_products.3.rest_0_ = bf16[4,3,128,128]{3,2,1,0:T(8,128)(2,1)} custom-call(s32[144]{0:T(256)S(1)} %copy-done.6, bf16[4,3,128,128]{3,2,1,0:T(8,128)(2,1)S(1)} %collective-permute-done.2.rest_0_, bf16[4,3,128,128]{3,2,1,0:T(8,128)(2,1)S(1)} %collective-permute-done.3.rest_1_, bf16[4,3,128,128]{3,2,1,0:T(8,128)(2,1)S(1)} %collective-permute-done.4.rest_2_, ...), custom_call_target="tpu_custom_call" | custom-call | flops 600000000 | bytes 6000000 | tf_op jit(solution)/shard_map/next_products/pallas_call | solution.py:199
  69.7 2.8 %collective-permute-start.10 = (bf16[4,3,128,128]{3,2,1,0:T(8,128)(2,1)}, bf16[4,3,128,128]{3,2,1,0:T(8,128)(2,1)S(1)}, u32[]{:S(2)}, u32[]{:S(2)}) collective-permute-start(bf16[4,3,128,128]{3,2,1,0:T(8,128)(2,1)} %next_products.3.rest_0_), channel_id=1, source_target_pairs={{0,2},{1,3},{2,4},{3,5},{4,6},{5,7},{6,0},{7,1},{8,10},{9,11},{10,... | collective-permute-start | bytes 1179656 | tf_op jit(solution)/shard_map/ppermute | solution.py:26
  72.5 4.9 %cube_tables.1 = (s32[144]{0:T(256)}, s32[144]{0:T(256)}) custom-call(s32[24,1024]{1,0:T(8,128)} %bitcast.15, s32[24,256]{1,0:T(8,128)} %bitcast.17), custom_call_target="tpu_custom_call" | custom-call | bytes 6000000 | tf_op jit(solution)/shard_map/cube_tables/pallas_call | solution.py:102
  79.3 2.0 %collective-permute-start.13 = (bf16[4,3,128,128]{3,2,1,0:T(8,128)(2,1)S(1)}, bf16[4,3,128,128]{3,2,1,0:T(8,128)(2,1)S(1)}, u32[]{:S(2)}, u32[]{:S(2)}) collective-permute-start(bf16[4,3,128,128]{3,2,1,0:T(8,128)(2,1)S(1)} %collective-permute-done.9.rest_1_), channel_id=1, source_target_pairs={{0,6},{1,7},{2,0},{3,1},{4,2},{5,3},{6,4},{7,5},{8,14},{9,15},{10,... | collective-permute-start | bytes 1179656 | tf_op jit(solution)/shard_map/ppermute | solution.py:26
  81.3 2.2 %collective-permute-start.15 = (bf16[4,3,128,128]{3,2,1,0:T(8,128)(2,1)}, bf16[4,3,128,128]{3,2,1,0:T(8,128)(2,1)S(1)}, u32[]{:S(2)}, u32[]{:S(2)}) collective-permute-start(bf16[4,3,128,128]{3,2,1,0:T(8,128)(2,1)} %next_products.3.rest_0_), channel_id=1, source_target_pairs={{0,6},{1,7},{2,0},{3,1},{4,2},{5,3},{6,4},{7,5},{8,14},{9,15},{10,... | collective-permute-start | bytes 1179656 | tf_op jit(solution)/shard_map/ppermute | solution.py:26
  83.5 4.9 %collective-permute-start.12 = (bf16[4,3,128,128]{3,2,1,0:T(8,128)(2,1)S(1)}, bf16[4,3,128,128]{3,2,1,0:T(8,128)(2,1)S(1)}, u32[]{:S(2)}, u32[]{:S(2)}) collective-permute-start(bf16[4,3,128,128]{3,2,1,0:T(8,128)(2,1)S(1)} %collective-permute-done.9.rest_1_), channel_id=1, source_target_pairs={{0,2},{1,3},{2,4},{3,5},{4,6},{5,7},{6,0},{7,1},{8,10},{9,11},{10,... | collective-permute-start | bytes 1179656 | tf_op jit(solution)/shard_map/ppermute | solution.py:26
  88.4 3.9 %collective-permute-start.11 = (bf16[4,3,128,128]{3,2,1,0:T(8,128)(2,1)S(1)}, bf16[4,3,128,128]{3,2,1,0:T(8,128)(2,1)S(1)}, u32[]{:S(2)}, u32[]{:S(2)}) collective-permute-start(bf16[4,3,128,128]{3,2,1,0:T(8,128)(2,1)S(1)} %collective-permute-done.10.rest_2_), channel_id=1, source_target_pairs={{0,2},{1,3},{2,4},{3,5},{4,6},{5,7},{6,0},{7,1},{8,10},{9,11},{10,... | collective-permute-start | bytes 1179656 | tf_op jit(solution)/shard_map/ppermute | solution.py:26
  92.3 2.2 %collective-permute-done.13.rest_2_ = bf16[4,3,128,128]{3,2,1,0:T(8,128)(2,1)S(1)} collective-permute-done((bf16[4,3,128,128]{3,2,1,0:T(8,128)(2,1)S(1)}, bf16[4,3,128,128]{3,2,1,0:T(8,128)(2,1)S(1)}, u32[]{:S(2)}, u32[]{:S(2)}) %collective-permute-start.13) | collective-permute-done | bytes 393248 | tf_op jit(solution)/shard_map/ppermute | solution.py:26
  96.5 6.5 %collective-permute-done.15.rest_3_ = bf16[4,3,128,128]{3,2,1,0:T(8,128)(2,1)S(1)} collective-permute-done((bf16[4,3,128,128]{3,2,1,0:T(8,128)(2,1)}, bf16[4,3,128,128]{3,2,1,0:T(8,128)(2,1)S(1)}, u32[]{:S(2)}, u32[]{:S(2)}) %collective-permute-start.15) | collective-permute-done | bytes 393248 | tf_op jit(solution)/shard_map/ppermute | solution.py:26
  103.0 2.3 %copy-done.1 = bf16[135,128,128]{2,1,0:T(8,128)(2,1)S(1)} copy-done((bf16[135,128,128]{2,1,0:T(8,128)(2,1)S(1)}, bf16[135,128,128]{2,1,0:T(8,128)(2,1)}, u32[]{:S(2)}) %copy-start.1) | copy-done | bytes 4423704
  108.5 2.3 %next_products.5 = bf16[4,3,128,128]{3,2,1,0:T(8,128)(2,1)} custom-call(s32[144]{0:T(256)S(1)} %copy-done.7, bf16[4,3,128,128]{3,2,1,0:T(8,128)(2,1)S(1)} %collective-permute-done.11.rest_0_, bf16[4,3,128,128]{3,2,1,0:T(8,128)(2,1)S(1)} %collective-permute-done.12.rest_1_, bf16[4,3,128,128]{3,2,1,0:T(8,128)(2,1)S(1)} %collective-permute-done.13.rest_2_, ...), custom_call_target="tpu_custom_call" | custom-call | flops 600000000 | bytes 6000000 | tf_op jit(solution)/shard_map/next_products/pallas_call | solution.py:199
  (31 shorter events, 15.9 us)
Async XLA Ops:
  1.7 52.3 %collective-permute-start.7 = (bf16[48,128,128]{2,1,0:T(8,128)(2,1)}, bf16[48,128,128]{2,1,0:T(8,128)(2,1)S(1)}, u32[]{:S(2)}, u32[]{:S(2)}) collective-permute-start(bf16[48,128,128]{2,1,0:T(8,128)(2,1)} %bitcast.11), channel_id=1, source_target_pairs={{0,8},{8,16},{16,24},{24,32},{32,40},{40,48},{48,56},{56,64},{64,7... | collective-permute-start | bytes 4718600 | tf_op jit(solution)/shard_map/ppermute | solution.py:18
  3.6 50.4 %collective-permute-start.8 = (bf16[48,128,128]{2,1,0:T(8,128)(2,1)}, bf16[48,128,128]{2,1,0:T(8,128)(2,1)S(1)}, u32[]{:S(2)}, u32[]{:S(2)}) collective-permute-start(bf16[48,128,128]{2,1,0:T(8,128)(2,1)} %bitcast.12), channel_id=1, source_target_pairs={{0,504},{8,0},{16,8},{24,16},{32,24},{40,32},{48,40},{56,48},{64,5... | collective-permute-start | bytes 4718600 | tf_op jit(solution)/shard_map/ppermute | solution.py:18
  16.9 20.5 %collective-permute-start = (bf16[4,3,128,128]{3,2,1,0:T(8,128)(2,1)S(1)}, bf16[4,3,128,128]{3,2,1,0:T(8,128)(2,1)}, u32[]{:S(2)}, u32[]{:S(2)}) collective-permute-start(bf16[4,3,128,128]{3,2,1,0:T(8,128)(2,1)S(1)} %slice_bitcast_fusion.rest_0_), channel_id=1, source_target_pairs={{0,1},{1,0},{2,3},{3,2},{4,5},{5,4},{6,7},{7,6},{8,9},{9,8},{10,11... | collective-permute-start | bytes 1179656 | tf_op jit(solution)/shard_map/ppermute | solution.py:26
  19.4 20.8 %collective-permute-start.1 = (bf16[4,3,128,128]{3,2,1,0:T(8,128)(2,1)S(1)}, bf16[4,3,128,128]{3,2,1,0:T(8,128)(2,1)}, u32[]{:S(2)}, u32[]{:S(2)}) collective-permute-start(bf16[4,3,128,128]{3,2,1,0:T(8,128)(2,1)S(1)} %slice_bitcast_fusion.rest_0_), channel_id=1, source_target_pairs={{0,2},{1,3},{2,4},{3,5},{4,6},{5,7},{6,0},{7,1},{8,10},{9,11},{10,... | collective-permute-start | bytes 1179656 | tf_op jit(solution)/shard_map/ppermute | solution.py:26
  21.6 23.1 %collective-permute-start.6 = (bf16[4,3,128,128]{3,2,1,0:T(8,128)(2,1)S(1)}, bf16[4,3,128,128]{3,2,1,0:T(8,128)(2,1)}, u32[]{:S(2)}, u32[]{:S(2)}) collective-permute-start(bf16[4,3,128,128]{3,2,1,0:T(8,128)(2,1)S(1)} %slice_bitcast_fusion.rest_0_), channel_id=1, source_target_pairs={{0,6},{1,7},{2,0},{3,1},{4,2},{5,3},{6,4},{7,5},{8,14},{9,15},{10,... | collective-permute-start | bytes 1179656 | tf_op jit(solution)/shard_map/ppermute | solution.py:26
  37.4 28.0 %copy-start.6 = (s32[144]{0:T(256)S(1)}, s32[144]{0:T(256)}, u32[]{:S(2)}) copy-start(s32[144]{0:T(256)} %get-tuple-element.22.table) | copy-start | bytes 1732
  37.4 14.6 %collective-permute-start.4 = (bf16[4,3,128,128]{3,2,1,0:T(8,128)(2,1)}, bf16[4,3,128,128]{3,2,1,0:T(8,128)(2,1)S(1)}, u32[]{:S(2)}, u32[]{:S(2)}) collective-permute-start(bf16[4,3,128,128]{3,2,1,0:T(8,128)(2,1)} %collective-permute-done.rest_1_), channel_id=1, source_target_pairs={{0,6},{1,7},{2,0},{3,1},{4,2},{5,3},{6,4},{7,5},{8,14},{9,15},{10,... | collective-permute-start | bytes 1179656 | tf_op jit(solution)/shard_map/ppermute | solution.py:26
  40.2 18.6 %collective-permute-start.3 = (bf16[4,3,128,128]{3,2,1,0:T(8,128)(2,1)}, bf16[4,3,128,128]{3,2,1,0:T(8,128)(2,1)S(1)}, u32[]{:S(2)}, u32[]{:S(2)}) collective-permute-start(bf16[4,3,128,128]{3,2,1,0:T(8,128)(2,1)} %collective-permute-done.rest_1_), channel_id=1, source_target_pairs={{0,2},{1,3},{2,4},{3,5},{4,6},{5,7},{6,0},{7,1},{8,10},{9,11},{10,... | collective-permute-start | bytes 1179656 | tf_op jit(solution)/shard_map/ppermute | solution.py:26
  44.6 17.1 %collective-permute-start.2 = (bf16[4,3,128,128]{3,2,1,0:T(8,128)(2,1)}, bf16[4,3,128,128]{3,2,1,0:T(8,128)(2,1)S(1)}, u32[]{:S(2)}, u32[]{:S(2)}) collective-permute-start(bf16[4,3,128,128]{3,2,1,0:T(8,128)(2,1)} %collective-permute-done.1.rest_2_), channel_id=1, source_target_pairs={{0,2},{1,3},{2,4},{3,5},{4,6},{5,7},{6,0},{7,1},{8,10},{9,11},{10,... | collective-permute-start | bytes 1179656 | tf_op jit(solution)/shard_map/ppermute | solution.py:26
  52.0 13.4 %collective-permute-start.5 = (bf16[4,3,128,128]{3,2,1,0:T(8,128)(2,1)S(1)}, bf16[4,3,128,128]{3,2,1,0:T(8,128)(2,1)S(1)}, u32[]{:S(2)}, u32[]{:S(2)}) collective-permute-start(bf16[4,3,128,128]{3,2,1,0:T(8,128)(2,1)S(1)} %collective-permute-done.4.rest_2_), channel_id=1, source_target_pairs={{0,6},{1,7},{2,0},{3,1},{4,2},{5,3},{6,4},{7,5},{8,14},{9,15},{10,... | collective-permute-start | bytes 1179656 | tf_op jit(solution)/shard_map/ppermute | solution.py:26
  54.0 1.4 %copy-start.2 = (bf16[16,3,128,128]{3,2,1,0:T(8,128)(2,1)S(1)}, bf16[16,3,128,128]{3,2,1,0:T(8,128)(2,1)}, u32[]{:S(2)}) copy-start(bf16[16,3,128,128]{3,2,1,0:T(8,128)(2,1)} %param.3) | copy-start | bytes 4718596
  55.4 0.7 copy-start.4
  58.8 9.0 %copy-start = (bf16[135,128,128]{2,1,0:T(8,128)(2,1)}, bf16[135,128,128]{2,1,0:T(8,128)(2,1)S(1)}, u32[]{:S(2)}) copy-start(bf16[135,128,128]{2,1,0:T(8,128)(2,1)S(1)} %get-tuple-element.26.rest_4_) | copy-start | bytes 13271044
  67.8 11.5 %collective-permute-start.9 = (bf16[4,3,128,128]{3,2,1,0:T(8,128)(2,1)}, bf16[4,3,128,128]{3,2,1,0:T(8,128)(2,1)S(1)}, u32[]{:S(2)}, u32[]{:S(2)}) collective-permute-start(bf16[4,3,128,128]{3,2,1,0:T(8,128)(2,1)} %next_products.3.rest_0_), channel_id=1, source_target_pairs={{0,1},{1,0},{2,3},{3,2},{4,5},{5,4},{6,7},{7,6},{8,9},{9,8},{10,11... | collective-permute-start | bytes 1179656 | tf_op jit(solution)/shard_map/ppermute | solution.py:26
  69.7 18.7 %collective-permute-start.10 = (bf16[4,3,128,128]{3,2,1,0:T(8,128)(2,1)}, bf16[4,3,128,128]{3,2,1,0:T(8,128)(2,1)S(1)}, u32[]{:S(2)}, u32[]{:S(2)}) collective-permute-start(bf16[4,3,128,128]{3,2,1,0:T(8,128)(2,1)} %next_products.3.rest_0_), channel_id=1, source_target_pairs={{0,2},{1,3},{2,4},{3,5},{4,6},{5,7},{6,0},{7,1},{8,10},{9,11},{10,... | collective-permute-start | bytes 1179656 | tf_op jit(solution)/shard_map/ppermute | solution.py:26
  79.3 29.2 %copy-start.7 = (s32[144]{0:T(256)S(1)}, s32[144]{0:T(256)}, u32[]{:S(2)}) copy-start(s32[144]{0:T(256)} %get-tuple-element.33.table) | copy-start | bytes 1732
  79.3 15.3 %collective-permute-start.13 = (bf16[4,3,128,128]{3,2,1,0:T(8,128)(2,1)S(1)}, bf16[4,3,128,128]{3,2,1,0:T(8,128)(2,1)S(1)}, u32[]{:S(2)}, u32[]{:S(2)}) collective-permute-start(bf16[4,3,128,128]{3,2,1,0:T(8,128)(2,1)S(1)} %collective-permute-done.9.rest_1_), channel_id=1, source_target_pairs={{0,6},{1,7},{2,0},{3,1},{4,2},{5,3},{6,4},{7,5},{8,14},{9,15},{10,... | collective-permute-start | bytes 1179656 | tf_op jit(solution)/shard_map/ppermute | solution.py:26
  81.3 21.7 %collective-permute-start.15 = (bf16[4,3,128,128]{3,2,1,0:T(8,128)(2,1)}, bf16[4,3,128,128]{3,2,1,0:T(8,128)(2,1)S(1)}, u32[]{:S(2)}, u32[]{:S(2)}) collective-permute-start(bf16[4,3,128,128]{3,2,1,0:T(8,128)(2,1)} %next_products.3.rest_0_), channel_id=1, source_target_pairs={{0,6},{1,7},{2,0},{3,1},{4,2},{5,3},{6,4},{7,5},{8,14},{9,15},{10,... | collective-permute-start | bytes 1179656 | tf_op jit(solution)/shard_map/ppermute | solution.py:26
  83.5 25.0 %collective-permute-start.12 = (bf16[4,3,128,128]{3,2,1,0:T(8,128)(2,1)S(1)}, bf16[4,3,128,128]{3,2,1,0:T(8,128)(2,1)S(1)}, u32[]{:S(2)}, u32[]{:S(2)}) collective-permute-start(bf16[4,3,128,128]{3,2,1,0:T(8,128)(2,1)S(1)} %collective-permute-done.9.rest_1_), channel_id=1, source_target_pairs={{0,2},{1,3},{2,4},{3,5},{4,6},{5,7},{6,0},{7,1},{8,10},{9,11},{10,... | collective-permute-start | bytes 1179656 | tf_op jit(solution)/shard_map/ppermute | solution.py:26
  88.4 20.1 %collective-permute-start.11 = (bf16[4,3,128,128]{3,2,1,0:T(8,128)(2,1)S(1)}, bf16[4,3,128,128]{3,2,1,0:T(8,128)(2,1)S(1)}, u32[]{:S(2)}, u32[]{:S(2)}) collective-permute-start(bf16[4,3,128,128]{3,2,1,0:T(8,128)(2,1)S(1)} %collective-permute-done.10.rest_2_), channel_id=1, source_target_pairs={{0,2},{1,3},{2,4},{3,5},{4,6},{5,7},{6,0},{7,1},{8,10},{9,11},{10,... | collective-permute-start | bytes 1179656 | tf_op jit(solution)/shard_map/ppermute | solution.py:26
  94.6 13.9 %collective-permute-start.14 = (bf16[4,3,128,128]{3,2,1,0:T(8,128)(2,1)S(1)}, bf16[4,3,128,128]{3,2,1,0:T(8,128)(2,1)S(1)}, u32[]{:S(2)}, u32[]{:S(2)}) collective-permute-start(bf16[4,3,128,128]{3,2,1,0:T(8,128)(2,1)S(1)} %collective-permute-done.13.rest_2_), channel_id=1, source_target_pairs={{0,6},{1,7},{2,0},{3,1},{4,2},{5,3},{6,4},{7,5},{8,14},{9,15},{10,... | collective-permute-start | bytes 1179656 | tf_op jit(solution)/shard_map/ppermute | solution.py:26
  103.0 2.3 %copy-start.1 = (bf16[135,128,128]{2,1,0:T(8,128)(2,1)S(1)}, bf16[135,128,128]{2,1,0:T(8,128)(2,1)}, u32[]{:S(2)}) copy-start(bf16[135,128,128]{2,1,0:T(8,128)(2,1)} %copy-done) | copy-start | bytes 13271044
  105.2 1.0 copy-start.3
  106.2 0.7 copy-start.5

commit v3 on v2

v3 whole, which is shorter than its diff:
```python
import functools

import jax
import jax.numpy as jnp
from jax import lax
from jax.experimental import pallas as pl
from jax.experimental.pallas import tpu as pltpu
from jax.sharding import PartitionSpec as P

Y = 4
LANES = 128
SOURCES = ((0, 0), (0, 1), (-1, 0), (1, 0), (2, 0), (-1, 1), (1, 1), (2, 1))
HALF = len(SOURCES) // 2


def moved(a, dy, dx):
    pairs = []
    for n in range(2 * Y):
        y, x = divmod(n, 2)
        pairs.append((n, (y + dy) % Y * 2 + (x ^ dx)))
    return lax.ppermute(a, "narrow", pairs)


def gather_rows_by_y(own, table):
    partner = moved(own, 0, 1)
    lower = moved(own, 1, 0)
    upper = moved(own, -1, 0)
    partner, table = lax.optimization_barrier((partner, table))
    partner_upper = moved(partner, -1, 0)
    partner_lower = moved(partner, 1, 0)
    far = moved(lower, 1, 0)
    partner_far = moved(partner_upper, -1, 0)
    return (own, partner, lower, upper), (far, partner_lower, partner_upper, partner_far), table


def gather_rows(own):
    partner = moved(own, 0, 1)
    lower = moved(own, 1, 0)
    upper = moved(own, -1, 0)
    far = moved(own, 2, 0)
    partner_lower = moved(lower, 0, 1)
    partner_upper = moved(upper, 0, 1)
    partner_far = moved(partner, 2, 0)
    return (own, partner, lower, upper), (far, partner_lower, partner_upper, partner_far)


def table_kernel(rows_dev, slots, window, block_ref, product_ref, table_ref):
    total_rows = block_ref.shape[1]
    entries = block_ref.shape[0]
    narrow_count = entries // slots
    narrow_at = lax.axis_index("narrow")
    first_row = lax.axis_index("wide") * rows_dev
    first_goal = lax.axis_index("wide") * window
    step = rows_dev // window
    ext_rows = 3 * rows_dev - step
    pad = ext_rows * slots
    row = lax.broadcasted_iota(jnp.int32, (1, total_rows), 1)
    goal = lax.broadcasted_iota(jnp.int32, (1, product_ref.shape[1]), 1)
    entry = lax.broadcasted_iota(jnp.int32, (entries, 1), 0)
    source = jnp.zeros((entries, 1), jnp.int32)
    for n in range(1, narrow_count):
        source += (entry >= n * slots).astype(jnp.int32)
    ext_row = row - first_row + rows_dev
    ext_row = jnp.where(ext_row < 0, ext_row + total_rows, ext_row)
    ext_row = jnp.where(ext_row >= total_rows, ext_row - total_rows, ext_row)
    inside = ext_row < ext_rows
    mine = [pl.ds(narrow_at * slots + t, 1) for t in range(slots)]
    right = [jnp.where(inside, block_ref[mine[t], :], -1) for t in range(slots)]
    table = jnp.full(table_ref.shape, pad, jnp.int32)
    column = lax.broadcasted_iota(jnp.int32, table_ref.shape, 1)

    def pick(values, where):
        return jnp.sum(jnp.where(where, values, 0), axis=1, keepdims=True)

    for g in range(window):
        at_goal = goal == first_goal + g
        names = []
        for q in range(slots):
            target = pick(product_ref[mine[q], :], at_goal)
            target = jnp.where(target < 0, -2, target)
            name = jnp.zeros((1, total_rows), jnp.int32)
            for t in range(slots):
                name = jnp.where(right[t] == target, ext_row * slots + (t - pad), name)
            names.append(name)
        for stage in range(2):
            if stage == 0:
                col = pick(block_ref[...], row == first_row + g * step)
            else:
                col = pick(product_ref[...], at_goal)
            meets = row == jnp.where(col < 0, -1, col * narrow_count + source)
            for q in range(slots):
                found = pick(names[q], meets) + pad
                table = jnp.where(column == 16 * stage + g * slots + q, found, table)
    table_ref[...] = table


def build_table(block_list, product_list, rows_dev, slots, window):
    return pl.pallas_call(
        functools.partial(table_kernel, rows_dev, slots, window),
        out_shape=jax.ShapeDtypeStruct((block_list.shape[1], LANES), jnp.int32),
        in_specs=[LOCAL] * 2,
        out_specs=LOCAL,
        compiler_params=pltpu.CompilerParams(vmem_limit_bytes=4 * 1024 * 1024),
        name="block_table",
        cost_estimate=pl.CostEstimate(flops=0, bytes_accessed=3_000_000, transcendentals=0),
    )(block_list.T, product_list.T)


LOCAL = pl.BlockSpec(memory_space=pltpu.VMEM)
SCALAR = pl.BlockSpec(memory_space=pltpu.SMEM)
PARAMS = pltpu.CompilerParams(vmem_limit_bytes=8 * 1024 * 1024)
COST = pl.CostEstimate(flops=600_000_000, bytes_accessed=6_000_000, transcendentals=0)


def add_products(stage, half, window, slots, table, lefts, ext, start, out_ref):
    capacity = HALF * slots
    size = out_ref.shape[2]
    pair = 2
    narrow_at = lax.axis_index("narrow")
    y_at = narrow_at // 2
    x_at = lax.rem(narrow_at, 2)
    entry = []
    for dy, dx in SOURCES[half * HALF : (half + 1) * HALF]:
        source = lax.rem(y_at + (dy + Y), Y) * 2 + lax.rem(x_at + dx, 2)
        entry += [source * slots + s for s in range(slots)]
    for g in range(window):
        total = [None if start is None else start[g, q] for q in range(slots)]
        for e in range(0, capacity, pair):
            near = range(e, e + pair)
            left = jnp.concatenate([lefts[i // slots][g, i % slots] for i in near], axis=1)
            right = jnp.concatenate(
                [
                    jnp.concatenate(
                        [ext[table[entry[i], 16 * stage + g * slots + q]] for i in near], axis=0
                    )
                    for q in range(slots)
                ],
                axis=1,
            )
            term = jnp.dot(left, right, preferred_element_type=jnp.float32)
            for q in range(slots):
                piece = term[:, q * size : (q + 1) * size]
                total[q] = piece if total[q] is None else total[q] + piece
        for q in range(slots):
            out_ref[g, q] = total[q].astype(out_ref.dtype)


def first_kernel(window, slots, table, *rest):
    lefts, (chip, own, next_chip, out_ref, ext, sem) = rest[:HALF], rest[HALF:]
    rows = own.shape[0]
    tail = ext.shape[0] - slots - 2 * rows
    even = lax.rem(lax.axis_index("wide"), 2) == 0

    def lay_out(below, above):
        copies = [
            (below, ext.at[pl.ds(0, rows)]),
            (own, ext.at[pl.ds(rows, rows)]),
            (above.at[pl.ds(0, tail)], ext.at[pl.ds(2 * rows, tail)]),
        ]
        copies = [pltpu.make_async_copy(a, b, sem.at[i]) for i, (a, b) in enumerate(copies)]
        for copy in copies:
            copy.start()
        for copy in copies:
            copy.wait()

    for s in range(slots):
        ext[ext.shape[0] - slots + s] = jnp.zeros(ext.shape[1:], ext.dtype)
    pl.when(even)(lambda: lay_out(next_chip, chip))
    pl.when(jnp.logical_not(even))(lambda: lay_out(chip, next_chip))
    add_products(0, 0, window, slots, table, lefts, ext, None, out_ref)


def next_kernel(stage, half, window, slots, table, *rest):
    lefts, rest = rest[:HALF], rest[HALF:]
    if len(rest) == 3:
        ext, start, out_ref = rest
    else:
        (ext, out_ref), start = rest, None
    add_products(stage, half, window, slots, table, lefts, ext, start, out_ref)


def multiply_first(table, lefts, rights, window, slots):
    block = lefts[0].shape[2:]
    rows = rights[0].shape[0]
    ext_blocks = 3 * rows - rows // window + slots
    return pl.pallas_call(
        functools.partial(first_kernel, window, slots),
        out_shape=(
            jax.ShapeDtypeStruct((window, slots) + block, jnp.float32),
            jax.ShapeDtypeStruct((ext_blocks,) + block, jnp.bfloat16),
        ),
        in_specs=[SCALAR] + [LOCAL] * (HALF + 3),
        out_specs=(LOCAL, LOCAL),
        scratch_shapes=[pltpu.SemaphoreType.DMA((3,))],
        compiler_params=PARAMS,
        name="first_products",
        cost_estimate=COST,
    )(table, *lefts, *rights)


def multiply(stage, half, table, lefts, ext, start, window, slots, out_type):
    block = lefts[0].shape[2:]
    extra = () if start is None else (start,)
    return pl.pallas_call(
        functools.partial(next_kernel, stage, half, window, slots),
        out_shape=jax.ShapeDtypeStruct((window, slots) + block, out_type),
        in_specs=[SCALAR] + [LOCAL] * (HALF + 1 + len(extra)),
        out_specs=LOCAL,
        compiler_params=PARAMS,
        name="next_products",
        cost_estimate=COST,
    )(table, *lefts, ext, *extra)


def swapped(x, axis, first):
    peers = lax.axis_size(axis)
    pairs = []
    for i in range(first, peers + first, 2):
        a, b = i % peers, (i + 1) % peers
        pairs += [(a, b), (b, a)]
    return lax.ppermute(x, axis, pairs)


def per_device(density, block_list, product_list):
    rows_dev, slots = density.shape[:2]
    window = product_list.shape[0] // lax.axis_size("wide")
    step = rows_dev // window
    table = build_table(block_list, product_list, rows_dev, slots, window)
    blocks = density.reshape((rows_dev * slots,) + density.shape[2:])
    next_chip = swapped(blocks, "wide", 1)
    local = density.reshape((window, step) + density.shape[1:])[:, 0]
    early, late, table = gather_rows_by_y(local, table)
    chip = swapped(blocks, "wide", 0)
    part, ext = multiply_first(table, early, (chip, blocks, next_chip), window, slots)
    square = multiply(0, 1, table, late, ext, part, window, slots, jnp.bfloat16)
    early, late = gather_rows(square)
    part = multiply(1, 0, table, early, ext, None, window, slots, jnp.float32)
    cube = multiply(1, 1, table, late, ext, part, window, slots, jnp.bfloat16)
    return square, cube


def solution(mesh):
    placed = P("wide", "narrow", None, None)
    return jax.shard_map(
        per_device,
        mesh=mesh,
        in_specs=(placed, P(), P()),
        out_specs=(placed, placed),
        check_vma=False,
    )
```

time: 112 us -> 112 us (level)
  waiting for transfers between devices: 28.2 us -> 40.2 us
  Pallas kernels: 18.6 us -> 9.7 us
  local copies, waits for them, and re-layouts: 7.05 us -> 5.05 us
  starting transfers between devices: 56.1 us -> 54.6 us
    ppermute x14, waiting for transfers between devices: 28.2 us -> 40.1 us  [moved(): return lax.ppermute(a, 'narrow', pairs)]
    pallas_call x5 -> x4, Pallas kernels: 15.9 us -> 7.46 us  [the longest x3 6.72 us: multiply(): pl.pallas_call(functools.partial(next_kernel, stage, half, window, slots)...]
    ppermute x14, starting transfers between devices: 40.8 us -> 38.8 us  [moved(): return lax.ppermute(a, 'narrow', pairs)]
    unnamed x16 -> x8, local copies, waits for them, and re-layouts: 6.02 us -> 4.02 us
  transfers between devices with their start and end apart: 16 -> 16, of which waited for: 7 -> 8; matrix products, arithmetic and copies ran while one was open for 0% -> 1% of each run, Pallas kernels for 13% -> 4%
where the time goes in v3:
time: 112 us; the launch traced here: 110 us
  starting transfers between devices  54.6 us (49%)
  waiting for transfers between devices  40.2 us (36%)
  Pallas kernels  9.7 us (9%)
  local copies, waits for them, and re-layouts  5.05 us (5%)
    ppermute x14, waiting for transfers between devices, moved(): return lax.ppermute(a, 'narrow', pairs)  40.1 us
    ppermute x14, starting transfers between devices, moved(): return lax.ppermute(a, 'narrow', pairs)  38.8 us
    ppermute x2, starting transfers between devices, swapped(): return lax.ppermute(x, axis, pairs)  15.9 us
    pallas_call x3, Pallas kernels, multiply(): pl.pallas_call(functools.partial(next_kernel, stage, half, window, slots)...  6.72 us
    unnamed x8, local copies, waits for them, and re-layouts  4.02 us
  transfers between devices with their start and end apart: 16, of which 8 were waited for; matrix products, arithmetic and copies ran while one was open for 1% of the time, Pallas kernels for 4%

profile of v3, /device:TPU:24, one launch (start us, length us, event | category | flops | bytes accessed | tf_op | source)
XLA Modules:
  0.0 110.4 jit_solution(12698079560248537348)
XLA Ops:
  0.6 1.9 %collective-permute-start.7 = (bf16[48,128,128]{2,1,0:T(8,128)(2,1)}, bf16[48,128,128]{2,1,0:T(8,128)(2,1)S(1)}, u32[]{:S(2)}, u32[]{:S(2)}) collective-permute-start(bf16[48,128,128]{2,1,0:T(8,128)(2,1)} %bitcast.8), channel_id=1, source_target_pairs={{0,8},{8,0},{16,24},{24,16},{32,40},{40,32},{48,56},{56,48},{64,72... | collective-permute-start | bytes 4718600 | tf_op jit(solution)/shard_map/ppermute | solution.py:221
  2.6 14.0 %collective-permute-start.8 = (bf16[48,128,128]{2,1,0:T(8,128)(2,1)}, bf16[48,128,128]{2,1,0:T(8,128)(2,1)S(1)}, u32[]{:S(2)}, u32[]{:S(2)}) collective-permute-start(bf16[48,128,128]{2,1,0:T(8,128)(2,1)} %bitcast.9), channel_id=1, source_target_pairs={{8,16},{16,8},{24,32},{32,24},{40,48},{48,40},{56,64},{64,56},{72,... | collective-permute-start | bytes 4718600 | tf_op jit(solution)/shard_map/ppermute | solution.py:221
  17.6 2.5 %collective-permute-start = (bf16[4,3,128,128]{3,2,1,0:T(8,128)(2,1)S(1)}, bf16[4,3,128,128]{3,2,1,0:T(8,128)(2,1)S(1)}, u32[]{:S(2)}, u32[]{:S(2)}) collective-permute-start(bf16[4,3,128,128]{3,2,1,0:T(8,128)(2,1)S(1)} %slice_bitcast_fusion.rest_0_), channel_id=1, source_target_pairs={{0,1},{1,0},{2,3},{3,2},{4,5},{5,4},{6,7},{7,6},{8,9},{9,8},{10,11... | collective-permute-start | bytes 1179656 | tf_op jit(solution)/shard_map/ppermute | solution.py:21
  20.1 2.1 %collective-permute-start.1 = (bf16[4,3,128,128]{3,2,1,0:T(8,128)(2,1)S(1)}, bf16[4,3,128,128]{3,2,1,0:T(8,128)(2,1)S(1)}, u32[]{:S(2)}, u32[]{:S(2)}) collective-permute-start(bf16[4,3,128,128]{3,2,1,0:T(8,128)(2,1)S(1)} %slice_bitcast_fusion.rest_0_), channel_id=1, source_target_pairs={{0,2},{1,3},{2,4},{3,5},{4,6},{5,7},{6,0},{7,1},{8,10},{9,11},{10,... | collective-permute-start | bytes 1179656 | tf_op jit(solution)/shard_map/ppermute | solution.py:21
  22.2 3.7 %collective-permute-start.6 = (bf16[4,3,128,128]{3,2,1,0:T(8,128)(2,1)S(1)}, bf16[4,3,128,128]{3,2,1,0:T(8,128)(2,1)S(1)}, u32[]{:S(2)}, u32[]{:S(2)}) collective-permute-start(bf16[4,3,128,128]{3,2,1,0:T(8,128)(2,1)S(1)} %slice_bitcast_fusion.rest_0_), channel_id=1, source_target_pairs={{0,6},{1,7},{2,0},{3,1},{4,2},{5,3},{6,4},{7,5},{8,14},{9,15},{10,... | collective-permute-start | bytes 1179656 | tf_op jit(solution)/shard_map/ppermute | solution.py:21
  28.3 9.2 %collective-permute-done.rest_1_ = bf16[4,3,128,128]{3,2,1,0:T(8,128)(2,1)S(1)} collective-permute-done((bf16[4,3,128,128]{3,2,1,0:T(8,128)(2,1)S(1)}, bf16[4,3,128,128]{3,2,1,0:T(8,128)(2,1)S(1)}, u32[]{:S(2)}, u32[]{:S(2)}) %collective-permute-start) | collective-permute-done | bytes 393248 | tf_op jit(solution)/shard_map/ppermute | solution.py:21
  37.5 2.6 %collective-permute-start.4 = (bf16[4,3,128,128]{3,2,1,0:T(8,128)(2,1)S(1)}, bf16[4,3,128,128]{3,2,1,0:T(8,128)(2,1)S(1)}, u32[]{:S(2)}, u32[]{:S(2)}) collective-permute-start(bf16[4,3,128,128]{3,2,1,0:T(8,128)(2,1)S(1)} %collective-permute-done.rest_1_), channel_id=1, source_target_pairs={{0,6},{1,7},{2,0},{3,1},{4,2},{5,3},{6,4},{7,5},{8,14},{9,15},{10,... | collective-permute-start | bytes 1179656 | tf_op jit(solution)/shard_map/ppermute | solution.py:21
  40.2 5.1 %collective-permute-start.3 = (bf16[4,3,128,128]{3,2,1,0:T(8,128)(2,1)S(1)}, bf16[4,3,128,128]{3,2,1,0:T(8,128)(2,1)S(1)}, u32[]{:S(2)}, u32[]{:S(2)}) collective-permute-start(bf16[4,3,128,128]{3,2,1,0:T(8,128)(2,1)S(1)} %collective-permute-done.rest_1_), channel_id=1, source_target_pairs={{0,2},{1,3},{2,4},{3,5},{4,6},{5,7},{6,0},{7,1},{8,10},{9,11},{10,... | collective-permute-start | bytes 1179656 | tf_op jit(solution)/shard_map/ppermute | solution.py:21
  45.2 3.9 %collective-permute-start.2 = (bf16[4,3,128,128]{3,2,1,0:T(8,128)(2,1)S(1)}, bf16[4,3,128,128]{3,2,1,0:T(8,128)(2,1)S(1)}, u32[]{:S(2)}, u32[]{:S(2)}) collective-permute-start(bf16[4,3,128,128]{3,2,1,0:T(8,128)(2,1)S(1)} %collective-permute-done.1.rest_2_), channel_id=1, source_target_pairs={{0,2},{1,3},{2,4},{3,5},{4,6},{5,7},{6,0},{7,1},{8,10},{9,11},{10,... | collective-permute-start | bytes 1179656 | tf_op jit(solution)/shard_map/ppermute | solution.py:21
  49.2 2.8 %collective-permute-done.4.rest_2_ = bf16[4,3,128,128]{3,2,1,0:T(8,128)(2,1)S(1)} collective-permute-done((bf16[4,3,128,128]{3,2,1,0:T(8,128)(2,1)S(1)}, bf16[4,3,128,128]{3,2,1,0:T(8,128)(2,1)S(1)}, u32[]{:S(2)}, u32[]{:S(2)}) %collective-permute-start.4) | collective-permute-done | bytes 393248 | tf_op jit(solution)/shard_map/ppermute | solution.py:21
  55.3 2.2 %first_products.1 = (f32[4,3,128,128]{3,2,1,0:T(8,128)S(1)}, bf16[135,128,128]{2,1,0:T(8,128)(2,1)S(1)}) custom-call(s32[24,128]{1,0:T(8,128)S(1)} %block_table.1.table, bf16[4,3,128,128]{3,2,1,0:T(8,128)(2,1)S(1)} %slice_bitcast_fusion.rest_0_, bf16[4,3,128,128]{3,2,1,0:T(8,128)(2,1)S(1)} %collective-permute-done.rest_1_, ...), custom_call_target="tpu_custom_call" | custom-call | flops 600000000 | bytes 6000000 | tf_op jit(solution)/shard_map/first_products/pallas_call | solution.py:186
  57.6 4.0 %collective-permute-done.2.rest_0_ = bf16[4,3,128,128]{3,2,1,0:T(8,128)(2,1)S(1)} collective-permute-done((bf16[4,3,128,128]{3,2,1,0:T(8,128)(2,1)S(1)}, bf16[4,3,128,128]{3,2,1,0:T(8,128)(2,1)S(1)}, u32[]{:S(2)}, u32[]{:S(2)}) %collective-permute-start.2) | collective-permute-done | bytes 393248 | tf_op jit(solution)/shard_map/ppermute | solution.py:21
  61.6 3.3 %collective-permute-done.5.rest_3_ = bf16[4,3,128,128]{3,2,1,0:T(8,128)(2,1)S(1)} collective-permute-done((bf16[4,3,128,128]{3,2,1,0:T(8,128)(2,1)S(1)}, bf16[4,3,128,128]{3,2,1,0:T(8,128)(2,1)S(1)}, u32[]{:S(2)}, u32[]{:S(2)}) %collective-permute-start.5) | collective-permute-done | bytes 393248 | tf_op jit(solution)/shard_map/ppermute | solution.py:21
  64.8 2.5 %next_products.3.rest_0_ = bf16[4,3,128,128]{3,2,1,0:T(8,128)(2,1)} custom-call(s32[24,128]{1,0:T(8,128)S(1)} %block_table.1.table, bf16[4,3,128,128]{3,2,1,0:T(8,128)(2,1)S(1)} %collective-permute-done.2.rest_0_, bf16[4,3,128,128]{3,2,1,0:T(8,128)(2,1)S(1)} %collective-permute-done.3.rest_1_, bf16[4,3,128,128]{3,2,1,0:T(8,128)(2,1)S(1)} %collective-permute-done.4.rest_2_, ...), custom_call_target="tpu_custom_call" | custom-call | flops 600000000 | bytes 6000000 | tf_op jit(solution)/shard_map/next_products/pallas_call | solution.py:204
  67.3 2.3 %collective-permute-start.10 = (bf16[4,3,128,128]{3,2,1,0:T(8,128)(2,1)}, bf16[4,3,128,128]{3,2,1,0:T(8,128)(2,1)S(1)}, u32[]{:S(2)}, u32[]{:S(2)}) collective-permute-start(bf16[4,3,128,128]{3,2,1,0:T(8,128)(2,1)} %next_products.3.rest_0_), channel_id=1, source_target_pairs={{0,2},{1,3},{2,4},{3,5},{4,6},{5,7},{6,0},{7,1},{8,10},{9,11},{10,... | collective-permute-start | bytes 1179656 | tf_op jit(solution)/shard_map/ppermute | solution.py:21
  69.7 3.5 %collective-permute-start.12 = (bf16[4,3,128,128]{3,2,1,0:T(8,128)(2,1)}, bf16[4,3,128,128]{3,2,1,0:T(8,128)(2,1)S(1)}, u32[]{:S(2)}, u32[]{:S(2)}) collective-permute-start(bf16[4,3,128,128]{3,2,1,0:T(8,128)(2,1)} %next_products.3.rest_0_), channel_id=1, source_target_pairs={{0,6},{1,7},{2,0},{3,1},{4,2},{5,3},{6,4},{7,5},{8,14},{9,15},{10,... | collective-permute-start | bytes 1179656 | tf_op jit(solution)/shard_map/ppermute | solution.py:21
  73.2 1.9 %collective-permute-start.14 = (bf16[4,3,128,128]{3,2,1,0:T(8,128)(2,1)}, bf16[4,3,128,128]{3,2,1,0:T(8,128)(2,1)S(1)}, u32[]{:S(2)}, u32[]{:S(2)}) collective-permute-start(bf16[4,3,128,128]{3,2,1,0:T(8,128)(2,1)} %next_products.3.rest_0_), channel_id=1, source_target_pairs={{0,1},{1,0},{2,3},{3,2},{4,5},{5,4},{6,7},{7,6},{8,9},{9,8},{10,11... | collective-permute-start | bytes 1179656 | tf_op jit(solution)/shard_map/ppermute | solution.py:21
  75.1 2.3 %collective-permute-start.9 = (bf16[4,3,128,128]{3,2,1,0:T(8,128)(2,1)}, bf16[4,3,128,128]{3,2,1,0:T(8,128)(2,1)S(1)}, u32[]{:S(2)}, u32[]{:S(2)}) collective-permute-start(bf16[4,3,128,128]{3,2,1,0:T(8,128)(2,1)} %next_products.3.rest_0_), channel_id=1, source_target_pairs={{0,4},{1,5},{2,6},{3,7},{4,0},{5,1},{6,2},{7,3},{8,12},{9,13},{10,... | collective-permute-start | bytes 1179656 | tf_op jit(solution)/shard_map/ppermute | solution.py:21
  78.3 3.0 %collective-permute-start.11 = (bf16[4,3,128,128]{3,2,1,0:T(8,128)(2,1)S(1)}, bf16[4,3,128,128]{3,2,1,0:T(8,128)(2,1)S(1)}, u32[]{:S(2)}, u32[]{:S(2)}) collective-permute-start(bf16[4,3,128,128]{3,2,1,0:T(8,128)(2,1)S(1)} %collective-permute-done.10.rest_2_), channel_id=1, source_target_pairs={{0,1},{1,0},{2,3},{3,2},{4,5},{5,4},{6,7},{7,6},{8,9},{9,8},{10,11... | collective-permute-start | bytes 1179656 | tf_op jit(solution)/shard_map/ppermute | solution.py:21
  81.3 13.5 %collective-permute-done.12.rest_3_ = bf16[4,3,128,128]{3,2,1,0:T(8,128)(2,1)S(1)} collective-permute-done((bf16[4,3,128,128]{3,2,1,0:T(8,128)(2,1)}, bf16[4,3,128,128]{3,2,1,0:T(8,128)(2,1)S(1)}, u32[]{:S(2)}, u32[]{:S(2)}) %collective-permute-start.12) | collective-permute-done | bytes 393248 | tf_op jit(solution)/shard_map/ppermute | solution.py:21
  96.7 1.9 %collective-permute-start.15 = (bf16[4,3,128,128]{3,2,1,0:T(8,128)(2,1)S(1)}, bf16[4,3,128,128]{3,2,1,0:T(8,128)(2,1)S(1)}, u32[]{:S(2)}, u32[]{:S(2)}) collective-permute-start(bf16[4,3,128,128]{3,2,1,0:T(8,128)(2,1)S(1)} %collective-permute-done.14.rest_1_), channel_id=1, source_target_pairs={{0,4},{1,5},{2,6},{3,7},{4,0},{5,1},{6,2},{7,3},{8,12},{9,13},{10,... | collective-permute-start | bytes 1179656 | tf_op jit(solution)/shard_map/ppermute | solution.py:21
  101.4 3.0 %collective-permute-done.13.rest_2_ = bf16[4,3,128,128]{3,2,1,0:T(8,128)(2,1)S(1)} collective-permute-done((bf16[4,3,128,128]{3,2,1,0:T(8,128)(2,1)S(1)}, bf16[4,3,128,128]{3,2,1,0:T(8,128)(2,1)S(1)}, u32[]{:S(2)}, u32[]{:S(2)}) %collective-permute-start.13) | collective-permute-done | bytes 393248 | tf_op jit(solution)/shard_map/ppermute | solution.py:21
  104.5 3.4 %collective-permute-done.15.rest_3_ = bf16[4,3,128,128]{3,2,1,0:T(8,128)(2,1)S(1)} collective-permute-done((bf16[4,3,128,128]{3,2,1,0:T(8,128)(2,1)S(1)}, bf16[4,3,128,128]{3,2,1,0:T(8,128)(2,1)S(1)}, u32[]{:S(2)}, u32[]{:S(2)}) %collective-permute-start.15) | collective-permute-done | bytes 393248 | tf_op jit(solution)/shard_map/ppermute | solution.py:21
  107.9 2.5 %next_products.5 = bf16[4,3,128,128]{3,2,1,0:T(8,128)(2,1)} custom-call(s32[24,128]{1,0:T(8,128)S(1)} %block_table.1.table, bf16[4,3,128,128]{3,2,1,0:T(8,128)(2,1)S(1)} %collective-permute-done.9.rest_0_, bf16[4,3,128,128]{3,2,1,0:T(8,128)(2,1)S(1)} %collective-permute-done.11.rest_1_, bf16[4,3,128,128]{3,2,1,0:T(8,128)(2,1)S(1)} %collective-permute-done.13.rest_2_, ...), custom_call_target="tpu_custom_call" | custom-call | flops 600000000 | bytes 6000000 | tf_op jit(solution)/shard_map/next_products/pallas_call | solution.py:204
  (22 shorter events, 12.3 us)
Async XLA Ops:
  0.6 53.2 %collective-permute-start.7 = (bf16[48,128,128]{2,1,0:T(8,128)(2,1)}, bf16[48,128,128]{2,1,0:T(8,128)(2,1)S(1)}, u32[]{:S(2)}, u32[]{:S(2)}) collective-permute-start(bf16[48,128,128]{2,1,0:T(8,128)(2,1)} %bitcast.8), channel_id=1, source_target_pairs={{0,8},{8,0},{16,24},{24,16},{32,40},{40,32},{48,56},{56,48},{64,72... | collective-permute-start | bytes 4718600 | tf_op jit(solution)/shard_map/ppermute | solution.py:221
  2.6 51.3 %collective-permute-start.8 = (bf16[48,128,128]{2,1,0:T(8,128)(2,1)}, bf16[48,128,128]{2,1,0:T(8,128)(2,1)S(1)}, u32[]{:S(2)}, u32[]{:S(2)}) collective-permute-start(bf16[48,128,128]{2,1,0:T(8,128)(2,1)} %bitcast.9), channel_id=1, source_target_pairs={{8,16},{16,8},{24,32},{32,24},{40,48},{48,40},{56,64},{64,56},{72,... | collective-permute-start | bytes 4718600 | tf_op jit(solution)/shard_map/ppermute | solution.py:221
  17.6 19.9 %collective-permute-start = (bf16[4,3,128,128]{3,2,1,0:T(8,128)(2,1)S(1)}, bf16[4,3,128,128]{3,2,1,0:T(8,128)(2,1)S(1)}, u32[]{:S(2)}, u32[]{:S(2)}) collective-permute-start(bf16[4,3,128,128]{3,2,1,0:T(8,128)(2,1)S(1)} %slice_bitcast_fusion.rest_0_), channel_id=1, source_target_pairs={{0,1},{1,0},{2,3},{3,2},{4,5},{5,4},{6,7},{7,6},{8,9},{9,8},{10,11... | collective-permute-start | bytes 1179656 | tf_op jit(solution)/shard_map/ppermute | solution.py:21
  20.1 20.1 %collective-permute-start.1 = (bf16[4,3,128,128]{3,2,1,0:T(8,128)(2,1)S(1)}, bf16[4,3,128,128]{3,2,1,0:T(8,128)(2,1)S(1)}, u32[]{:S(2)}, u32[]{:S(2)}) collective-permute-start(bf16[4,3,128,128]{3,2,1,0:T(8,128)(2,1)S(1)} %slice_bitcast_fusion.rest_0_), channel_id=1, source_target_pairs={{0,2},{1,3},{2,4},{3,5},{4,6},{5,7},{6,0},{7,1},{8,10},{9,11},{10,... | collective-permute-start | bytes 1179656 | tf_op jit(solution)/shard_map/ppermute | solution.py:21
  22.2 23.0 %collective-permute-start.6 = (bf16[4,3,128,128]{3,2,1,0:T(8,128)(2,1)S(1)}, bf16[4,3,128,128]{3,2,1,0:T(8,128)(2,1)S(1)}, u32[]{:S(2)}, u32[]{:S(2)}) collective-permute-start(bf16[4,3,128,128]{3,2,1,0:T(8,128)(2,1)S(1)} %slice_bitcast_fusion.rest_0_), channel_id=1, source_target_pairs={{0,6},{1,7},{2,0},{3,1},{4,2},{5,3},{6,4},{7,5},{8,14},{9,15},{10,... | collective-permute-start | bytes 1179656 | tf_op jit(solution)/shard_map/ppermute | solution.py:21
  25.9 0.9 copy-start.2
  26.8 0.7 copy-start.3
  37.5 14.4 %collective-permute-start.4 = (bf16[4,3,128,128]{3,2,1,0:T(8,128)(2,1)S(1)}, bf16[4,3,128,128]{3,2,1,0:T(8,128)(2,1)S(1)}, u32[]{:S(2)}, u32[]{:S(2)}) collective-permute-start(bf16[4,3,128,128]{3,2,1,0:T(8,128)(2,1)S(1)} %collective-permute-done.rest_1_), channel_id=1, source_target_pairs={{0,6},{1,7},{2,0},{3,1},{4,2},{5,3},{6,4},{7,5},{8,14},{9,15},{10,... | collective-permute-start | bytes 1179656 | tf_op jit(solution)/shard_map/ppermute | solution.py:21
  40.2 17.4 %collective-permute-start.3 = (bf16[4,3,128,128]{3,2,1,0:T(8,128)(2,1)S(1)}, bf16[4,3,128,128]{3,2,1,0:T(8,128)(2,1)S(1)}, u32[]{:S(2)}, u32[]{:S(2)}) collective-permute-start(bf16[4,3,128,128]{3,2,1,0:T(8,128)(2,1)S(1)} %collective-permute-done.rest_1_), channel_id=1, source_target_pairs={{0,2},{1,3},{2,4},{3,5},{4,6},{5,7},{6,0},{7,1},{8,10},{9,11},{10,... | collective-permute-start | bytes 1179656 | tf_op jit(solution)/shard_map/ppermute | solution.py:21
  45.2 16.3 %collective-permute-start.2 = (bf16[4,3,128,128]{3,2,1,0:T(8,128)(2,1)S(1)}, bf16[4,3,128,128]{3,2,1,0:T(8,128)(2,1)S(1)}, u32[]{:S(2)}, u32[]{:S(2)}) collective-permute-start(bf16[4,3,128,128]{3,2,1,0:T(8,128)(2,1)S(1)} %collective-permute-done.1.rest_2_), channel_id=1, source_target_pairs={{0,2},{1,3},{2,4},{3,5},{4,6},{5,7},{6,0},{7,1},{8,10},{9,11},{10,... | collective-permute-start | bytes 1179656 | tf_op jit(solution)/shard_map/ppermute | solution.py:21
  51.9 12.9 %collective-permute-start.5 = (bf16[4,3,128,128]{3,2,1,0:T(8,128)(2,1)S(1)}, bf16[4,3,128,128]{3,2,1,0:T(8,128)(2,1)S(1)}, u32[]{:S(2)}, u32[]{:S(2)}) collective-permute-start(bf16[4,3,128,128]{3,2,1,0:T(8,128)(2,1)S(1)} %collective-permute-done.4.rest_2_), channel_id=1, source_target_pairs={{0,6},{1,7},{2,0},{3,1},{4,2},{5,3},{6,4},{7,5},{8,14},{9,15},{10,... | collective-permute-start | bytes 1179656 | tf_op jit(solution)/shard_map/ppermute | solution.py:21
  53.9 1.4 %copy-start = (bf16[16,3,128,128]{3,2,1,0:T(8,128)(2,1)S(1)}, bf16[16,3,128,128]{3,2,1,0:T(8,128)(2,1)}, u32[]{:S(2)}) copy-start(bf16[16,3,128,128]{3,2,1,0:T(8,128)(2,1)} %param.3) | copy-start | bytes 4718596
  67.3 11.0 %collective-permute-start.10 = (bf16[4,3,128,128]{3,2,1,0:T(8,128)(2,1)}, bf16[4,3,128,128]{3,2,1,0:T(8,128)(2,1)S(1)}, u32[]{:S(2)}, u32[]{:S(2)}) collective-permute-start(bf16[4,3,128,128]{3,2,1,0:T(8,128)(2,1)} %next_products.3.rest_0_), channel_id=1, source_target_pairs={{0,2},{1,3},{2,4},{3,5},{4,6},{5,7},{6,0},{7,1},{8,10},{9,11},{10,... | collective-permute-start | bytes 1179656 | tf_op jit(solution)/shard_map/ppermute | solution.py:21
  69.7 25.2 %collective-permute-start.12 = (bf16[4,3,128,128]{3,2,1,0:T(8,128)(2,1)}, bf16[4,3,128,128]{3,2,1,0:T(8,128)(2,1)S(1)}, u32[]{:S(2)}, u32[]{:S(2)}) collective-permute-start(bf16[4,3,128,128]{3,2,1,0:T(8,128)(2,1)} %next_products.3.rest_0_), channel_id=1, source_target_pairs={{0,6},{1,7},{2,0},{3,1},{4,2},{5,3},{6,4},{7,5},{8,14},{9,15},{10,... | collective-permute-start | bytes 1179656 | tf_op jit(solution)/shard_map/ppermute | solution.py:21
  73.2 23.6 %collective-permute-start.14 = (bf16[4,3,128,128]{3,2,1,0:T(8,128)(2,1)}, bf16[4,3,128,128]{3,2,1,0:T(8,128)(2,1)S(1)}, u32[]{:S(2)}, u32[]{:S(2)}) collective-permute-start(bf16[4,3,128,128]{3,2,1,0:T(8,128)(2,1)} %next_products.3.rest_0_), channel_id=1, source_target_pairs={{0,1},{1,0},{2,3},{3,2},{4,5},{5,4},{6,7},{7,6},{8,9},{9,8},{10,11... | collective-permute-start | bytes 1179656 | tf_op jit(solution)/shard_map/ppermute | solution.py:21
  75.1 26.3 %collective-permute-start.9 = (bf16[4,3,128,128]{3,2,1,0:T(8,128)(2,1)}, bf16[4,3,128,128]{3,2,1,0:T(8,128)(2,1)S(1)}, u32[]{:S(2)}, u32[]{:S(2)}) collective-permute-start(bf16[4,3,128,128]{3,2,1,0:T(8,128)(2,1)} %next_products.3.rest_0_), channel_id=1, source_target_pairs={{0,4},{1,5},{2,6},{3,7},{4,0},{5,1},{6,2},{7,3},{8,12},{9,13},{10,... | collective-permute-start | bytes 1179656 | tf_op jit(solution)/shard_map/ppermute | solution.py:21
  78.3 23.1 %collective-permute-start.11 = (bf16[4,3,128,128]{3,2,1,0:T(8,128)(2,1)S(1)}, bf16[4,3,128,128]{3,2,1,0:T(8,128)(2,1)S(1)}, u32[]{:S(2)}, u32[]{:S(2)}) collective-permute-start(bf16[4,3,128,128]{3,2,1,0:T(8,128)(2,1)S(1)} %collective-permute-done.10.rest_2_), channel_id=1, source_target_pairs={{0,1},{1,0},{2,3},{3,2},{4,5},{5,4},{6,7},{7,6},{8,9},{9,8},{10,11... | collective-permute-start | bytes 1179656 | tf_op jit(solution)/shard_map/ppermute | solution.py:21
  94.8 9.7 %collective-permute-start.13 = (bf16[4,3,128,128]{3,2,1,0:T(8,128)(2,1)S(1)}, bf16[4,3,128,128]{3,2,1,0:T(8,128)(2,1)S(1)}, u32[]{:S(2)}, u32[]{:S(2)}) collective-permute-start(bf16[4,3,128,128]{3,2,1,0:T(8,128)(2,1)S(1)} %collective-permute-done.12.rest_3_), channel_id=1, source_target_pairs={{0,1},{1,0},{2,3},{3,2},{4,5},{5,4},{6,7},{7,6},{8,9},{9,8},{10,11... | collective-permute-start | bytes 1179656 | tf_op jit(solution)/shard_map/ppermute | solution.py:21
  96.7 11.2 %collective-permute-start.15 = (bf16[4,3,128,128]{3,2,1,0:T(8,128)(2,1)S(1)}, bf16[4,3,128,128]{3,2,1,0:T(8,128)(2,1)S(1)}, u32[]{:S(2)}, u32[]{:S(2)}) collective-permute-start(bf16[4,3,128,128]{3,2,1,0:T(8,128)(2,1)S(1)} %collective-permute-done.14.rest_1_), channel_id=1, source_target_pairs={{0,4},{1,5},{2,6},{3,7},{4,0},{5,1},{6,2},{7,3},{8,12},{9,13},{10,... | collective-permute-start | bytes 1179656 | tf_op jit(solution)/shard_map/ppermute | solution.py:21
  98.7 1.0 copy-start.1

commit v4 on v3

--- a/solution.py
+++ b/solution.py
@@ -9,6 +9,7 @@
 
 Y = 4
 LANES = 128
+ORDER_FLOPS = 7_000_000_000
 SOURCES = ((0, 0), (0, 1), (-1, 0), (1, 0), (2, 0), (-1, 1), (1, 1), (2, 1))
 HALF = len(SOURCES) // 2
 
@@ -106,21 +107,36 @@
     )(block_list.T, product_list.T)
 
 
+def passed(table, after):
+    def kernel(table_ref, *rest):
+        rest[-1][...] = table_ref[...]
+
+    return pl.pallas_call(
+        kernel,
+        out_shape=jax.ShapeDtypeStruct(table.shape, table.dtype),
+        in_specs=[LOCAL] + [pl.BlockSpec(memory_space=pl.ANY)] * len(after),
+        out_specs=LOCAL,
+        compiler_params=pltpu.CompilerParams(vmem_limit_bytes=1024 * 1024),
+        name="pass_table",
+        cost_estimate=pl.CostEstimate(flops=ORDER_FLOPS, bytes_accessed=0, transcendentals=0),
+    )(table, *after)
+
+
 LOCAL = pl.BlockSpec(memory_space=pltpu.VMEM)
 SCALAR = pl.BlockSpec(memory_space=pltpu.SMEM)
 PARAMS = pltpu.CompilerParams(vmem_limit_bytes=8 * 1024 * 1024)
 COST = pl.CostEstimate(flops=600_000_000, bytes_accessed=6_000_000, transcendentals=0)
 
 
-def add_products(stage, half, window, slots, table, lefts, ext, start, out_ref):
-    capacity = HALF * slots
+def add_products(stage, sources, window, slots, table, lefts, ext, start, out_ref):
+    capacity = len(lefts) * slots
     size = out_ref.shape[2]
     pair = 2
     narrow_at = lax.axis_index("narrow")
     y_at = narrow_at // 2
     x_at = lax.rem(narrow_at, 2)
     entry = []
-    for dy, dx in SOURCES[half * HALF : (half + 1) * HALF]:
+    for dy, dx in sources:
         source = lax.rem(y_at + (dy + Y), Y) * 2 + lax.rem(x_at + dx, 2)
         entry += [source * slots + s for s in range(slots)]
     for g in range(window):
@@ -146,7 +162,7 @@
 
 
 def first_kernel(window, slots, table, *rest):
-    lefts, (chip, own, next_chip, out_ref, ext, sem) = rest[:HALF], rest[HALF:]
+    lefts, (chip, own, next_chip, out_ref, ext, sem) = rest[: 2 * HALF], rest[2 * HALF :]
     rows = own.shape[0]
     tail = ext.shape[0] - slots - 2 * rows
     even = lax.rem(lax.axis_index("wide"), 2) == 0
@@ -167,16 +183,17 @@
         ext[ext.shape[0] - slots + s] = jnp.zeros(ext.shape[1:], ext.dtype)
     pl.when(even)(lambda: lay_out(next_chip, chip))
     pl.when(jnp.logical_not(even))(lambda: lay_out(chip, next_chip))
-    add_products(0, 0, window, slots, table, lefts, ext, None, out_ref)
-
-
-def next_kernel(stage, half, window, slots, table, *rest):
+    add_products(0, SOURCES, window, slots, table, lefts, ext, None, out_ref)
+
+
+def next_kernel(half, window, slots, table, *rest):
     lefts, rest = rest[:HALF], rest[HALF:]
     if len(rest) == 3:
         ext, start, out_ref = rest
     else:
         (ext, out_ref), start = rest, None
-    add_products(stage, half, window, slots, table, lefts, ext, start, out_ref)
+    sources = SOURCES[half * HALF : (half + 1) * HALF]
+    add_products(1, sources, window, slots, table, lefts, ext, start, out_ref)
 
 
 def multiply_first(table, lefts, rights, window, slots):
@@ -186,28 +203,28 @@
     return pl.pallas_call(
         functools.partial(first_kernel, window, slots),
         out_shape=(
-            jax.ShapeDtypeStruct((window, slots) + block, jnp.float32),
+            jax.ShapeDtypeStruct((window, slots) + block, jnp.bfloat16),
             jax.ShapeDtypeStruct((ext_blocks,) + block, jnp.bfloat16),
         ),
-        in_specs=[SCALAR] + [LOCAL] * (HALF + 3),
+        in_specs=[SCALAR] + [LOCAL] * (2 * HALF + 3),
         out_specs=(LOCAL, LOCAL),
         scratch_shapes=[pltpu.SemaphoreType.DMA((3,))],
         compiler_params=PARAMS,
-        name="first_products",
+        name="square_products",
         cost_estimate=COST,
     )(table, *lefts, *rights)
 
 
-def multiply(stage, half, table, lefts, ext, start, window, slots, out_type):
+def multiply(half, table, lefts, ext, start, window, slots, out_type):
     block = lefts[0].shape[2:]
     extra = () if start is None else (start,)
     return pl.pallas_call(
-        functools.partial(next_kernel, stage, half, window, slots),
+        functools.partial(next_kernel, half, window, slots),
         out_shape=jax.ShapeDtypeStruct((window, slots) + block, out_type),
         in_specs=[SCALAR] + [LOCAL] * (HALF + 1 + len(extra)),
         out_specs=LOCAL,
         compiler_params=PARAMS,
-        name="next_products",
+        name="cube_products",
         cost_estimate=COST,
     )(table, *lefts, ext, *extra)
 
@@ -225,17 +242,17 @@
     rows_dev, slots = density.shape[:2]
     window = product_list.shape[0] // lax.axis_size("wide")
     step = rows_dev // window
-    table = build_table(block_list, product_list, rows_dev, slots, window)
     blocks = density.reshape((rows_dev * slots,) + density.shape[2:])
     next_chip = swapped(blocks, "wide", 1)
     local = density.reshape((window, step) + density.shape[1:])[:, 0]
+    table = build_table(block_list, product_list, rows_dev, slots, window)
     early, late, table = gather_rows_by_y(local, table)
+    table = passed(table, early[1:] + late)
     chip = swapped(blocks, "wide", 0)
-    part, ext = multiply_first(table, early, (chip, blocks, next_chip), window, slots)
-    square = multiply(0, 1, table, late, ext, part, window, slots, jnp.bfloat16)
+    square, ext = multiply_first(table, early + late, (chip, blocks, next_chip), window, slots)
     early, late = gather_rows(square)
-    part = multiply(1, 0, table, early, ext, None, window, slots, jnp.float32)
-    cube = multiply(1, 1, table, late, ext, part, window, slots, jnp.bfloat16)
+    part = multiply(0, table, early, ext, None, window, slots, jnp.float32)
+    cube = multiply(1, table, late, ext, part, window, slots, jnp.bfloat16)
     return square, cube
 
 

time: 112 us -> 109 us (0.973)
  waiting for transfers between devices: 40.2 us -> 36.7 us
  starting transfers between devices: 54.6 us -> 58 us
  local copies, waits for them, and re-layouts: 5.05 us -> 3.65 us
    ppermute x14, starting transfers between devices: 38.8 us -> 43.4 us  [moved(): return lax.ppermute(a, 'narrow', pairs)]
    ppermute x14, waiting for transfers between devices: 40.1 us -> 36.7 us  [moved(): return lax.ppermute(a, 'narrow', pairs)]
    pallas_call x3, Pallas kernels: 6.72 us -> 4.2 us  [the longest x2 4.2 us: multiply(): pl.pallas_call(functools.partial(next_kernel, half, window, slots), out_s...]
    pallas_call x1, Pallas kernels: 2.24 us -> 3.85 us  [multiply_first(): pl.pallas_call(functools.partial(first_kernel, window, slots), out_shape=...]
    unnamed x8, local copies, waits for them, and re-layouts: 4.02 us -> 2.62 us
    ppermute x2, starting transfers between devices: 15.9 us -> 14.7 us  [swapped(): return lax.ppermute(x, axis, pairs)]
  transfers between devices with their start and end apart: 16 -> 16, of which waited for: 8 -> 8; matrix products, arithmetic and copies ran while one was open for 1% -> 0% of each run, Pallas kernels for 4% -> 2%
where the time goes in v4:
time: 109 us; the launch traced here: 108 us
  starting transfers between devices  58 us (53%)
  waiting for transfers between devices  36.7 us (34%)
  Pallas kernels  8.8 us (8%)
  local copies, waits for them, and re-layouts  3.65 us (3%)
    ppermute x14, starting transfers between devices, moved(): return lax.ppermute(a, 'narrow', pairs)  43.4 us
    ppermute x14, waiting for transfers between devices, moved(): return lax.ppermute(a, 'narrow', pairs)  36.7 us
    ppermute x2, starting transfers between devices, swapped(): return lax.ppermute(x, axis, pairs)  14.7 us
    pallas_call x2, Pallas kernels, multiply(): pl.pallas_call(functools.partial(next_kernel, half, window, slots), out_s...  4.2 us
    pallas_call x1, Pallas kernels, multiply_first(): pl.pallas_call(functools.partial(first_kernel, window, slots), out_shape=...  3.85 us
    unnamed x8, local copies, waits for them, and re-layouts  2.62 us
  transfers between devices with their start and end apart: 16, of which 8 were waited for; matrix products, arithmetic and copies ran while one was open for 0% of the time, Pallas kernels for 2%

profile of v4, /device:TPU:24, one launch (start us, length us, event | category | flops | bytes accessed | tf_op | source)
XLA Modules:
  0.0 108.1 jit_solution(15110312270274390772)
XLA Ops:
  1.7 3.4 %collective-permute-start = (bf16[4,3,128,128]{3,2,1,0:T(8,128)(2,1)S(1)}, bf16[4,3,128,128]{3,2,1,0:T(8,128)(2,1)S(1)}, u32[]{:S(2)}, u32[]{:S(2)}) collective-permute-start(bf16[4,3,128,128]{3,2,1,0:T(8,128)(2,1)S(1)} %slice_bitcast_fusion.rest_0_), channel_id=1, source_target_pairs={{0,1},{1,0},{2,3},{3,2},{4,5},{5,4},{6,7},{7,6},{8,9},{9,8},{10,11... | collective-permute-start | bytes 1179656 | tf_op jit(solution)/shard_map/ppermute | solution.py:22
  5.1 12.7 %collective-permute-start.8 = (bf16[48,128,128]{2,1,0:T(8,128)(2,1)}, bf16[48,128,128]{2,1,0:T(8,128)(2,1)S(1)}, u32[]{:S(2)}, u32[]{:S(2)}) collective-permute-start(bf16[48,128,128]{2,1,0:T(8,128)(2,1)} %bitcast.9), channel_id=1, source_target_pairs={{8,16},{16,8},{24,32},{32,24},{40,48},{48,40},{56,64},{64,56},{72,... | collective-permute-start | bytes 4718600 | tf_op jit(solution)/shard_map/ppermute | solution.py:238
  17.8 1.9 %collective-permute-start.7 = (bf16[48,128,128]{2,1,0:T(8,128)(2,1)}, bf16[48,128,128]{2,1,0:T(8,128)(2,1)S(1)}, u32[]{:S(2)}, u32[]{:S(2)}) collective-permute-start(bf16[48,128,128]{2,1,0:T(8,128)(2,1)} %bitcast.10), channel_id=1, source_target_pairs={{0,8},{8,0},{16,24},{24,16},{32,40},{40,32},{48,56},{56,48},{64,72... | collective-permute-start | bytes 4718600 | tf_op jit(solution)/shard_map/ppermute | solution.py:238
  19.7 2.7 %collective-permute-start.2 = (bf16[4,3,128,128]{3,2,1,0:T(8,128)(2,1)S(1)}, bf16[4,3,128,128]{3,2,1,0:T(8,128)(2,1)S(1)}, u32[]{:S(2)}, u32[]{:S(2)}) collective-permute-start(bf16[4,3,128,128]{3,2,1,0:T(8,128)(2,1)S(1)} %slice_bitcast_fusion.rest_0_), channel_id=1, source_target_pairs={{0,6},{1,7},{2,0},{3,1},{4,2},{5,3},{6,4},{7,5},{8,14},{9,15},{10,... | collective-permute-start | bytes 1179656 | tf_op jit(solution)/shard_map/ppermute | solution.py:22
  22.4 4.4 %collective-permute-start.1 = (bf16[4,3,128,128]{3,2,1,0:T(8,128)(2,1)S(1)}, bf16[4,3,128,128]{3,2,1,0:T(8,128)(2,1)S(1)}, u32[]{:S(2)}, u32[]{:S(2)}) collective-permute-start(bf16[4,3,128,128]{3,2,1,0:T(8,128)(2,1)S(1)} %slice_bitcast_fusion.rest_0_), channel_id=1, source_target_pairs={{0,2},{1,3},{2,4},{3,5},{4,6},{5,7},{6,0},{7,1},{8,10},{9,11},{10,... | collective-permute-start | bytes 1179656 | tf_op jit(solution)/shard_map/ppermute | solution.py:22
  29.2 2.1 %collective-permute-start.5 = (bf16[4,3,128,128]{3,2,1,0:T(8,128)(2,1)S(1)}, bf16[4,3,128,128]{3,2,1,0:T(8,128)(2,1)S(1)}, u32[]{:S(2)}, u32[]{:S(2)}) collective-permute-start(bf16[4,3,128,128]{3,2,1,0:T(8,128)(2,1)S(1)} %collective-permute-done.rest_0_.rest_1_), channel_id=1, source_target_pairs={{0,6},{1,7},{2,0},{3,1},{4,2},{5,3},{6,4},{7,5},{8,14},{9,15},{10,... | collective-permute-start | bytes 1179656 | tf_op jit(solution)/shard_map/ppermute | solution.py:22
  31.3 3.1 %collective-permute-done.2.rest_2_.rest_3_ = bf16[4,3,128,128]{3,2,1,0:T(8,128)(2,1)S(1)} collective-permute-done((bf16[4,3,128,128]{3,2,1,0:T(8,128)(2,1)S(1)}, bf16[4,3,128,128]{3,2,1,0:T(8,128)(2,1)S(1)}, u32[]{:S(2)}, u32[]{:S(2)}) %collective-permute-start.2) | collective-permute-done | bytes 393248 | tf_op jit(solution)/shard_map/ppermute | solution.py:22
  34.4 2.1 %collective-permute-start.4 = (bf16[4,3,128,128]{3,2,1,0:T(8,128)(2,1)S(1)}, bf16[4,3,128,128]{3,2,1,0:T(8,128)(2,1)S(1)}, u32[]{:S(2)}, u32[]{:S(2)}) collective-permute-start(bf16[4,3,128,128]{3,2,1,0:T(8,128)(2,1)S(1)} %collective-permute-done.rest_0_.rest_1_), channel_id=1, source_target_pairs={{0,2},{1,3},{2,4},{3,5},{4,6},{5,7},{6,0},{7,1},{8,10},{9,11},{10,... | collective-permute-start | bytes 1179656 | tf_op jit(solution)/shard_map/ppermute | solution.py:22
  36.4 4.7 %collective-permute-start.3 = (bf16[4,3,128,128]{3,2,1,0:T(8,128)(2,1)S(1)}, bf16[4,3,128,128]{3,2,1,0:T(8,128)(2,1)S(1)}, u32[]{:S(2)}, u32[]{:S(2)}) collective-permute-start(bf16[4,3,128,128]{3,2,1,0:T(8,128)(2,1)S(1)} %collective-permute-done.1.rest_1_.rest_2_), channel_id=1, source_target_pairs={{0,2},{1,3},{2,4},{3,5},{4,6},{5,7},{6,0},{7,1},{8,10},{9,11},{10,... | collective-permute-start | bytes 1179656 | tf_op jit(solution)/shard_map/ppermute | solution.py:22
  41.1 2.3 %collective-permute-done.5.rest_5_.rest_6_ = bf16[4,3,128,128]{3,2,1,0:T(8,128)(2,1)S(1)} collective-permute-done((bf16[4,3,128,128]{3,2,1,0:T(8,128)(2,1)S(1)}, bf16[4,3,128,128]{3,2,1,0:T(8,128)(2,1)S(1)}, u32[]{:S(2)}, u32[]{:S(2)}) %collective-permute-start.5) | collective-permute-done | bytes 393248 | tf_op jit(solution)/shard_map/ppermute | solution.py:22
  43.4 1.9 %collective-permute-start.6 = (bf16[4,3,128,128]{3,2,1,0:T(8,128)(2,1)S(1)}, bf16[4,3,128,128]{3,2,1,0:T(8,128)(2,1)S(1)}, u32[]{:S(2)}, u32[]{:S(2)}) collective-permute-start(bf16[4,3,128,128]{3,2,1,0:T(8,128)(2,1)S(1)} %collective-permute-done.5.rest_5_.rest_6_), channel_id=1, source_target_pairs={{0,6},{1,7},{2,0},{3,1},{4,2},{5,3},{6,4},{7,5},{8,14},{9,15},{10,... | collective-permute-start | bytes 1179656 | tf_op jit(solution)/shard_map/ppermute | solution.py:22
  45.3 10.1 %collective-permute-done.3.rest_3_.rest_4_ = bf16[4,3,128,128]{3,2,1,0:T(8,128)(2,1)S(1)} collective-permute-done((bf16[4,3,128,128]{3,2,1,0:T(8,128)(2,1)S(1)}, bf16[4,3,128,128]{3,2,1,0:T(8,128)(2,1)S(1)}, u32[]{:S(2)}, u32[]{:S(2)}) %collective-permute-start.3) | collective-permute-done | bytes 393248 | tf_op jit(solution)/shard_map/ppermute | solution.py:22
  56.6 3.9 %square_products.1 = (bf16[4,3,128,128]{3,2,1,0:T(8,128)(2,1)}, bf16[135,128,128]{2,1,0:T(8,128)(2,1)S(1)}) custom-call(s32[24,128]{1,0:T(8,128)S(1)} %pass_table.1.table, bf16[4,3,128,128]{3,2,1,0:T(8,128)(2,1)S(1)} %slice_bitcast_fusion.rest_0_, bf16[4,3,128,128]{3,2,1,0:T(8,128)(2,1)S(1)} %collective-permute-done.rest_0_.rest_1_, ...), custom_call_target="tpu_custom_call" | custom-call | flops 600000000 | bytes 6000000 | tf_op jit(solution)/shard_map/square_products/pallas_call | solution.py:203
  60.5 2.1 %collective-permute-start.14 = (bf16[4,3,128,128]{3,2,1,0:T(8,128)(2,1)}, bf16[4,3,128,128]{3,2,1,0:T(8,128)(2,1)S(1)}, u32[]{:S(2)}, u32[]{:S(2)}) collective-permute-start(bf16[4,3,128,128]{3,2,1,0:T(8,128)(2,1)} %get-tuple-element.4.rest_0_), channel_id=1, source_target_pairs={{0,1},{1,0},{2,3},{3,2},{4,5},{5,4},{6,7},{7,6},{8,9},{9,8},{10,11... | collective-permute-start | bytes 1179656 | tf_op jit(solution)/shard_map/ppermute | solution.py:22
  62.6 1.9 %collective-permute-start.12 = (bf16[4,3,128,128]{3,2,1,0:T(8,128)(2,1)}, bf16[4,3,128,128]{3,2,1,0:T(8,128)(2,1)S(1)}, u32[]{:S(2)}, u32[]{:S(2)}) collective-permute-start(bf16[4,3,128,128]{3,2,1,0:T(8,128)(2,1)} %get-tuple-element.4.rest_0_), channel_id=1, source_target_pairs={{0,6},{1,7},{2,0},{3,1},{4,2},{5,3},{6,4},{7,5},{8,14},{9,15},{10,... | collective-permute-start | bytes 1179656 | tf_op jit(solution)/shard_map/ppermute | solution.py:22
  64.5 5.1 %collective-permute-start.10 = (bf16[4,3,128,128]{3,2,1,0:T(8,128)(2,1)}, bf16[4,3,128,128]{3,2,1,0:T(8,128)(2,1)S(1)}, u32[]{:S(2)}, u32[]{:S(2)}) collective-permute-start(bf16[4,3,128,128]{3,2,1,0:T(8,128)(2,1)} %get-tuple-element.4.rest_0_), channel_id=1, source_target_pairs={{0,2},{1,3},{2,4},{3,5},{4,6},{5,7},{6,0},{7,1},{8,10},{9,11},{10,... | collective-permute-start | bytes 1179656 | tf_op jit(solution)/shard_map/ppermute | solution.py:22
  69.7 1.9 %collective-permute-start.9 = (bf16[4,3,128,128]{3,2,1,0:T(8,128)(2,1)}, bf16[4,3,128,128]{3,2,1,0:T(8,128)(2,1)S(1)}, u32[]{:S(2)}, u32[]{:S(2)}) collective-permute-start(bf16[4,3,128,128]{3,2,1,0:T(8,128)(2,1)} %get-tuple-element.4.rest_0_), channel_id=1, source_target_pairs={{0,4},{1,5},{2,6},{3,7},{4,0},{5,1},{6,2},{7,3},{8,12},{9,13},{10,... | collective-permute-start | bytes 1179656 | tf_op jit(solution)/shard_map/ppermute | solution.py:22
  71.8 5.3 %collective-permute-start.15 = (bf16[4,3,128,128]{3,2,1,0:T(8,128)(2,1)S(1)}, bf16[4,3,128,128]{3,2,1,0:T(8,128)(2,1)S(1)}, u32[]{:S(2)}, u32[]{:S(2)}) collective-permute-start(bf16[4,3,128,128]{3,2,1,0:T(8,128)(2,1)S(1)} %collective-permute-done.14.rest_1_), channel_id=1, source_target_pairs={{0,4},{1,5},{2,6},{3,7},{4,0},{5,1},{6,2},{7,3},{8,12},{9,13},{10,... | collective-permute-start | bytes 1179656 | tf_op jit(solution)/shard_map/ppermute | solution.py:22
  77.1 14.7 %collective-permute-done.12.rest_3_ = bf16[4,3,128,128]{3,2,1,0:T(8,128)(2,1)S(1)} collective-permute-done((bf16[4,3,128,128]{3,2,1,0:T(8,128)(2,1)}, bf16[4,3,128,128]{3,2,1,0:T(8,128)(2,1)S(1)}, u32[]{:S(2)}, u32[]{:S(2)}) %collective-permute-start.12) | collective-permute-done | bytes 393248 | tf_op jit(solution)/shard_map/ppermute | solution.py:22
  91.7 3.6 %collective-permute-start.13 = (bf16[4,3,128,128]{3,2,1,0:T(8,128)(2,1)S(1)}, bf16[4,3,128,128]{3,2,1,0:T(8,128)(2,1)S(1)}, u32[]{:S(2)}, u32[]{:S(2)}) collective-permute-start(bf16[4,3,128,128]{3,2,1,0:T(8,128)(2,1)S(1)} %collective-permute-done.12.rest_3_), channel_id=1, source_target_pairs={{0,1},{1,0},{2,3},{3,2},{4,5},{5,4},{6,7},{7,6},{8,9},{9,8},{10,11... | collective-permute-start | bytes 1179656 | tf_op jit(solution)/shard_map/ppermute | solution.py:22
  95.4 2.2 %collective-permute-start.11 = (bf16[4,3,128,128]{3,2,1,0:T(8,128)(2,1)S(1)}, bf16[4,3,128,128]{3,2,1,0:T(8,128)(2,1)S(1)}, u32[]{:S(2)}, u32[]{:S(2)}) collective-permute-start(bf16[4,3,128,128]{3,2,1,0:T(8,128)(2,1)S(1)} %collective-permute-done.10.rest_2_), channel_id=1, source_target_pairs={{0,1},{1,0},{2,3},{3,2},{4,5},{5,4},{6,7},{7,6},{8,9},{9,8},{10,11... | collective-permute-start | bytes 1179656 | tf_op jit(solution)/shard_map/ppermute | solution.py:22
  98.6 1.7 %cube_products.2.rest_5_ = f32[4,3,128,128]{3,2,1,0:T(8,128)S(1)} custom-call(s32[24,128]{1,0:T(8,128)S(1)} %pass_table.1.table, bf16[4,3,128,128]{3,2,1,0:T(8,128)(2,1)S(1)} %copy-done.1, bf16[4,3,128,128]{3,2,1,0:T(8,128)(2,1)S(1)} %collective-permute-done.14.rest_1_, bf16[4,3,128,128]{3,2,1,0:T(8,128)(2,1)S(1)} %collective-permute-done.10.rest_2_, ...), custom_call_target="tpu_custom_call" | custom-call | flops 600000000 | bytes 6000000 | tf_op jit(solution)/shard_map/cube_products/pallas_call | solution.py:221
  101.4 4.2 %collective-permute-done.11.rest_1_ = bf16[4,3,128,128]{3,2,1,0:T(8,128)(2,1)S(1)} collective-permute-done((bf16[4,3,128,128]{3,2,1,0:T(8,128)(2,1)S(1)}, bf16[4,3,128,128]{3,2,1,0:T(8,128)(2,1)S(1)}, u32[]{:S(2)}, u32[]{:S(2)}) %collective-permute-start.11) | collective-permute-done | bytes 393248 | tf_op jit(solution)/shard_map/ppermute | solution.py:22
  105.6 2.5 %cube_products.3 = bf16[4,3,128,128]{3,2,1,0:T(8,128)(2,1)} custom-call(s32[24,128]{1,0:T(8,128)S(1)} %pass_table.1.table, bf16[4,3,128,128]{3,2,1,0:T(8,128)(2,1)S(1)} %collective-permute-done.9.rest_0_, bf16[4,3,128,128]{3,2,1,0:T(8,128)(2,1)S(1)} %collective-permute-done.11.rest_1_, bf16[4,3,128,128]{3,2,1,0:T(8,128)(2,1)S(1)} %collective-permute-done.13.rest_2_, ...), custom_call_target="tpu_custom_call" | custom-call | flops 600000000 | bytes 6000000 | tf_op jit(solution)/shard_map/cube_products/pallas_call | solution.py:221
  (22 shorter events, 6.8 us)
Async XLA Ops:
  1.7 27.5 %collective-permute-start = (bf16[4,3,128,128]{3,2,1,0:T(8,128)(2,1)S(1)}, bf16[4,3,128,128]{3,2,1,0:T(8,128)(2,1)S(1)}, u32[]{:S(2)}, u32[]{:S(2)}) collective-permute-start(bf16[4,3,128,128]{3,2,1,0:T(8,128)(2,1)S(1)} %slice_bitcast_fusion.rest_0_), channel_id=1, source_target_pairs={{0,1},{1,0},{2,3},{3,2},{4,5},{5,4},{6,7},{7,6},{8,9},{9,8},{10,11... | collective-permute-start | bytes 1179656 | tf_op jit(solution)/shard_map/ppermute | solution.py:22
  5.1 51.5 %collective-permute-start.8 = (bf16[48,128,128]{2,1,0:T(8,128)(2,1)}, bf16[48,128,128]{2,1,0:T(8,128)(2,1)S(1)}, u32[]{:S(2)}, u32[]{:S(2)}) collective-permute-start(bf16[48,128,128]{2,1,0:T(8,128)(2,1)} %bitcast.9), channel_id=1, source_target_pairs={{8,16},{16,8},{24,32},{32,24},{40,48},{48,40},{56,64},{64,56},{72,... | collective-permute-start | bytes 4718600 | tf_op jit(solution)/shard_map/ppermute | solution.py:238
  17.8 38.8 %collective-permute-start.7 = (bf16[48,128,128]{2,1,0:T(8,128)(2,1)}, bf16[48,128,128]{2,1,0:T(8,128)(2,1)S(1)}, u32[]{:S(2)}, u32[]{:S(2)}) collective-permute-start(bf16[48,128,128]{2,1,0:T(8,128)(2,1)} %bitcast.10), channel_id=1, source_target_pairs={{0,8},{8,0},{16,24},{24,16},{32,40},{40,32},{48,56},{56,48},{64,72... | collective-permute-start | bytes 4718600 | tf_op jit(solution)/shard_map/ppermute | solution.py:238
  19.7 14.6 %collective-permute-start.2 = (bf16[4,3,128,128]{3,2,1,0:T(8,128)(2,1)S(1)}, bf16[4,3,128,128]{3,2,1,0:T(8,128)(2,1)S(1)}, u32[]{:S(2)}, u32[]{:S(2)}) collective-permute-start(bf16[4,3,128,128]{3,2,1,0:T(8,128)(2,1)S(1)} %slice_bitcast_fusion.rest_0_), channel_id=1, source_target_pairs={{0,6},{1,7},{2,0},{3,1},{4,2},{5,3},{6,4},{7,5},{8,14},{9,15},{10,... | collective-permute-start | bytes 1179656 | tf_op jit(solution)/shard_map/ppermute | solution.py:22
  22.4 14.0 %collective-permute-start.1 = (bf16[4,3,128,128]{3,2,1,0:T(8,128)(2,1)S(1)}, bf16[4,3,128,128]{3,2,1,0:T(8,128)(2,1)S(1)}, u32[]{:S(2)}, u32[]{:S(2)}) collective-permute-start(bf16[4,3,128,128]{3,2,1,0:T(8,128)(2,1)S(1)} %slice_bitcast_fusion.rest_0_), channel_id=1, source_target_pairs={{0,2},{1,3},{2,4},{3,5},{4,6},{5,7},{6,0},{7,1},{8,10},{9,11},{10,... | collective-permute-start | bytes 1179656 | tf_op jit(solution)/shard_map/ppermute | solution.py:22
  26.8 0.9 copy-start.2
  27.7 0.7 copy-start.3
  29.2 27.4 %copy-start = (bf16[16,3,128,128]{3,2,1,0:T(8,128)(2,1)S(1)}, bf16[16,3,128,128]{3,2,1,0:T(8,128)(2,1)}, u32[]{:S(2)}) copy-start(bf16[16,3,128,128]{3,2,1,0:T(8,128)(2,1)} %param.3) | copy-start | bytes 4718596
  29.2 14.2 %collective-permute-start.5 = (bf16[4,3,128,128]{3,2,1,0:T(8,128)(2,1)S(1)}, bf16[4,3,128,128]{3,2,1,0:T(8,128)(2,1)S(1)}, u32[]{:S(2)}, u32[]{:S(2)}) collective-permute-start(bf16[4,3,128,128]{3,2,1,0:T(8,128)(2,1)S(1)} %collective-permute-done.rest_0_.rest_1_), channel_id=1, source_target_pairs={{0,6},{1,7},{2,0},{3,1},{4,2},{5,3},{6,4},{7,5},{8,14},{9,15},{10,... | collective-permute-start | bytes 1179656 | tf_op jit(solution)/shard_map/ppermute | solution.py:22
  34.4 21.0 %collective-permute-start.4 = (bf16[4,3,128,128]{3,2,1,0:T(8,128)(2,1)S(1)}, bf16[4,3,128,128]{3,2,1,0:T(8,128)(2,1)S(1)}, u32[]{:S(2)}, u32[]{:S(2)}) collective-permute-start(bf16[4,3,128,128]{3,2,1,0:T(8,128)(2,1)S(1)} %collective-permute-done.rest_0_.rest_1_), channel_id=1, source_target_pairs={{0,2},{1,3},{2,4},{3,5},{4,6},{5,7},{6,0},{7,1},{8,10},{9,11},{10,... | collective-permute-start | bytes 1179656 | tf_op jit(solution)/shard_map/ppermute | solution.py:22
  36.4 19.0 %collective-permute-start.3 = (bf16[4,3,128,128]{3,2,1,0:T(8,128)(2,1)S(1)}, bf16[4,3,128,128]{3,2,1,0:T(8,128)(2,1)S(1)}, u32[]{:S(2)}, u32[]{:S(2)}) collective-permute-start(bf16[4,3,128,128]{3,2,1,0:T(8,128)(2,1)S(1)} %collective-permute-done.1.rest_1_.rest_2_), channel_id=1, source_target_pairs={{0,2},{1,3},{2,4},{3,5},{4,6},{5,7},{6,0},{7,1},{8,10},{9,11},{10,... | collective-permute-start | bytes 1179656 | tf_op jit(solution)/shard_map/ppermute | solution.py:22
  43.4 13.2 %collective-permute-start.6 = (bf16[4,3,128,128]{3,2,1,0:T(8,128)(2,1)S(1)}, bf16[4,3,128,128]{3,2,1,0:T(8,128)(2,1)S(1)}, u32[]{:S(2)}, u32[]{:S(2)}) collective-permute-start(bf16[4,3,128,128]{3,2,1,0:T(8,128)(2,1)S(1)} %collective-permute-done.5.rest_5_.rest_6_), channel_id=1, source_target_pairs={{0,6},{1,7},{2,0},{3,1},{4,2},{5,3},{6,4},{7,5},{8,14},{9,15},{10,... | collective-permute-start | bytes 1179656 | tf_op jit(solution)/shard_map/ppermute | solution.py:22
  60.5 11.3 %collective-permute-start.14 = (bf16[4,3,128,128]{3,2,1,0:T(8,128)(2,1)}, bf16[4,3,128,128]{3,2,1,0:T(8,128)(2,1)S(1)}, u32[]{:S(2)}, u32[]{:S(2)}) collective-permute-start(bf16[4,3,128,128]{3,2,1,0:T(8,128)(2,1)} %get-tuple-element.4.rest_0_), channel_id=1, source_target_pairs={{0,1},{1,0},{2,3},{3,2},{4,5},{5,4},{6,7},{7,6},{8,9},{9,8},{10,11... | collective-permute-start | bytes 1179656 | tf_op jit(solution)/shard_map/ppermute | solution.py:22
  62.6 29.1 %collective-permute-start.12 = (bf16[4,3,128,128]{3,2,1,0:T(8,128)(2,1)}, bf16[4,3,128,128]{3,2,1,0:T(8,128)(2,1)S(1)}, u32[]{:S(2)}, u32[]{:S(2)}) collective-permute-start(bf16[4,3,128,128]{3,2,1,0:T(8,128)(2,1)} %get-tuple-element.4.rest_0_), channel_id=1, source_target_pairs={{0,6},{1,7},{2,0},{3,1},{4,2},{5,3},{6,4},{7,5},{8,14},{9,15},{10,... | collective-permute-start | bytes 1179656 | tf_op jit(solution)/shard_map/ppermute | solution.py:22
  64.5 30.8 %collective-permute-start.10 = (bf16[4,3,128,128]{3,2,1,0:T(8,128)(2,1)}, bf16[4,3,128,128]{3,2,1,0:T(8,128)(2,1)S(1)}, u32[]{:S(2)}, u32[]{:S(2)}) collective-permute-start(bf16[4,3,128,128]{3,2,1,0:T(8,128)(2,1)} %get-tuple-element.4.rest_0_), channel_id=1, source_target_pairs={{0,2},{1,3},{2,4},{3,5},{4,6},{5,7},{6,0},{7,1},{8,10},{9,11},{10,... | collective-permute-start | bytes 1179656 | tf_op jit(solution)/shard_map/ppermute | solution.py:22
  69.7 30.7 %collective-permute-start.9 = (bf16[4,3,128,128]{3,2,1,0:T(8,128)(2,1)}, bf16[4,3,128,128]{3,2,1,0:T(8,128)(2,1)S(1)}, u32[]{:S(2)}, u32[]{:S(2)}) collective-permute-start(bf16[4,3,128,128]{3,2,1,0:T(8,128)(2,1)} %get-tuple-element.4.rest_0_), channel_id=1, source_target_pairs={{0,4},{1,5},{2,6},{3,7},{4,0},{5,1},{6,2},{7,3},{8,12},{9,13},{10,... | collective-permute-start | bytes 1179656 | tf_op jit(solution)/shard_map/ppermute | solution.py:22
  71.8 28.6 %collective-permute-start.15 = (bf16[4,3,128,128]{3,2,1,0:T(8,128)(2,1)S(1)}, bf16[4,3,128,128]{3,2,1,0:T(8,128)(2,1)S(1)}, u32[]{:S(2)}, u32[]{:S(2)}) collective-permute-start(bf16[4,3,128,128]{3,2,1,0:T(8,128)(2,1)S(1)} %collective-permute-done.14.rest_1_), channel_id=1, source_target_pairs={{0,4},{1,5},{2,6},{3,7},{4,0},{5,1},{6,2},{7,3},{8,12},{9,13},{10,... | collective-permute-start | bytes 1179656 | tf_op jit(solution)/shard_map/ppermute | solution.py:22
  91.7 9.7 %collective-permute-start.13 = (bf16[4,3,128,128]{3,2,1,0:T(8,128)(2,1)S(1)}, bf16[4,3,128,128]{3,2,1,0:T(8,128)(2,1)S(1)}, u32[]{:S(2)}, u32[]{:S(2)}) collective-permute-start(bf16[4,3,128,128]{3,2,1,0:T(8,128)(2,1)S(1)} %collective-permute-done.12.rest_3_), channel_id=1, source_target_pairs={{0,1},{1,0},{2,3},{3,2},{4,5},{5,4},{6,7},{7,6},{8,9},{9,8},{10,11... | collective-permute-start | bytes 1179656 | tf_op jit(solution)/shard_map/ppermute | solution.py:22
  95.4 10.2 %collective-permute-start.11 = (bf16[4,3,128,128]{3,2,1,0:T(8,128)(2,1)S(1)}, bf16[4,3,128,128]{3,2,1,0:T(8,128)(2,1)S(1)}, u32[]{:S(2)}, u32[]{:S(2)}) collective-permute-start(bf16[4,3,128,128]{3,2,1,0:T(8,128)(2,1)S(1)} %collective-permute-done.10.rest_2_), channel_id=1, source_target_pairs={{0,1},{1,0},{2,3},{3,2},{4,5},{5,4},{6,7},{7,6},{8,9},{9,8},{10,11... | collective-permute-start | bytes 1179656 | tf_op jit(solution)/shard_map/ppermute | solution.py:22
  97.6 1.0 copy-start.1

commit v5 on v4

--- a/solution.py
+++ b/solution.py
@@ -9,9 +9,8 @@
 
 Y = 4
 LANES = 128
-ORDER_FLOPS = 7_000_000_000
+ORDER_FLOPS = 6_000_000_000
 SOURCES = ((0, 0), (0, 1), (-1, 0), (1, 0), (2, 0), (-1, 1), (1, 1), (2, 1))
-HALF = len(SOURCES) // 2
 
 
 def moved(a, dy, dx):
@@ -22,27 +21,16 @@
     return lax.ppermute(a, "narrow", pairs)
 
 
-def gather_rows_by_y(own, table):
+def gather_rows(own, *beside):
     partner = moved(own, 0, 1)
+    upper = moved(own, -1, 0)
     lower = moved(own, 1, 0)
-    upper = moved(own, -1, 0)
-    partner, table = lax.optimization_barrier((partner, table))
+    partner, upper, lower, *beside = lax.optimization_barrier((partner, upper, lower, *beside))
     partner_upper = moved(partner, -1, 0)
     partner_lower = moved(partner, 1, 0)
     far = moved(lower, 1, 0)
     partner_far = moved(partner_upper, -1, 0)
-    return (own, partner, lower, upper), (far, partner_lower, partner_upper, partner_far), table
-
-
-def gather_rows(own):
-    partner = moved(own, 0, 1)
-    lower = moved(own, 1, 0)
-    upper = moved(own, -1, 0)
-    far = moved(own, 2, 0)
-    partner_lower = moved(lower, 0, 1)
-    partner_upper = moved(upper, 0, 1)
-    partner_far = moved(partner, 2, 0)
-    return (own, partner, lower, upper), (far, partner_lower, partner_upper, partner_far)
+    return (own, partner, lower, upper, far, partner_lower, partner_upper, partner_far), *beside
 
 
 def table_kernel(rows_dev, slots, window, block_ref, product_ref, table_ref):
@@ -142,7 +130,7 @@
     for g in range(window):
         total = [None if start is None else start[g, q] for q in range(slots)]
         for e in range(0, capacity, pair):
-            near = range(e, e + pair)
+            near = range(e, min(e + pair, capacity))
             left = jnp.concatenate([lefts[i // slots][g, i % slots] for i in near], axis=1)
             right = jnp.concatenate(
                 [
@@ -162,7 +150,7 @@
 
 
 def first_kernel(window, slots, table, *rest):
-    lefts, (chip, own, next_chip, out_ref, ext, sem) = rest[: 2 * HALF], rest[2 * HALF :]
+    lefts, (chip, own, next_chip, out_ref, ext, sem) = rest[:-6], rest[-6:]
     rows = own.shape[0]
     tail = ext.shape[0] - slots - 2 * rows
     even = lax.rem(lax.axis_index("wide"), 2) == 0
@@ -186,13 +174,12 @@
     add_products(0, SOURCES, window, slots, table, lefts, ext, None, out_ref)
 
 
-def next_kernel(half, window, slots, table, *rest):
-    lefts, rest = rest[:HALF], rest[HALF:]
+def next_kernel(sources, window, slots, table, *rest):
+    lefts, rest = rest[: len(sources)], rest[len(sources) :]
     if len(rest) == 3:
         ext, start, out_ref = rest
     else:
         (ext, out_ref), start = rest, None
-    sources = SOURCES[half * HALF : (half + 1) * HALF]
     add_products(1, sources, window, slots, table, lefts, ext, start, out_ref)
 
 
@@ -206,7 +193,7 @@
             jax.ShapeDtypeStruct((window, slots) + block, jnp.bfloat16),
             jax.ShapeDtypeStruct((ext_blocks,) + block, jnp.bfloat16),
         ),
-        in_specs=[SCALAR] + [LOCAL] * (2 * HALF + 3),
+        in_specs=[SCALAR] + [LOCAL] * (len(lefts) + 3),
         out_specs=(LOCAL, LOCAL),
         scratch_shapes=[pltpu.SemaphoreType.DMA((3,))],
         compiler_params=PARAMS,
@@ -215,13 +202,13 @@
     )(table, *lefts, *rights)
 
 
-def multiply(half, table, lefts, ext, start, window, slots, out_type):
+def multiply(sources, table, lefts, ext, start, window, slots, out_type):
     block = lefts[0].shape[2:]
     extra = () if start is None else (start,)
     return pl.pallas_call(
-        functools.partial(next_kernel, half, window, slots),
+        functools.partial(next_kernel, sources, window, slots),
         out_shape=jax.ShapeDtypeStruct((window, slots) + block, out_type),
-        in_specs=[SCALAR] + [LOCAL] * (HALF + 1 + len(extra)),
+        in_specs=[SCALAR] + [LOCAL] * (len(lefts) + 1 + len(extra)),
         out_specs=LOCAL,
         compiler_params=PARAMS,
         name="cube_products",
@@ -246,13 +233,13 @@
     next_chip = swapped(blocks, "wide", 1)
     local = density.reshape((window, step) + density.shape[1:])[:, 0]
     table = build_table(block_list, product_list, rows_dev, slots, window)
-    early, late, table = gather_rows_by_y(local, table)
-    table = passed(table, early[1:] + late)
+    lefts, table = gather_rows(local, table)
+    table = passed(table, lefts[1:])
     chip = swapped(blocks, "wide", 0)
-    square, ext = multiply_first(table, early + late, (chip, blocks, next_chip), window, slots)
-    early, late = gather_rows(square)
-    part = multiply(0, table, early, ext, None, window, slots, jnp.float32)
-    cube = multiply(1, table, late, ext, part, window, slots, jnp.bfloat16)
+    square, ext = multiply_first(table, lefts, (chip, blocks, next_chip), window, slots)
+    (lefts,) = gather_rows(square)
+    part = multiply(SOURCES[:-1], table, lefts[:-1], ext, None, window, slots, jnp.float32)
+    cube = multiply(SOURCES[-1:], table, lefts[-1:], ext, part, window, slots, jnp.bfloat16)
     return square, cube
 
 

time: 109 us -> 112 us (1.028)
  starting transfers between devices: 58 us -> 65 us
  waiting for transfers between devices: 36.7 us -> 32.8 us
    ppermute x14, starting transfers between devices: 43.4 us -> 53 us  [moved(): return lax.ppermute(a, 'narrow', pairs)]
    ppermute x14, waiting for transfers between devices: 36.7 us -> 32.8 us  [moved(): return lax.ppermute(a, 'narrow', pairs)]
    ppermute x2, starting transfers between devices: 14.7 us -> 12 us  [swapped(): return lax.ppermute(x, axis, pairs)]
  transfers between devices with their start and end apart: 16 -> 16, of which waited for: 8 -> 7; matrix products, arithmetic and copies ran while one was open for 0% -> 0% of each run, Pallas kernels for 2% -> 3%
where the time goes in v5:
time: 112 us; the launch traced here: 111 us
  starting transfers between devices  65 us (58%)
  waiting for transfers between devices  32.8 us (29%)
  Pallas kernels  8.91 us (8%)
  local copies, waits for them, and re-layouts  3.65 us (3%)
    ppermute x14, starting transfers between devices, moved(): return lax.ppermute(a, 'narrow', pairs)  53 us
    ppermute x14, waiting for transfers between devices, moved(): return lax.ppermute(a, 'narrow', pairs)  32.8 us
    ppermute x2, starting transfers between devices, swapped(): return lax.ppermute(x, axis, pairs)  12 us
    pallas_call x2, Pallas kernels, multiply(): pl.pallas_call(functools.partial(next_kernel, sources, window, slots), ou...  4.32 us
    pallas_call x1, Pallas kernels, multiply_first(): pl.pallas_call(functools.partial(first_kernel, window, slots), out_shape=...  3.84 us
    unnamed x8, local copies, waits for them, and re-layouts  2.63 us
  transfers between devices with their start and end apart: 16, of which 7 were waited for; matrix products, arithmetic and copies ran while one was open for 0% of the time, Pallas kernels for 3%

profile of v5, /device:TPU:24, one launch (start us, length us, event | category | flops | bytes accessed | tf_op | source)
XLA Modules:
  0.0 111.2 jit_solution(13796915219749457723)
XLA Ops:
  1.7 7.5 %collective-permute-start.2 = (bf16[4,3,128,128]{3,2,1,0:T(8,128)(2,1)S(1)}, bf16[4,3,128,128]{3,2,1,0:T(8,128)(2,1)S(1)}, u32[]{:S(2)}, u32[]{:S(2)}) collective-permute-start(bf16[4,3,128,128]{3,2,1,0:T(8,128)(2,1)S(1)} %slice_bitcast_fusion.rest_0_), channel_id=1, source_target_pairs={{0,2},{1,3},{2,4},{3,5},{4,6},{5,7},{6,0},{7,1},{8,10},{9,11},{10,... | collective-permute-start | bytes 1179656 | tf_op jit(solution)/shard_map/ppermute | solution.py:21
  9.2 1.9 %collective-permute-start.1 = (bf16[4,3,128,128]{3,2,1,0:T(8,128)(2,1)S(1)}, bf16[4,3,128,128]{3,2,1,0:T(8,128)(2,1)S(1)}, u32[]{:S(2)}, u32[]{:S(2)}) collective-permute-start(bf16[4,3,128,128]{3,2,1,0:T(8,128)(2,1)S(1)} %slice_bitcast_fusion.rest_0_), channel_id=1, source_target_pairs={{0,6},{1,7},{2,0},{3,1},{4,2},{5,3},{6,4},{7,5},{8,14},{9,15},{10,... | collective-permute-start | bytes 1179656 | tf_op jit(solution)/shard_map/ppermute | solution.py:21
  11.1 1.9 %collective-permute-start = (bf16[4,3,128,128]{3,2,1,0:T(8,128)(2,1)S(1)}, bf16[4,3,128,128]{3,2,1,0:T(8,128)(2,1)S(1)}, u32[]{:S(2)}, u32[]{:S(2)}) collective-permute-start(bf16[4,3,128,128]{3,2,1,0:T(8,128)(2,1)S(1)} %slice_bitcast_fusion.rest_0_), channel_id=1, source_target_pairs={{0,1},{1,0},{2,3},{3,2},{4,5},{5,4},{6,7},{7,6},{8,9},{9,8},{10,11... | collective-permute-start | bytes 1179656 | tf_op jit(solution)/shard_map/ppermute | solution.py:21
  13.0 10.1 %collective-permute-start.8 = (bf16[48,128,128]{2,1,0:T(8,128)(2,1)}, bf16[48,128,128]{2,1,0:T(8,128)(2,1)S(1)}, u32[]{:S(2)}, u32[]{:S(2)}) collective-permute-start(bf16[48,128,128]{2,1,0:T(8,128)(2,1)} %bitcast.9), channel_id=1, source_target_pairs={{8,16},{16,8},{24,32},{32,24},{40,48},{48,40},{56,64},{64,56},{72,... | collective-permute-start | bytes 4718600 | tf_op jit(solution)/shard_map/ppermute | solution.py:225
  23.1 1.9 %collective-permute-start.7 = (bf16[48,128,128]{2,1,0:T(8,128)(2,1)}, bf16[48,128,128]{2,1,0:T(8,128)(2,1)S(1)}, u32[]{:S(2)}, u32[]{:S(2)}) collective-permute-start(bf16[48,128,128]{2,1,0:T(8,128)(2,1)} %bitcast.10), channel_id=1, source_target_pairs={{0,8},{8,0},{16,24},{24,16},{32,40},{40,32},{48,56},{56,48},{64,72... | collective-permute-start | bytes 4718600 | tf_op jit(solution)/shard_map/ppermute | solution.py:225
  27.5 2.8 %collective-permute-start.5 = (bf16[4,3,128,128]{3,2,1,0:T(8,128)(2,1)S(1)}, bf16[4,3,128,128]{3,2,1,0:T(8,128)(2,1)S(1)}, u32[]{:S(2)}, u32[]{:S(2)}) collective-permute-start(bf16[4,3,128,128]{3,2,1,0:T(8,128)(2,1)S(1)} %collective-permute-done.rest_0_.rest_1_), channel_id=1, source_target_pairs={{0,6},{1,7},{2,0},{3,1},{4,2},{5,3},{6,4},{7,5},{8,14},{9,15},{10,... | collective-permute-start | bytes 1179656 | tf_op jit(solution)/shard_map/ppermute | solution.py:21
  30.2 14.4 %collective-permute-start.4 = (bf16[4,3,128,128]{3,2,1,0:T(8,128)(2,1)S(1)}, bf16[4,3,128,128]{3,2,1,0:T(8,128)(2,1)S(1)}, u32[]{:S(2)}, u32[]{:S(2)}) collective-permute-start(bf16[4,3,128,128]{3,2,1,0:T(8,128)(2,1)S(1)} %collective-permute-done.rest_0_.rest_1_), channel_id=1, source_target_pairs={{0,2},{1,3},{2,4},{3,5},{4,6},{5,7},{6,0},{7,1},{8,10},{9,11},{10,... | collective-permute-start | bytes 1179656 | tf_op jit(solution)/shard_map/ppermute | solution.py:21
  44.7 3.9 %collective-permute-start.3 = (bf16[4,3,128,128]{3,2,1,0:T(8,128)(2,1)S(1)}, bf16[4,3,128,128]{3,2,1,0:T(8,128)(2,1)S(1)}, u32[]{:S(2)}, u32[]{:S(2)}) collective-permute-start(bf16[4,3,128,128]{3,2,1,0:T(8,128)(2,1)S(1)} %collective-permute-done.2.rest_1_.rest_2_), channel_id=1, source_target_pairs={{0,2},{1,3},{2,4},{3,5},{4,6},{5,7},{6,0},{7,1},{8,10},{9,11},{10,... | collective-permute-start | bytes 1179656 | tf_op jit(solution)/shard_map/ppermute | solution.py:21
  48.6 3.8 %collective-permute-done.5.rest_5_.rest_6_ = bf16[4,3,128,128]{3,2,1,0:T(8,128)(2,1)S(1)} collective-permute-done((bf16[4,3,128,128]{3,2,1,0:T(8,128)(2,1)S(1)}, bf16[4,3,128,128]{3,2,1,0:T(8,128)(2,1)S(1)}, u32[]{:S(2)}, u32[]{:S(2)}) %collective-permute-start.5) | collective-permute-done | bytes 393248 | tf_op jit(solution)/shard_map/ppermute | solution.py:21
  52.4 1.9 %collective-permute-start.6 = (bf16[4,3,128,128]{3,2,1,0:T(8,128)(2,1)S(1)}, bf16[4,3,128,128]{3,2,1,0:T(8,128)(2,1)S(1)}, u32[]{:S(2)}, u32[]{:S(2)}) collective-permute-start(bf16[4,3,128,128]{3,2,1,0:T(8,128)(2,1)S(1)} %collective-permute-done.5.rest_5_.rest_6_), channel_id=1, source_target_pairs={{0,6},{1,7},{2,0},{3,1},{4,2},{5,3},{6,4},{7,5},{8,14},{9,15},{10,... | collective-permute-start | bytes 1179656 | tf_op jit(solution)/shard_map/ppermute | solution.py:21
  54.4 8.9 %collective-permute-done.6.rest_6_.rest_7_ = bf16[4,3,128,128]{3,2,1,0:T(8,128)(2,1)S(1)} collective-permute-done((bf16[4,3,128,128]{3,2,1,0:T(8,128)(2,1)S(1)}, bf16[4,3,128,128]{3,2,1,0:T(8,128)(2,1)S(1)}, u32[]{:S(2)}, u32[]{:S(2)}) %collective-permute-start.6) | collective-permute-done | bytes 393248 | tf_op jit(solution)/shard_map/ppermute | solution.py:21
  63.3 3.8 %square_products.1 = (bf16[4,3,128,128]{3,2,1,0:T(8,128)(2,1)}, bf16[135,128,128]{2,1,0:T(8,128)(2,1)S(1)}) custom-call(s32[24,128]{1,0:T(8,128)S(1)} %pass_table.1.table, bf16[4,3,128,128]{3,2,1,0:T(8,128)(2,1)S(1)} %slice_bitcast_fusion.rest_0_, bf16[4,3,128,128]{3,2,1,0:T(8,128)(2,1)S(1)} %collective-permute-done.rest_0_.rest_1_, ...), custom_call_target="tpu_custom_call" | custom-call | flops 600000000 | bytes 6000000 | tf_op jit(solution)/shard_map/square_products/pallas_call | solution.py:190
  67.1 2.0 %collective-permute-start.11 = (bf16[4,3,128,128]{3,2,1,0:T(8,128)(2,1)}, bf16[4,3,128,128]{3,2,1,0:T(8,128)(2,1)S(1)}, u32[]{:S(2)}, u32[]{:S(2)}) collective-permute-start(bf16[4,3,128,128]{3,2,1,0:T(8,128)(2,1)} %get-tuple-element.9.rest_0_), channel_id=1, source_target_pairs={{0,2},{1,3},{2,4},{3,5},{4,6},{5,7},{6,0},{7,1},{8,10},{9,11},{10,... | collective-permute-start | bytes 1179656 | tf_op jit(solution)/shard_map/ppermute | solution.py:21
  69.2 3.8 %collective-permute-start.10 = (bf16[4,3,128,128]{3,2,1,0:T(8,128)(2,1)}, bf16[4,3,128,128]{3,2,1,0:T(8,128)(2,1)S(1)}, u32[]{:S(2)}, u32[]{:S(2)}) collective-permute-start(bf16[4,3,128,128]{3,2,1,0:T(8,128)(2,1)} %get-tuple-element.9.rest_0_), channel_id=1, source_target_pairs={{0,6},{1,7},{2,0},{3,1},{4,2},{5,3},{6,4},{7,5},{8,14},{9,15},{10,... | collective-permute-start | bytes 1179656 | tf_op jit(solution)/shard_map/ppermute | solution.py:21
  73.0 1.9 %collective-permute-start.9 = (bf16[4,3,128,128]{3,2,1,0:T(8,128)(2,1)}, bf16[4,3,128,128]{3,2,1,0:T(8,128)(2,1)S(1)}, u32[]{:S(2)}, u32[]{:S(2)}) collective-permute-start(bf16[4,3,128,128]{3,2,1,0:T(8,128)(2,1)} %get-tuple-element.9.rest_0_), channel_id=1, source_target_pairs={{0,1},{1,0},{2,3},{3,2},{4,5},{5,4},{6,7},{7,6},{8,9},{9,8},{10,11... | collective-permute-start | bytes 1179656 | tf_op jit(solution)/shard_map/ppermute | solution.py:21
  74.9 2.1 %collective-permute-done.11.rest_2_ = bf16[4,3,128,128]{3,2,1,0:T(8,128)(2,1)S(1)} collective-permute-done((bf16[4,3,128,128]{3,2,1,0:T(8,128)(2,1)}, bf16[4,3,128,128]{3,2,1,0:T(8,128)(2,1)S(1)}, u32[]{:S(2)}, u32[]{:S(2)}) %collective-permute-start.11) | collective-permute-done | bytes 393248 | tf_op jit(solution)/shard_map/ppermute | solution.py:21
  77.0 6.5 %collective-permute-done.10.rest_3_ = bf16[4,3,128,128]{3,2,1,0:T(8,128)(2,1)S(1)} collective-permute-done((bf16[4,3,128,128]{3,2,1,0:T(8,128)(2,1)}, bf16[4,3,128,128]{3,2,1,0:T(8,128)(2,1)S(1)}, u32[]{:S(2)}, u32[]{:S(2)}) %collective-permute-start.10) | collective-permute-done | bytes 393248 | tf_op jit(solution)/shard_map/ppermute | solution.py:21
  83.6 3.1 %collective-permute-start.12 = (bf16[4,3,128,128]{3,2,1,0:T(8,128)(2,1)S(1)}, bf16[4,3,128,128]{3,2,1,0:T(8,128)(2,1)S(1)}, u32[]{:S(2)}, u32[]{:S(2)}) collective-permute-start(bf16[4,3,128,128]{3,2,1,0:T(8,128)(2,1)S(1)} %collective-permute-done.9.rest_1_), channel_id=1, source_target_pairs={{0,6},{1,7},{2,0},{3,1},{4,2},{5,3},{6,4},{7,5},{8,14},{9,15},{10,... | collective-permute-start | bytes 1179656 | tf_op jit(solution)/shard_map/ppermute | solution.py:21
  86.7 4.0 %collective-permute-start.14 = (bf16[4,3,128,128]{3,2,1,0:T(8,128)(2,1)S(1)}, bf16[4,3,128,128]{3,2,1,0:T(8,128)(2,1)S(1)}, u32[]{:S(2)}, u32[]{:S(2)}) collective-permute-start(bf16[4,3,128,128]{3,2,1,0:T(8,128)(2,1)S(1)} %collective-permute-done.11.rest_2_), channel_id=1, source_target_pairs={{0,2},{1,3},{2,4},{3,5},{4,6},{5,7},{6,0},{7,1},{8,10},{9,11},{10,... | collective-permute-start | bytes 1179656 | tf_op jit(solution)/shard_map/ppermute | solution.py:21
  90.6 1.9 %collective-permute-start.15 = (bf16[4,3,128,128]{3,2,1,0:T(8,128)(2,1)S(1)}, bf16[4,3,128,128]{3,2,1,0:T(8,128)(2,1)S(1)}, u32[]{:S(2)}, u32[]{:S(2)}) collective-permute-start(bf16[4,3,128,128]{3,2,1,0:T(8,128)(2,1)S(1)} %collective-permute-done.9.rest_1_), channel_id=1, source_target_pairs={{0,2},{1,3},{2,4},{3,5},{4,6},{5,7},{6,0},{7,1},{8,10},{9,11},{10,... | collective-permute-start | bytes 1179656 | tf_op jit(solution)/shard_map/ppermute | solution.py:21
  92.6 5.8 %collective-permute-done.12.rest_6_ = bf16[4,3,128,128]{3,2,1,0:T(8,128)(2,1)S(1)} collective-permute-done((bf16[4,3,128,128]{3,2,1,0:T(8,128)(2,1)S(1)}, bf16[4,3,128,128]{3,2,1,0:T(8,128)(2,1)S(1)}, u32[]{:S(2)}, u32[]{:S(2)}) %collective-permute-start.12) | collective-permute-done | bytes 393248 | tf_op jit(solution)/shard_map/ppermute | solution.py:21
  101.5 2.4 %cube_products.2.rest_2_ = f32[4,3,128,128]{3,2,1,0:T(8,128)S(1)} custom-call(s32[24,128]{1,0:T(8,128)S(1)} %pass_table.1.table, bf16[4,3,128,128]{3,2,1,0:T(8,128)(2,1)S(1)} %copy-done.1, bf16[4,3,128,128]{3,2,1,0:T(8,128)(2,1)S(1)} %collective-permute-done.9.rest_1_, bf16[4,3,128,128]{3,2,1,0:T(8,128)(2,1)S(1)} %collective-permute-done.11.rest_2_, ...), custom_call_target="tpu_custom_call" | custom-call | flops 600000000 | bytes 6000000 | tf_op jit(solution)/shard_map/cube_products/pallas_call | solution.py:208
  103.9 5.3 %collective-permute-done.13.rest_0_ = bf16[4,3,128,128]{3,2,1,0:T(8,128)(2,1)S(1)} collective-permute-done((bf16[4,3,128,128]{3,2,1,0:T(8,128)(2,1)S(1)}, bf16[4,3,128,128]{3,2,1,0:T(8,128)(2,1)S(1)}, u32[]{:S(2)}, u32[]{:S(2)}) %collective-permute-start.13) | collective-permute-done | bytes 393248 | tf_op jit(solution)/shard_map/ppermute | solution.py:21
  109.3 1.9 %cube_products.3 = bf16[4,3,128,128]{3,2,1,0:T(8,128)(2,1)} custom-call(s32[24,128]{1,0:T(8,128)S(1)} %pass_table.1.table, bf16[4,3,128,128]{3,2,1,0:T(8,128)(2,1)S(1)} %collective-permute-done.13.rest_0_, bf16[135,128,128]{2,1,0:T(8,128)(2,1)S(1)} %get-tuple-element.17.rest_7_.rest_1_, f32[4,3,128,128]{3,2,1,0:T(8,128)S(1)} %cube_products.2.rest_2_), custom_call_target="tpu_custom_call" | custom-call | flops 600000000 | bytes 6000000 | tf_op jit(solution)/shard_map/cube_products/pallas_call | solution.py:208
  (22 shorter events, 6.6 us)
Async XLA Ops:
  1.7 25.8 %collective-permute-start.2 = (bf16[4,3,128,128]{3,2,1,0:T(8,128)(2,1)S(1)}, bf16[4,3,128,128]{3,2,1,0:T(8,128)(2,1)S(1)}, u32[]{:S(2)}, u32[]{:S(2)}) collective-permute-start(bf16[4,3,128,128]{3,2,1,0:T(8,128)(2,1)S(1)} %slice_bitcast_fusion.rest_0_), channel_id=1, source_target_pairs={{0,2},{1,3},{2,4},{3,5},{4,6},{5,7},{6,0},{7,1},{8,10},{9,11},{10,... | collective-permute-start | bytes 1179656 | tf_op jit(solution)/shard_map/ppermute | solution.py:21
  9.2 18.3 %collective-permute-start.1 = (bf16[4,3,128,128]{3,2,1,0:T(8,128)(2,1)S(1)}, bf16[4,3,128,128]{3,2,1,0:T(8,128)(2,1)S(1)}, u32[]{:S(2)}, u32[]{:S(2)}) collective-permute-start(bf16[4,3,128,128]{3,2,1,0:T(8,128)(2,1)S(1)} %slice_bitcast_fusion.rest_0_), channel_id=1, source_target_pairs={{0,6},{1,7},{2,0},{3,1},{4,2},{5,3},{6,4},{7,5},{8,14},{9,15},{10,... | collective-permute-start | bytes 1179656 | tf_op jit(solution)/shard_map/ppermute | solution.py:21
  11.1 16.4 %collective-permute-start = (bf16[4,3,128,128]{3,2,1,0:T(8,128)(2,1)S(1)}, bf16[4,3,128,128]{3,2,1,0:T(8,128)(2,1)S(1)}, u32[]{:S(2)}, u32[]{:S(2)}) collective-permute-start(bf16[4,3,128,128]{3,2,1,0:T(8,128)(2,1)S(1)} %slice_bitcast_fusion.rest_0_), channel_id=1, source_target_pairs={{0,1},{1,0},{2,3},{3,2},{4,5},{5,4},{6,7},{7,6},{8,9},{9,8},{10,11... | collective-permute-start | bytes 1179656 | tf_op jit(solution)/shard_map/ppermute | solution.py:21
  13.0 50.3 %collective-permute-start.8 = (bf16[48,128,128]{2,1,0:T(8,128)(2,1)}, bf16[48,128,128]{2,1,0:T(8,128)(2,1)S(1)}, u32[]{:S(2)}, u32[]{:S(2)}) collective-permute-start(bf16[48,128,128]{2,1,0:T(8,128)(2,1)} %bitcast.9), channel_id=1, source_target_pairs={{8,16},{16,8},{24,32},{32,24},{40,48},{48,40},{56,64},{64,56},{72,... | collective-permute-start | bytes 4718600 | tf_op jit(solution)/shard_map/ppermute | solution.py:225
  23.1 40.2 %collective-permute-start.7 = (bf16[48,128,128]{2,1,0:T(8,128)(2,1)}, bf16[48,128,128]{2,1,0:T(8,128)(2,1)S(1)}, u32[]{:S(2)}, u32[]{:S(2)}) collective-permute-start(bf16[48,128,128]{2,1,0:T(8,128)(2,1)} %bitcast.10), channel_id=1, source_target_pairs={{0,8},{8,0},{16,24},{24,16},{32,40},{40,32},{48,56},{56,48},{64,72... | collective-permute-start | bytes 4718600 | tf_op jit(solution)/shard_map/ppermute | solution.py:225
  25.0 0.9 copy-start.2
  25.9 0.7 copy-start.3
  27.4 35.9 %copy-start = (bf16[16,3,128,128]{3,2,1,0:T(8,128)(2,1)S(1)}, bf16[16,3,128,128]{3,2,1,0:T(8,128)(2,1)}, u32[]{:S(2)}) copy-start(bf16[16,3,128,128]{3,2,1,0:T(8,128)(2,1)} %param.3) | copy-start | bytes 4718596
  27.5 24.9 %collective-permute-start.5 = (bf16[4,3,128,128]{3,2,1,0:T(8,128)(2,1)S(1)}, bf16[4,3,128,128]{3,2,1,0:T(8,128)(2,1)S(1)}, u32[]{:S(2)}, u32[]{:S(2)}) collective-permute-start(bf16[4,3,128,128]{3,2,1,0:T(8,128)(2,1)S(1)} %collective-permute-done.rest_0_.rest_1_), channel_id=1, source_target_pairs={{0,6},{1,7},{2,0},{3,1},{4,2},{5,3},{6,4},{7,5},{8,14},{9,15},{10,... | collective-permute-start | bytes 1179656 | tf_op jit(solution)/shard_map/ppermute | solution.py:21
  30.2 24.1 %collective-permute-start.4 = (bf16[4,3,128,128]{3,2,1,0:T(8,128)(2,1)S(1)}, bf16[4,3,128,128]{3,2,1,0:T(8,128)(2,1)S(1)}, u32[]{:S(2)}, u32[]{:S(2)}) collective-permute-start(bf16[4,3,128,128]{3,2,1,0:T(8,128)(2,1)S(1)} %collective-permute-done.rest_0_.rest_1_), channel_id=1, source_target_pairs={{0,2},{1,3},{2,4},{3,5},{4,6},{5,7},{6,0},{7,1},{8,10},{9,11},{10,... | collective-permute-start | bytes 1179656 | tf_op jit(solution)/shard_map/ppermute | solution.py:21
  44.7 9.7 %collective-permute-start.3 = (bf16[4,3,128,128]{3,2,1,0:T(8,128)(2,1)S(1)}, bf16[4,3,128,128]{3,2,1,0:T(8,128)(2,1)S(1)}, u32[]{:S(2)}, u32[]{:S(2)}) collective-permute-start(bf16[4,3,128,128]{3,2,1,0:T(8,128)(2,1)S(1)} %collective-permute-done.2.rest_1_.rest_2_), channel_id=1, source_target_pairs={{0,2},{1,3},{2,4},{3,5},{4,6},{5,7},{6,0},{7,1},{8,10},{9,11},{10,... | collective-permute-start | bytes 1179656 | tf_op jit(solution)/shard_map/ppermute | solution.py:21
  52.4 10.9 %collective-permute-start.6 = (bf16[4,3,128,128]{3,2,1,0:T(8,128)(2,1)S(1)}, bf16[4,3,128,128]{3,2,1,0:T(8,128)(2,1)S(1)}, u32[]{:S(2)}, u32[]{:S(2)}) collective-permute-start(bf16[4,3,128,128]{3,2,1,0:T(8,128)(2,1)S(1)} %collective-permute-done.5.rest_5_.rest_6_), channel_id=1, source_target_pairs={{0,6},{1,7},{2,0},{3,1},{4,2},{5,3},{6,4},{7,5},{8,14},{9,15},{10,... | collective-permute-start | bytes 1179656 | tf_op jit(solution)/shard_map/ppermute | solution.py:21
  67.1 9.9 %collective-permute-start.11 = (bf16[4,3,128,128]{3,2,1,0:T(8,128)(2,1)}, bf16[4,3,128,128]{3,2,1,0:T(8,128)(2,1)S(1)}, u32[]{:S(2)}, u32[]{:S(2)}) collective-permute-start(bf16[4,3,128,128]{3,2,1,0:T(8,128)(2,1)} %get-tuple-element.9.rest_0_), channel_id=1, source_target_pairs={{0,2},{1,3},{2,4},{3,5},{4,6},{5,7},{6,0},{7,1},{8,10},{9,11},{10,... | collective-permute-start | bytes 1179656 | tf_op jit(solution)/shard_map/ppermute | solution.py:21
  69.2 14.4 %collective-permute-start.10 = (bf16[4,3,128,128]{3,2,1,0:T(8,128)(2,1)}, bf16[4,3,128,128]{3,2,1,0:T(8,128)(2,1)S(1)}, u32[]{:S(2)}, u32[]{:S(2)}) collective-permute-start(bf16[4,3,128,128]{3,2,1,0:T(8,128)(2,1)} %get-tuple-element.9.rest_0_), channel_id=1, source_target_pairs={{0,6},{1,7},{2,0},{3,1},{4,2},{5,3},{6,4},{7,5},{8,14},{9,15},{10,... | collective-permute-start | bytes 1179656 | tf_op jit(solution)/shard_map/ppermute | solution.py:21
  73.0 10.6 %collective-permute-start.9 = (bf16[4,3,128,128]{3,2,1,0:T(8,128)(2,1)}, bf16[4,3,128,128]{3,2,1,0:T(8,128)(2,1)S(1)}, u32[]{:S(2)}, u32[]{:S(2)}) collective-permute-start(bf16[4,3,128,128]{3,2,1,0:T(8,128)(2,1)} %get-tuple-element.9.rest_0_), channel_id=1, source_target_pairs={{0,1},{1,0},{2,3},{3,2},{4,5},{5,4},{6,7},{7,6},{8,9},{9,8},{10,11... | collective-permute-start | bytes 1179656 | tf_op jit(solution)/shard_map/ppermute | solution.py:21
  83.6 14.8 %collective-permute-start.12 = (bf16[4,3,128,128]{3,2,1,0:T(8,128)(2,1)S(1)}, bf16[4,3,128,128]{3,2,1,0:T(8,128)(2,1)S(1)}, u32[]{:S(2)}, u32[]{:S(2)}) collective-permute-start(bf16[4,3,128,128]{3,2,1,0:T(8,128)(2,1)S(1)} %collective-permute-done.9.rest_1_), channel_id=1, source_target_pairs={{0,6},{1,7},{2,0},{3,1},{4,2},{5,3},{6,4},{7,5},{8,14},{9,15},{10,... | collective-permute-start | bytes 1179656 | tf_op jit(solution)/shard_map/ppermute | solution.py:21
  86.7 13.7 %collective-permute-start.14 = (bf16[4,3,128,128]{3,2,1,0:T(8,128)(2,1)S(1)}, bf16[4,3,128,128]{3,2,1,0:T(8,128)(2,1)S(1)}, u32[]{:S(2)}, u32[]{:S(2)}) collective-permute-start(bf16[4,3,128,128]{3,2,1,0:T(8,128)(2,1)S(1)} %collective-permute-done.11.rest_2_), channel_id=1, source_target_pairs={{0,2},{1,3},{2,4},{3,5},{4,6},{5,7},{6,0},{7,1},{8,10},{9,11},{10,... | collective-permute-start | bytes 1179656 | tf_op jit(solution)/shard_map/ppermute | solution.py:21
  90.6 9.9 %collective-permute-start.15 = (bf16[4,3,128,128]{3,2,1,0:T(8,128)(2,1)S(1)}, bf16[4,3,128,128]{3,2,1,0:T(8,128)(2,1)S(1)}, u32[]{:S(2)}, u32[]{:S(2)}) collective-permute-start(bf16[4,3,128,128]{3,2,1,0:T(8,128)(2,1)S(1)} %collective-permute-done.9.rest_1_), channel_id=1, source_target_pairs={{0,2},{1,3},{2,4},{3,5},{4,6},{5,7},{6,0},{7,1},{8,10},{9,11},{10,... | collective-permute-start | bytes 1179656 | tf_op jit(solution)/shard_map/ppermute | solution.py:21
  98.4 10.9 %collective-permute-start.13 = (bf16[4,3,128,128]{3,2,1,0:T(8,128)(2,1)S(1)}, bf16[4,3,128,128]{3,2,1,0:T(8,128)(2,1)S(1)}, u32[]{:S(2)}, u32[]{:S(2)}) collective-permute-start(bf16[4,3,128,128]{3,2,1,0:T(8,128)(2,1)S(1)} %collective-permute-done.12.rest_6_), channel_id=1, source_target_pairs={{0,6},{1,7},{2,0},{3,1},{4,2},{5,3},{6,4},{7,5},{8,14},{9,15},{10,... | collective-permute-start | bytes 1179656 | tf_op jit(solution)/shard_map/ppermute | solution.py:21
  100.5 1.0 copy-start.1

commit v6 on v5

--- a/solution.py
+++ b/solution.py
@@ -9,7 +9,11 @@
 
 Y = 4
 LANES = 128
-ORDER_FLOPS = 6_000_000_000
+ORDER_FLOPS = 10_000_000_000
+FIRST_FLOPS = 3_000_000_000
+SOON_FLOPS = 8000_000_000
+HOW = ((False, False), (True, True))
+SOON, LATE = (0, 1, 2, 3), (4, 5, 6, 7)
 SOURCES = ((0, 0), (0, 1), (-1, 0), (1, 0), (2, 0), (-1, 1), (1, 1), (2, 1))
 
 
@@ -21,16 +25,16 @@
     return lax.ppermute(a, "narrow", pairs)
 
 
-def gather_rows(own, *beside):
+def gather_rows(own, table, by_x, direct):
     partner = moved(own, 0, 1)
+    lower = moved(own, 1, 0)
     upper = moved(own, -1, 0)
-    lower = moved(own, 1, 0)
-    partner, upper, lower, *beside = lax.optimization_barrier((partner, upper, lower, *beside))
+    partner, table = lax.optimization_barrier((partner, table))
     partner_upper = moved(partner, -1, 0)
-    partner_lower = moved(partner, 1, 0)
+    partner_lower = moved(lower, 0, 1) if by_x else moved(partner, 1, 0)
     far = moved(lower, 1, 0)
-    partner_far = moved(partner_upper, -1, 0)
-    return (own, partner, lower, upper, far, partner_lower, partner_upper, partner_far), *beside
+    partner_far = moved(partner, 2, 0) if direct else moved(partner_upper, -1, 0)
+    return (own, partner, lower, upper, far, partner_lower, partner_upper, partner_far), table
 
 
 def table_kernel(rows_dev, slots, window, block_ref, product_ref, table_ref):
@@ -95,7 +99,7 @@
     )(block_list.T, product_list.T)
 
 
-def passed(table, after):
+def passed(table, after, flops):
     def kernel(table_ref, *rest):
         rest[-1][...] = table_ref[...]
 
@@ -106,13 +110,14 @@
         out_specs=LOCAL,
         compiler_params=pltpu.CompilerParams(vmem_limit_bytes=1024 * 1024),
         name="pass_table",
-        cost_estimate=pl.CostEstimate(flops=ORDER_FLOPS, bytes_accessed=0, transcendentals=0),
+        cost_estimate=pl.CostEstimate(flops=flops, bytes_accessed=0, transcendentals=0),
     )(table, *after)
 
 
 LOCAL = pl.BlockSpec(memory_space=pltpu.VMEM)
 SCALAR = pl.BlockSpec(memory_space=pltpu.SMEM)
 PARAMS = pltpu.CompilerParams(vmem_limit_bytes=8 * 1024 * 1024)
+SOON_COST = pl.CostEstimate(flops=SOON_FLOPS, bytes_accessed=6_000_000, transcendentals=0)
 COST = pl.CostEstimate(flops=600_000_000, bytes_accessed=6_000_000, transcendentals=0)
 
 
@@ -202,7 +207,9 @@
     )(table, *lefts, *rights)
 
 
-def multiply(sources, table, lefts, ext, start, window, slots, out_type):
+def multiply(which, table, lefts, ext, start, window, slots, out_type):
+    sources = [SOURCES[j] for j in which]
+    lefts = [lefts[j] for j in which]
     block = lefts[0].shape[2:]
     extra = () if start is None else (start,)
     return pl.pallas_call(
@@ -212,7 +219,7 @@
         out_specs=LOCAL,
         compiler_params=PARAMS,
         name="cube_products",
-        cost_estimate=COST,
+        cost_estimate=SOON_COST if start is None else COST,
     )(table, *lefts, ext, *extra)
 
 
@@ -233,13 +240,14 @@
     next_chip = swapped(blocks, "wide", 1)
     local = density.reshape((window, step) + density.shape[1:])[:, 0]
     table = build_table(block_list, product_list, rows_dev, slots, window)
-    lefts, table = gather_rows(local, table)
-    table = passed(table, lefts[1:])
+    lefts, table = gather_rows(local, table, *HOW[0])
     chip = swapped(blocks, "wide", 0)
+    table = passed(table, (lefts[3], lefts[5]), FIRST_FLOPS)
+    table = passed(table, lefts[1:], ORDER_FLOPS)
     square, ext = multiply_first(table, lefts, (chip, blocks, next_chip), window, slots)
-    (lefts,) = gather_rows(square)
-    part = multiply(SOURCES[:-1], table, lefts[:-1], ext, None, window, slots, jnp.float32)
-    cube = multiply(SOURCES[-1:], table, lefts[-1:], ext, part, window, slots, jnp.bfloat16)
+    lefts, table = gather_rows(square, table, *HOW[1])
+    part = multiply(SOON, table, lefts, ext, None, window, slots, jnp.float32)
+    cube = multiply(LATE, table, lefts, ext, part, window, slots, jnp.bfloat16)
     return square, cube
 
 

time: 112 us -> 94.1 us (0.84)
  waiting for transfers between devices: 32.8 us -> 21.6 us
  starting transfers between devices: 65 us -> 58 us
    ppermute x14, waiting for transfers between devices: 32.8 us -> 21.6 us  [moved(): return lax.ppermute(a, 'narrow', pairs)]
    ppermute x14, starting transfers between devices: 53 us -> 45.2 us  [moved(): return lax.ppermute(a, 'narrow', pairs)]
  transfers between devices with their start and end apart: 16 -> 16, of which waited for: 7 -> 6; matrix products, arithmetic and copies ran while one was open for 0% -> 0% of each run, Pallas kernels for 3% -> 3%
where the time goes in v6:
time: 94.1 us; the launch traced here: 93 us
  starting transfers between devices  58 us (62%)
  waiting for transfers between devices  21.6 us (23%)
  Pallas kernels  8.81 us (9%)
  local copies, waits for them, and re-layouts  3.65 us (4%)
    ppermute x14, starting transfers between devices, moved(): return lax.ppermute(a, 'narrow', pairs)  45.2 us
    ppermute x14, waiting for transfers between devices, moved(): return lax.ppermute(a, 'narrow', pairs)  21.6 us
    ppermute x2, starting transfers between devices, swapped(): return lax.ppermute(x, axis, pairs)  12.8 us
    pallas_call x2, Pallas kernels, multiply(): pl.pallas_call(functools.partial(next_kernel, sources, window, slots), ou...  4.21 us
    pallas_call x1, Pallas kernels, multiply_first(): pl.pallas_call(functools.partial(first_kernel, window, slots), out_shape=...  3.85 us
    unnamed x8, local copies, waits for them, and re-layouts  2.62 us
  transfers between devices with their start and end apart: 16, of which 6 were waited for; matrix products, arithmetic and copies ran while one was open for 0% of the time, Pallas kernels for 3%

profile of v6, /device:TPU:24, one launch (start us, length us, event | category | flops | bytes accessed | tf_op | source)
XLA Modules:
  0.0 93.0 jit_solution(15765258620093999490)
XLA Ops:
  1.7 3.4 %collective-permute-start = (bf16[4,3,128,128]{3,2,1,0:T(8,128)(2,1)S(1)}, bf16[4,3,128,128]{3,2,1,0:T(8,128)(2,1)S(1)}, u32[]{:S(2)}, u32[]{:S(2)}) collective-permute-start(bf16[4,3,128,128]{3,2,1,0:T(8,128)(2,1)S(1)} %slice_bitcast_fusion.rest_0_), channel_id=1, source_target_pairs={{0,1},{1,0},{2,3},{3,2},{4,5},{5,4},{6,7},{7,6},{8,9},{9,8},{10,11... | collective-permute-start | bytes 1179656 | tf_op jit(solution)/shard_map/ppermute | solution.py:25
  5.1 6.0 %collective-permute-start.3 = (bf16[4,3,128,128]{3,2,1,0:T(8,128)(2,1)S(1)}, bf16[4,3,128,128]{3,2,1,0:T(8,128)(2,1)S(1)}, u32[]{:S(2)}, u32[]{:S(2)}) collective-permute-start(bf16[4,3,128,128]{3,2,1,0:T(8,128)(2,1)S(1)} %slice_bitcast_fusion.rest_0_), channel_id=1, source_target_pairs={{0,2},{1,3},{2,4},{3,5},{4,6},{5,7},{6,0},{7,1},{8,10},{9,11},{10,... | collective-permute-start | bytes 1179656 | tf_op jit(solution)/shard_map/ppermute | solution.py:25
  11.1 1.9 %collective-permute-start.1 = (bf16[4,3,128,128]{3,2,1,0:T(8,128)(2,1)S(1)}, bf16[4,3,128,128]{3,2,1,0:T(8,128)(2,1)S(1)}, u32[]{:S(2)}, u32[]{:S(2)}) collective-permute-start(bf16[4,3,128,128]{3,2,1,0:T(8,128)(2,1)S(1)} %slice_bitcast_fusion.rest_0_), channel_id=1, source_target_pairs={{0,6},{1,7},{2,0},{3,1},{4,2},{5,3},{6,4},{7,5},{8,14},{9,15},{10,... | collective-permute-start | bytes 1179656 | tf_op jit(solution)/shard_map/ppermute | solution.py:25
  15.4 1.9 %collective-permute-start.5 = (bf16[4,3,128,128]{3,2,1,0:T(8,128)(2,1)S(1)}, bf16[4,3,128,128]{3,2,1,0:T(8,128)(2,1)S(1)}, u32[]{:S(2)}, u32[]{:S(2)}) collective-permute-start(bf16[4,3,128,128]{3,2,1,0:T(8,128)(2,1)S(1)} %collective-permute-done.rest_0_.rest_1_), channel_id=1, source_target_pairs={{0,6},{1,7},{2,0},{3,1},{4,2},{5,3},{6,4},{7,5},{8,14},{9,15},{10,... | collective-permute-start | bytes 1179656 | tf_op jit(solution)/shard_map/ppermute | solution.py:25
  17.3 5.1 %collective-permute-start.2 = (bf16[4,3,128,128]{3,2,1,0:T(8,128)(2,1)S(1)}, bf16[4,3,128,128]{3,2,1,0:T(8,128)(2,1)S(1)}, u32[]{:S(2)}, u32[]{:S(2)}) collective-permute-start(bf16[4,3,128,128]{3,2,1,0:T(8,128)(2,1)S(1)} %collective-permute-done.rest_0_.rest_1_), channel_id=1, source_target_pairs={{0,2},{1,3},{2,4},{3,5},{4,6},{5,7},{6,0},{7,1},{8,10},{9,11},{10,... | collective-permute-start | bytes 1179656 | tf_op jit(solution)/shard_map/ppermute | solution.py:25
  22.5 10.9 %collective-permute-start.8 = (bf16[48,128,128]{2,1,0:T(8,128)(2,1)}, bf16[48,128,128]{2,1,0:T(8,128)(2,1)S(1)}, u32[]{:S(2)}, u32[]{:S(2)}) collective-permute-start(bf16[48,128,128]{2,1,0:T(8,128)(2,1)} %bitcast.9), channel_id=1, source_target_pairs={{8,16},{16,8},{24,32},{32,24},{40,48},{48,40},{56,64},{64,56},{72,... | collective-permute-start | bytes 4718600 | tf_op jit(solution)/shard_map/ppermute | solution.py:232
  33.4 1.9 %collective-permute-start.7 = (bf16[48,128,128]{2,1,0:T(8,128)(2,1)}, bf16[48,128,128]{2,1,0:T(8,128)(2,1)S(1)}, u32[]{:S(2)}, u32[]{:S(2)}) collective-permute-start(bf16[48,128,128]{2,1,0:T(8,128)(2,1)} %bitcast.10), channel_id=1, source_target_pairs={{0,8},{8,0},{16,24},{24,16},{32,40},{40,32},{48,56},{56,48},{64,72... | collective-permute-start | bytes 4718600 | tf_op jit(solution)/shard_map/ppermute | solution.py:232
  35.3 2.2 %collective-permute-start.4 = (bf16[4,3,128,128]{3,2,1,0:T(8,128)(2,1)S(1)}, bf16[4,3,128,128]{3,2,1,0:T(8,128)(2,1)S(1)}, u32[]{:S(2)}, u32[]{:S(2)}) collective-permute-start(bf16[4,3,128,128]{3,2,1,0:T(8,128)(2,1)S(1)} %collective-permute-done.3.rest_1_.rest_2_), channel_id=1, source_target_pairs={{0,2},{1,3},{2,4},{3,5},{4,6},{5,7},{6,0},{7,1},{8,10},{9,11},{10,... | collective-permute-start | bytes 1179656 | tf_op jit(solution)/shard_map/ppermute | solution.py:25
  37.5 3.6 %collective-permute-start.6 = (bf16[4,3,128,128]{3,2,1,0:T(8,128)(2,1)S(1)}, bf16[4,3,128,128]{3,2,1,0:T(8,128)(2,1)S(1)}, u32[]{:S(2)}, u32[]{:S(2)}) collective-permute-start(bf16[4,3,128,128]{3,2,1,0:T(8,128)(2,1)S(1)} %collective-permute-done.5.rest_5_.rest_6_), channel_id=1, source_target_pairs={{0,6},{1,7},{2,0},{3,1},{4,2},{5,3},{6,4},{7,5},{8,14},{9,15},{10,... | collective-permute-start | bytes 1179656 | tf_op jit(solution)/shard_map/ppermute | solution.py:25
  41.2 7.5 %collective-permute-done.4.rest_3_.rest_4_ = bf16[4,3,128,128]{3,2,1,0:T(8,128)(2,1)S(1)} collective-permute-done((bf16[4,3,128,128]{3,2,1,0:T(8,128)(2,1)S(1)}, bf16[4,3,128,128]{3,2,1,0:T(8,128)(2,1)S(1)}, u32[]{:S(2)}, u32[]{:S(2)}) %collective-permute-start.4) | collective-permute-done | bytes 393248 | tf_op jit(solution)/shard_map/ppermute | solution.py:25
  48.7 3.1 %collective-permute-done.6.rest_6_.rest_7_ = bf16[4,3,128,128]{3,2,1,0:T(8,128)(2,1)S(1)} collective-permute-done((bf16[4,3,128,128]{3,2,1,0:T(8,128)(2,1)S(1)}, bf16[4,3,128,128]{3,2,1,0:T(8,128)(2,1)S(1)}, u32[]{:S(2)}, u32[]{:S(2)}) %collective-permute-start.6) | collective-permute-done | bytes 393248 | tf_op jit(solution)/shard_map/ppermute | solution.py:25
  51.9 3.9 %square_products.1 = (bf16[4,3,128,128]{3,2,1,0:T(8,128)(2,1)}, bf16[135,128,128]{2,1,0:T(8,128)(2,1)S(1)}) custom-call(s32[24,128]{1,0:T(8,128)S(1)} %pass_table.3.table, bf16[4,3,128,128]{3,2,1,0:T(8,128)(2,1)S(1)} %slice_bitcast_fusion.rest_0_, bf16[4,3,128,128]{3,2,1,0:T(8,128)(2,1)S(1)} %collective-permute-done.rest_0_.rest_1_, ...), custom_call_target="tpu_custom_call" | custom-call | flops 600000000 | bytes 6000000 | tf_op jit(solution)/shard_map/square_products/pallas_call | solution.py:195
  55.7 2.5 %collective-permute-start.9 = (bf16[4,3,128,128]{3,2,1,0:T(8,128)(2,1)}, bf16[4,3,128,128]{3,2,1,0:T(8,128)(2,1)S(1)}, u32[]{:S(2)}, u32[]{:S(2)}) collective-permute-start(bf16[4,3,128,128]{3,2,1,0:T(8,128)(2,1)} %get-tuple-element.6.rest_0_), channel_id=1, source_target_pairs={{0,1},{1,0},{2,3},{3,2},{4,5},{5,4},{6,7},{7,6},{8,9},{9,8},{10,11... | collective-permute-start | bytes 1179656 | tf_op jit(solution)/shard_map/ppermute | solution.py:25
  58.2 2.0 %collective-permute-start.10 = (bf16[4,3,128,128]{3,2,1,0:T(8,128)(2,1)}, bf16[4,3,128,128]{3,2,1,0:T(8,128)(2,1)S(1)}, u32[]{:S(2)}, u32[]{:S(2)}) collective-permute-start(bf16[4,3,128,128]{3,2,1,0:T(8,128)(2,1)} %get-tuple-element.6.rest_0_), channel_id=1, source_target_pairs={{0,2},{1,3},{2,4},{3,5},{4,6},{5,7},{6,0},{7,1},{8,10},{9,11},{10,... | collective-permute-start | bytes 1179656 | tf_op jit(solution)/shard_map/ppermute | solution.py:25
  60.2 3.9 %collective-permute-start.15 = (bf16[4,3,128,128]{3,2,1,0:T(8,128)(2,1)}, bf16[4,3,128,128]{3,2,1,0:T(8,128)(2,1)S(1)}, u32[]{:S(2)}, u32[]{:S(2)}) collective-permute-start(bf16[4,3,128,128]{3,2,1,0:T(8,128)(2,1)} %get-tuple-element.6.rest_0_), channel_id=1, source_target_pairs={{0,6},{1,7},{2,0},{3,1},{4,2},{5,3},{6,4},{7,5},{8,14},{9,15},{10,... | collective-permute-start | bytes 1179656 | tf_op jit(solution)/shard_map/ppermute | solution.py:25
  64.1 4.2 %collective-permute-done.9.rest_1_ = bf16[4,3,128,128]{3,2,1,0:T(8,128)(2,1)S(1)} collective-permute-done((bf16[4,3,128,128]{3,2,1,0:T(8,128)(2,1)}, bf16[4,3,128,128]{3,2,1,0:T(8,128)(2,1)S(1)}, u32[]{:S(2)}, u32[]{:S(2)}) %collective-permute-start.9) | collective-permute-done | bytes 393248 | tf_op jit(solution)/shard_map/ppermute | solution.py:25
  68.3 3.1 %collective-permute-start.14 = (bf16[4,3,128,128]{3,2,1,0:T(8,128)(2,1)S(1)}, bf16[4,3,128,128]{3,2,1,0:T(8,128)(2,1)S(1)}, u32[]{:S(2)}, u32[]{:S(2)}) collective-permute-start(bf16[4,3,128,128]{3,2,1,0:T(8,128)(2,1)S(1)} %collective-permute-done.9.rest_1_), channel_id=1, source_target_pairs={{0,4},{1,5},{2,6},{3,7},{4,0},{5,1},{6,2},{7,3},{8,12},{9,13},{10,... | collective-permute-start | bytes 1179656 | tf_op jit(solution)/shard_map/ppermute | solution.py:25
  71.3 1.9 %collective-permute-start.13 = (bf16[4,3,128,128]{3,2,1,0:T(8,128)(2,1)S(1)}, bf16[4,3,128,128]{3,2,1,0:T(8,128)(2,1)S(1)}, u32[]{:S(2)}, u32[]{:S(2)}) collective-permute-start(bf16[4,3,128,128]{3,2,1,0:T(8,128)(2,1)S(1)} %collective-permute-done.9.rest_1_), channel_id=1, source_target_pairs={{0,6},{1,7},{2,0},{3,1},{4,2},{5,3},{6,4},{7,5},{8,14},{9,15},{10,... | collective-permute-start | bytes 1179656 | tf_op jit(solution)/shard_map/ppermute | solution.py:25
  73.3 2.5 %collective-permute-start.12 = (bf16[4,3,128,128]{3,2,1,0:T(8,128)(2,1)S(1)}, bf16[4,3,128,128]{3,2,1,0:T(8,128)(2,1)S(1)}, u32[]{:S(2)}, u32[]{:S(2)}) collective-permute-start(bf16[4,3,128,128]{3,2,1,0:T(8,128)(2,1)S(1)} %collective-permute-done.10.rest_2_), channel_id=1, source_target_pairs={{0,1},{1,0},{2,3},{3,2},{4,5},{5,4},{6,7},{7,6},{8,9},{9,8},{10,11... | collective-permute-start | bytes 1179656 | tf_op jit(solution)/shard_map/ppermute | solution.py:25
  75.8 5.1 %collective-permute-start.11 = (bf16[4,3,128,128]{3,2,1,0:T(8,128)(2,1)S(1)}, bf16[4,3,128,128]{3,2,1,0:T(8,128)(2,1)S(1)}, u32[]{:S(2)}, u32[]{:S(2)}) collective-permute-start(bf16[4,3,128,128]{3,2,1,0:T(8,128)(2,1)S(1)} %collective-permute-done.10.rest_2_), channel_id=1, source_target_pairs={{0,2},{1,3},{2,4},{3,5},{4,6},{5,7},{6,0},{7,1},{8,10},{9,11},{10,... | collective-permute-start | bytes 1179656 | tf_op jit(solution)/shard_map/ppermute | solution.py:25
  81.9 1.7 %cube_products.2.rest_5_ = f32[4,3,128,128]{3,2,1,0:T(8,128)S(1)} custom-call(s32[24,128]{1,0:T(8,128)S(1)} %pass_table.3.table, bf16[4,3,128,128]{3,2,1,0:T(8,128)(2,1)S(1)} %copy-done.3, bf16[4,3,128,128]{3,2,1,0:T(8,128)(2,1)S(1)} %collective-permute-done.9.rest_1_, bf16[4,3,128,128]{3,2,1,0:T(8,128)(2,1)S(1)} %collective-permute-done.10.rest_2_, ...), custom_call_target="tpu_custom_call" | custom-call | flops 8000000000 | bytes 6000000 | tf_op jit(solution)/shard_map/cube_products/pallas_call | solution.py:215
  84.7 2.7 %collective-permute-done.11.rest_0_ = bf16[4,3,128,128]{3,2,1,0:T(8,128)(2,1)S(1)} collective-permute-done((bf16[4,3,128,128]{3,2,1,0:T(8,128)(2,1)S(1)}, bf16[4,3,128,128]{3,2,1,0:T(8,128)(2,1)S(1)}, u32[]{:S(2)}, u32[]{:S(2)}) %collective-permute-start.11) | collective-permute-done | bytes 393248 | tf_op jit(solution)/shard_map/ppermute | solution.py:25
  87.4 3.0 %collective-permute-done.13.rest_2_ = bf16[4,3,128,128]{3,2,1,0:T(8,128)(2,1)S(1)} collective-permute-done((bf16[4,3,128,128]{3,2,1,0:T(8,128)(2,1)S(1)}, bf16[4,3,128,128]{3,2,1,0:T(8,128)(2,1)S(1)}, u32[]{:S(2)}, u32[]{:S(2)}) %collective-permute-start.13) | collective-permute-done | bytes 393248 | tf_op jit(solution)/shard_map/ppermute | solution.py:25
  90.5 2.5 %cube_products.3 = bf16[4,3,128,128]{3,2,1,0:T(8,128)(2,1)} custom-call(s32[24,128]{1,0:T(8,128)S(1)} %pass_table.3.table, bf16[4,3,128,128]{3,2,1,0:T(8,128)(2,1)S(1)} %collective-permute-done.11.rest_0_, bf16[4,3,128,128]{3,2,1,0:T(8,128)(2,1)S(1)} %collective-permute-done.12.rest_1_, bf16[4,3,128,128]{3,2,1,0:T(8,128)(2,1)S(1)} %collective-permute-done.13.rest_2_, ...), custom_call_target="tpu_custom_call" | custom-call | flops 600000000 | bytes 6000000 | tf_op jit(solution)/shard_map/cube_products/pallas_call | solution.py:215
  (23 shorter events, 5.5 us)
Async XLA Ops:
  1.7 13.8 %collective-permute-start = (bf16[4,3,128,128]{3,2,1,0:T(8,128)(2,1)S(1)}, bf16[4,3,128,128]{3,2,1,0:T(8,128)(2,1)S(1)}, u32[]{:S(2)}, u32[]{:S(2)}) collective-permute-start(bf16[4,3,128,128]{3,2,1,0:T(8,128)(2,1)S(1)} %slice_bitcast_fusion.rest_0_), channel_id=1, source_target_pairs={{0,1},{1,0},{2,3},{3,2},{4,5},{5,4},{6,7},{7,6},{8,9},{9,8},{10,11... | collective-permute-start | bytes 1179656 | tf_op jit(solution)/shard_map/ppermute | solution.py:25
  5.1 28.3 %collective-permute-start.3 = (bf16[4,3,128,128]{3,2,1,0:T(8,128)(2,1)S(1)}, bf16[4,3,128,128]{3,2,1,0:T(8,128)(2,1)S(1)}, u32[]{:S(2)}, u32[]{:S(2)}) collective-permute-start(bf16[4,3,128,128]{3,2,1,0:T(8,128)(2,1)S(1)} %slice_bitcast_fusion.rest_0_), channel_id=1, source_target_pairs={{0,2},{1,3},{2,4},{3,5},{4,6},{5,7},{6,0},{7,1},{8,10},{9,11},{10,... | collective-permute-start | bytes 1179656 | tf_op jit(solution)/shard_map/ppermute | solution.py:25
  11.1 24.2 %collective-permute-start.1 = (bf16[4,3,128,128]{3,2,1,0:T(8,128)(2,1)S(1)}, bf16[4,3,128,128]{3,2,1,0:T(8,128)(2,1)S(1)}, u32[]{:S(2)}, u32[]{:S(2)}) collective-permute-start(bf16[4,3,128,128]{3,2,1,0:T(8,128)(2,1)S(1)} %slice_bitcast_fusion.rest_0_), channel_id=1, source_target_pairs={{0,6},{1,7},{2,0},{3,1},{4,2},{5,3},{6,4},{7,5},{8,14},{9,15},{10,... | collective-permute-start | bytes 1179656 | tf_op jit(solution)/shard_map/ppermute | solution.py:25
  13.0 0.9 copy-start.1
  13.9 0.7 copy-start.2
  15.4 22.1 %collective-permute-start.5 = (bf16[4,3,128,128]{3,2,1,0:T(8,128)(2,1)S(1)}, bf16[4,3,128,128]{3,2,1,0:T(8,128)(2,1)S(1)}, u32[]{:S(2)}, u32[]{:S(2)}) collective-permute-start(bf16[4,3,128,128]{3,2,1,0:T(8,128)(2,1)S(1)} %collective-permute-done.rest_0_.rest_1_), channel_id=1, source_target_pairs={{0,6},{1,7},{2,0},{3,1},{4,2},{5,3},{6,4},{7,5},{8,14},{9,15},{10,... | collective-permute-start | bytes 1179656 | tf_op jit(solution)/shard_map/ppermute | solution.py:25
  17.3 23.8 %collective-permute-start.2 = (bf16[4,3,128,128]{3,2,1,0:T(8,128)(2,1)S(1)}, bf16[4,3,128,128]{3,2,1,0:T(8,128)(2,1)S(1)}, u32[]{:S(2)}, u32[]{:S(2)}) collective-permute-start(bf16[4,3,128,128]{3,2,1,0:T(8,128)(2,1)S(1)} %collective-permute-done.rest_0_.rest_1_), channel_id=1, source_target_pairs={{0,2},{1,3},{2,4},{3,5},{4,6},{5,7},{6,0},{7,1},{8,10},{9,11},{10,... | collective-permute-start | bytes 1179656 | tf_op jit(solution)/shard_map/ppermute | solution.py:25
  22.5 29.4 %collective-permute-start.8 = (bf16[48,128,128]{2,1,0:T(8,128)(2,1)}, bf16[48,128,128]{2,1,0:T(8,128)(2,1)S(1)}, u32[]{:S(2)}, u32[]{:S(2)}) collective-permute-start(bf16[48,128,128]{2,1,0:T(8,128)(2,1)} %bitcast.9), channel_id=1, source_target_pairs={{8,16},{16,8},{24,32},{32,24},{40,48},{48,40},{56,64},{64,56},{72,... | collective-permute-start | bytes 4718600 | tf_op jit(solution)/shard_map/ppermute | solution.py:232
  33.4 18.5 %collective-permute-start.7 = (bf16[48,128,128]{2,1,0:T(8,128)(2,1)}, bf16[48,128,128]{2,1,0:T(8,128)(2,1)S(1)}, u32[]{:S(2)}, u32[]{:S(2)}) collective-permute-start(bf16[48,128,128]{2,1,0:T(8,128)(2,1)} %bitcast.10), channel_id=1, source_target_pairs={{0,8},{8,0},{16,24},{24,16},{32,40},{40,32},{48,56},{56,48},{64,72... | collective-permute-start | bytes 4718600 | tf_op jit(solution)/shard_map/ppermute | solution.py:232
  35.3 13.4 %collective-permute-start.4 = (bf16[4,3,128,128]{3,2,1,0:T(8,128)(2,1)S(1)}, bf16[4,3,128,128]{3,2,1,0:T(8,128)(2,1)S(1)}, u32[]{:S(2)}, u32[]{:S(2)}) collective-permute-start(bf16[4,3,128,128]{3,2,1,0:T(8,128)(2,1)S(1)} %collective-permute-done.3.rest_1_.rest_2_), channel_id=1, source_target_pairs={{0,2},{1,3},{2,4},{3,5},{4,6},{5,7},{6,0},{7,1},{8,10},{9,11},{10,... | collective-permute-start | bytes 1179656 | tf_op jit(solution)/shard_map/ppermute | solution.py:25
  37.5 14.3 %collective-permute-start.6 = (bf16[4,3,128,128]{3,2,1,0:T(8,128)(2,1)S(1)}, bf16[4,3,128,128]{3,2,1,0:T(8,128)(2,1)S(1)}, u32[]{:S(2)}, u32[]{:S(2)}) collective-permute-start(bf16[4,3,128,128]{3,2,1,0:T(8,128)(2,1)S(1)} %collective-permute-done.5.rest_5_.rest_6_), channel_id=1, source_target_pairs={{0,6},{1,7},{2,0},{3,1},{4,2},{5,3},{6,4},{7,5},{8,14},{9,15},{10,... | collective-permute-start | bytes 1179656 | tf_op jit(solution)/shard_map/ppermute | solution.py:25
  41.2 10.7 %copy-start = (bf16[16,3,128,128]{3,2,1,0:T(8,128)(2,1)S(1)}, bf16[16,3,128,128]{3,2,1,0:T(8,128)(2,1)}, u32[]{:S(2)}) copy-start(bf16[16,3,128,128]{3,2,1,0:T(8,128)(2,1)} %param.3) | copy-start | bytes 4718596
  55.7 12.5 %collective-permute-start.9 = (bf16[4,3,128,128]{3,2,1,0:T(8,128)(2,1)}, bf16[4,3,128,128]{3,2,1,0:T(8,128)(2,1)S(1)}, u32[]{:S(2)}, u32[]{:S(2)}) collective-permute-start(bf16[4,3,128,128]{3,2,1,0:T(8,128)(2,1)} %get-tuple-element.6.rest_0_), channel_id=1, source_target_pairs={{0,1},{1,0},{2,3},{3,2},{4,5},{5,4},{6,7},{7,6},{8,9},{9,8},{10,11... | collective-permute-start | bytes 1179656 | tf_op jit(solution)/shard_map/ppermute | solution.py:25
  58.2 15.0 %collective-permute-start.10 = (bf16[4,3,128,128]{3,2,1,0:T(8,128)(2,1)}, bf16[4,3,128,128]{3,2,1,0:T(8,128)(2,1)S(1)}, u32[]{:S(2)}, u32[]{:S(2)}) collective-permute-start(bf16[4,3,128,128]{3,2,1,0:T(8,128)(2,1)} %get-tuple-element.6.rest_0_), channel_id=1, source_target_pairs={{0,2},{1,3},{2,4},{3,5},{4,6},{5,7},{6,0},{7,1},{8,10},{9,11},{10,... | collective-permute-start | bytes 1179656 | tf_op jit(solution)/shard_map/ppermute | solution.py:25
  60.2 20.7 %collective-permute-start.15 = (bf16[4,3,128,128]{3,2,1,0:T(8,128)(2,1)}, bf16[4,3,128,128]{3,2,1,0:T(8,128)(2,1)S(1)}, u32[]{:S(2)}, u32[]{:S(2)}) collective-permute-start(bf16[4,3,128,128]{3,2,1,0:T(8,128)(2,1)} %get-tuple-element.6.rest_0_), channel_id=1, source_target_pairs={{0,6},{1,7},{2,0},{3,1},{4,2},{5,3},{6,4},{7,5},{8,14},{9,15},{10,... | collective-permute-start | bytes 1179656 | tf_op jit(solution)/shard_map/ppermute | solution.py:25
  68.3 19.2 %collective-permute-start.14 = (bf16[4,3,128,128]{3,2,1,0:T(8,128)(2,1)S(1)}, bf16[4,3,128,128]{3,2,1,0:T(8,128)(2,1)S(1)}, u32[]{:S(2)}, u32[]{:S(2)}) collective-permute-start(bf16[4,3,128,128]{3,2,1,0:T(8,128)(2,1)S(1)} %collective-permute-done.9.rest_1_), channel_id=1, source_target_pairs={{0,4},{1,5},{2,6},{3,7},{4,0},{5,1},{6,2},{7,3},{8,12},{9,13},{10,... | collective-permute-start | bytes 1179656 | tf_op jit(solution)/shard_map/ppermute | solution.py:25
  71.3 19.1 %collective-permute-start.13 = (bf16[4,3,128,128]{3,2,1,0:T(8,128)(2,1)S(1)}, bf16[4,3,128,128]{3,2,1,0:T(8,128)(2,1)S(1)}, u32[]{:S(2)}, u32[]{:S(2)}) collective-permute-start(bf16[4,3,128,128]{3,2,1,0:T(8,128)(2,1)S(1)} %collective-permute-done.9.rest_1_), channel_id=1, source_target_pairs={{0,6},{1,7},{2,0},{3,1},{4,2},{5,3},{6,4},{7,5},{8,14},{9,15},{10,... | collective-permute-start | bytes 1179656 | tf_op jit(solution)/shard_map/ppermute | solution.py:25
  73.3 11.5 %collective-permute-start.12 = (bf16[4,3,128,128]{3,2,1,0:T(8,128)(2,1)S(1)}, bf16[4,3,128,128]{3,2,1,0:T(8,128)(2,1)S(1)}, u32[]{:S(2)}, u32[]{:S(2)}) collective-permute-start(bf16[4,3,128,128]{3,2,1,0:T(8,128)(2,1)S(1)} %collective-permute-done.10.rest_2_), channel_id=1, source_target_pairs={{0,1},{1,0},{2,3},{3,2},{4,5},{5,4},{6,7},{7,6},{8,9},{9,8},{10,11... | collective-permute-start | bytes 1179656 | tf_op jit(solution)/shard_map/ppermute | solution.py:25
  75.8 11.6 %collective-permute-start.11 = (bf16[4,3,128,128]{3,2,1,0:T(8,128)(2,1)S(1)}, bf16[4,3,128,128]{3,2,1,0:T(8,128)(2,1)S(1)}, u32[]{:S(2)}, u32[]{:S(2)}) collective-permute-start(bf16[4,3,128,128]{3,2,1,0:T(8,128)(2,1)S(1)} %collective-permute-done.10.rest_2_), channel_id=1, source_target_pairs={{0,2},{1,3},{2,4},{3,5},{4,6},{5,7},{6,0},{7,1},{8,10},{9,11},{10,... | collective-permute-start | bytes 1179656 | tf_op jit(solution)/shard_map/ppermute | solution.py:25
  80.9 1.0 %copy-start.3 = (bf16[4,3,128,128]{3,2,1,0:T(8,128)(2,1)S(1)}, bf16[4,3,128,128]{3,2,1,0:T(8,128)(2,1)}, u32[]{:S(2)}) copy-start(bf16[4,3,128,128]{3,2,1,0:T(8,128)(2,1)} %get-tuple-element.6.rest_0_) | copy-start | bytes 1179652

commit v7 on v6

--- a/solution.py
+++ b/solution.py
@@ -9,10 +9,10 @@
 
 Y = 4
 LANES = 128
-ORDER_FLOPS = 10_000_000_000
-FIRST_FLOPS = 3_000_000_000
+ORDER_FLOPS = 6_000_000_000
+FIRST_FLOPS = 6_000_000_000
 SOON_FLOPS = 8000_000_000
-HOW = ((False, False), (True, True))
+HOW = (("", False), ("l", True))
 SOON, LATE = (0, 1, 2, 3), (4, 5, 6, 7)
 SOURCES = ((0, 0), (0, 1), (-1, 0), (1, 0), (2, 0), (-1, 1), (1, 1), (2, 1))
 
@@ -30,10 +30,13 @@
     lower = moved(own, 1, 0)
     upper = moved(own, -1, 0)
     partner, table = lax.optimization_barrier((partner, table))
-    partner_upper = moved(partner, -1, 0)
-    partner_lower = moved(lower, 0, 1) if by_x else moved(partner, 1, 0)
+    partner_upper = moved(upper, 0, 1) if "u" in by_x else moved(partner, -1, 0)
+    partner_lower = moved(lower, 0, 1) if "l" in by_x else moved(partner, 1, 0)
     far = moved(lower, 1, 0)
-    partner_far = moved(partner, 2, 0) if direct else moved(partner_upper, -1, 0)
+    if "f" in by_x:
+        partner_far = moved(far, 0, 1)
+    else:
+        partner_far = moved(partner, 2, 0) if direct else moved(partner_upper, -1, 0)
     return (own, partner, lower, upper, far, partner_lower, partner_upper, partner_far), table
 
 
@@ -155,7 +158,7 @@
 
 
 def first_kernel(window, slots, table, *rest):
-    lefts, (chip, own, next_chip, out_ref, ext, sem) = rest[:-6], rest[-6:]
+    lefts, (next_chip, own, chip, out_ref, ext, sem) = rest[:-6], rest[-6:]
     rows = own.shape[0]
     tail = ext.shape[0] - slots - 2 * rows
     even = lax.rem(lax.axis_index("wide"), 2) == 0
@@ -237,14 +240,14 @@
     window = product_list.shape[0] // lax.axis_size("wide")
     step = rows_dev // window
     blocks = density.reshape((rows_dev * slots,) + density.shape[2:])
+    chip = swapped(blocks, "wide", 0)
     next_chip = swapped(blocks, "wide", 1)
     local = density.reshape((window, step) + density.shape[1:])[:, 0]
     table = build_table(block_list, product_list, rows_dev, slots, window)
-    lefts, table = gather_rows(local, table, *HOW[0])
-    chip = swapped(blocks, "wide", 0)
-    table = passed(table, (lefts[3], lefts[5]), FIRST_FLOPS)
+    lefts, _ = gather_rows(local, (), *HOW[0])
+    table = passed(table, (lefts[3], lefts[4], lefts[5]), FIRST_FLOPS)
     table = passed(table, lefts[1:], ORDER_FLOPS)
-    square, ext = multiply_first(table, lefts, (chip, blocks, next_chip), window, slots)
+    square, ext = multiply_first(table, lefts, (next_chip, blocks, chip), window, slots)
     lefts, table = gather_rows(square, table, *HOW[1])
     part = multiply(SOON, table, lefts, ext, None, window, slots, jnp.float32)
     cube = multiply(LATE, table, lefts, ext, part, window, slots, jnp.bfloat16)

time: 94.1 us -> 90.9 us (0.966)
  the two profiles are of different devices: /device:TPU:24 before, /device:TPU:32 now
where the time goes in v7:
time: 90.9 us; the launch traced here: 90.2 us
  starting transfers between devices  58.4 us (64%)
  waiting for transfers between devices  17.2 us (19%)
  Pallas kernels  8.8 us (10%)
  local copies, waits for them, and re-layouts  5.01 us (6%)
    ppermute x14, starting transfers between devices, moved(): return lax.ppermute(a, 'narrow', pairs)  50.4 us
    ppermute x14, waiting for transfers between devices, moved(): return lax.ppermute(a, 'narrow', pairs)  17.2 us
    ppermute x2, starting transfers between devices, swapped(): return lax.ppermute(x, axis, pairs)  7.94 us
    pallas_call x2, Pallas kernels, multiply(): pl.pallas_call(functools.partial(next_kernel, sources, window, slots), ou...  4.21 us
    unnamed x8, local copies, waits for them, and re-layouts  3.98 us
    pallas_call x1, Pallas kernels, multiply_first(): pl.pallas_call(functools.partial(first_kernel, window, slots), out_shape=...  3.84 us
  transfers between devices with their start and end apart: 16, of which 6 were waited for; matrix products, arithmetic and copies ran while one was open for 0% of the time, Pallas kernels for 3%

profile of v7, /device:TPU:32, one launch (start us, length us, event | category | flops | bytes accessed | tf_op | source)
XLA Modules:
  0.0 90.2 jit_solution(15042342768790698132)
XLA Ops:
  1.7 3.4 %collective-permute-start.3 = (bf16[4,3,128,128]{3,2,1,0:T(8,128)(2,1)S(1)}, bf16[4,3,128,128]{3,2,1,0:T(8,128)(2,1)S(1)}, u32[]{:S(2)}, u32[]{:S(2)}) collective-permute-start(bf16[4,3,128,128]{3,2,1,0:T(8,128)(2,1)S(1)} %slice_bitcast_fusion.rest_0_), channel_id=1, source_target_pairs={{0,1},{1,0},{2,3},{3,2},{4,5},{5,4},{6,7},{7,6},{8,9},{9,8},{10,11... | collective-permute-start | bytes 1179656 | tf_op jit(solution)/shard_map/ppermute | solution.py:25
  5.1 3.5 %collective-permute-start.1 = (bf16[4,3,128,128]{3,2,1,0:T(8,128)(2,1)S(1)}, bf16[4,3,128,128]{3,2,1,0:T(8,128)(2,1)S(1)}, u32[]{:S(2)}, u32[]{:S(2)}) collective-permute-start(bf16[4,3,128,128]{3,2,1,0:T(8,128)(2,1)S(1)} %slice_bitcast_fusion.rest_0_), channel_id=1, source_target_pairs={{0,2},{1,3},{2,4},{3,5},{4,6},{5,7},{6,0},{7,1},{8,10},{9,11},{10,... | collective-permute-start | bytes 1179656 | tf_op jit(solution)/shard_map/ppermute | solution.py:25
  8.6 3.6 %collective-permute-start = (bf16[4,3,128,128]{3,2,1,0:T(8,128)(2,1)S(1)}, bf16[4,3,128,128]{3,2,1,0:T(8,128)(2,1)S(1)}, u32[]{:S(2)}, u32[]{:S(2)}) collective-permute-start(bf16[4,3,128,128]{3,2,1,0:T(8,128)(2,1)S(1)} %slice_bitcast_fusion.rest_0_), channel_id=1, source_target_pairs={{0,6},{1,7},{2,0},{3,1},{4,2},{5,3},{6,4},{7,5},{8,14},{9,15},{10,... | collective-permute-start | bytes 1179656 | tf_op jit(solution)/shard_map/ppermute | solution.py:25
  12.1 1.9 %collective-permute-start.8 = (bf16[48,128,128]{2,1,0:T(8,128)(2,1)}, bf16[48,128,128]{2,1,0:T(8,128)(2,1)S(1)}, u32[]{:S(2)}, u32[]{:S(2)}) collective-permute-start(bf16[48,128,128]{2,1,0:T(8,128)(2,1)} %bitcast.9), channel_id=1, source_target_pairs={{0,8},{8,0},{16,24},{24,16},{32,40},{40,32},{48,56},{56,48},{64,72... | collective-permute-start | bytes 4718600 | tf_op jit(solution)/shard_map/ppermute | solution.py:235
  14.1 6.0 %collective-permute-start.7 = (bf16[48,128,128]{2,1,0:T(8,128)(2,1)}, bf16[48,128,128]{2,1,0:T(8,128)(2,1)S(1)}, u32[]{:S(2)}, u32[]{:S(2)}) collective-permute-start(bf16[48,128,128]{2,1,0:T(8,128)(2,1)} %bitcast.10), channel_id=1, source_target_pairs={{8,16},{16,8},{24,32},{32,24},{40,48},{48,40},{56,64},{64,56},{72,... | collective-permute-start | bytes 4718600 | tf_op jit(solution)/shard_map/ppermute | solution.py:235
  20.1 1.9 %collective-permute-start.5 = (bf16[4,3,128,128]{3,2,1,0:T(8,128)(2,1)S(1)}, bf16[4,3,128,128]{3,2,1,0:T(8,128)(2,1)S(1)}, u32[]{:S(2)}, u32[]{:S(2)}) collective-permute-start(bf16[4,3,128,128]{3,2,1,0:T(8,128)(2,1)S(1)} %collective-permute-done.3.rest_0_.rest_1_), channel_id=1, source_target_pairs={{0,6},{1,7},{2,0},{3,1},{4,2},{5,3},{6,4},{7,5},{8,14},{9,15},{10,... | collective-permute-start | bytes 1179656 | tf_op jit(solution)/shard_map/ppermute | solution.py:25
  22.0 3.9 %collective-permute-start.4 = (bf16[4,3,128,128]{3,2,1,0:T(8,128)(2,1)S(1)}, bf16[4,3,128,128]{3,2,1,0:T(8,128)(2,1)S(1)}, u32[]{:S(2)}, u32[]{:S(2)}) collective-permute-start(bf16[4,3,128,128]{3,2,1,0:T(8,128)(2,1)S(1)} %collective-permute-done.3.rest_0_.rest_1_), channel_id=1, source_target_pairs={{0,2},{1,3},{2,4},{3,5},{4,6},{5,7},{6,0},{7,1},{8,10},{9,11},{10,... | collective-permute-start | bytes 1179656 | tf_op jit(solution)/shard_map/ppermute | solution.py:25
  26.0 1.9 %collective-permute-start.2 = (bf16[4,3,128,128]{3,2,1,0:T(8,128)(2,1)S(1)}, bf16[4,3,128,128]{3,2,1,0:T(8,128)(2,1)S(1)}, u32[]{:S(2)}, u32[]{:S(2)}) collective-permute-start(bf16[4,3,128,128]{3,2,1,0:T(8,128)(2,1)S(1)} %collective-permute-done.1.rest_1_.rest_2_), channel_id=1, source_target_pairs={{0,2},{1,3},{2,4},{3,5},{4,6},{5,7},{6,0},{7,1},{8,10},{9,11},{10,... | collective-permute-start | bytes 1179656 | tf_op jit(solution)/shard_map/ppermute | solution.py:25
  30.9 4.9 %collective-permute-start.6 = (bf16[4,3,128,128]{3,2,1,0:T(8,128)(2,1)S(1)}, bf16[4,3,128,128]{3,2,1,0:T(8,128)(2,1)S(1)}, u32[]{:S(2)}, u32[]{:S(2)}) collective-permute-start(bf16[4,3,128,128]{3,2,1,0:T(8,128)(2,1)S(1)} %collective-permute-done.5.rest_5_.rest_6_), channel_id=1, source_target_pairs={{0,6},{1,7},{2,0},{3,1},{4,2},{5,3},{6,4},{7,5},{8,14},{9,15},{10,... | collective-permute-start | bytes 1179656 | tf_op jit(solution)/shard_map/ppermute | solution.py:25
  35.9 1.3 %collective-permute-done.4.rest_2_.rest_4_.rest_5_ = bf16[4,3,128,128]{3,2,1,0:T(8,128)(2,1)S(1)} collective-permute-done((bf16[4,3,128,128]{3,2,1,0:T(8,128)(2,1)S(1)}, bf16[4,3,128,128]{3,2,1,0:T(8,128)(2,1)S(1)}, u32[]{:S(2)}, u32[]{:S(2)}) %collective-permute-start.4) | collective-permute-done | bytes 393248 | tf_op jit(solution)/shard_map/ppermute | solution.py:25
  37.2 6.8 %collective-permute-done.2.rest_1_.rest_3_.rest_4_ = bf16[4,3,128,128]{3,2,1,0:T(8,128)(2,1)S(1)} collective-permute-done((bf16[4,3,128,128]{3,2,1,0:T(8,128)(2,1)S(1)}, bf16[4,3,128,128]{3,2,1,0:T(8,128)(2,1)S(1)}, u32[]{:S(2)}, u32[]{:S(2)}) %collective-permute-start.2) | collective-permute-done | bytes 393248 | tf_op jit(solution)/shard_map/ppermute | solution.py:25
  44.1 1.4 %copy-done = bf16[16,3,128,128]{3,2,1,0:T(8,128)(2,1)S(1)} copy-done((bf16[16,3,128,128]{3,2,1,0:T(8,128)(2,1)S(1)}, bf16[16,3,128,128]{3,2,1,0:T(8,128)(2,1)}, u32[]{:S(2)}) %copy-start) | copy-done | bytes 1572888
  45.4 3.8 %square_products.1 = (bf16[4,3,128,128]{3,2,1,0:T(8,128)(2,1)}, bf16[135,128,128]{2,1,0:T(8,128)(2,1)S(1)}) custom-call(s32[24,128]{1,0:T(8,128)S(1)} %pass_table.3.table, bf16[4,3,128,128]{3,2,1,0:T(8,128)(2,1)S(1)} %slice_bitcast_fusion.rest_0_, bf16[4,3,128,128]{3,2,1,0:T(8,128)(2,1)S(1)} %collective-permute-done.3.rest_0_.rest_1_, ...), custom_call_target="tpu_custom_call" | custom-call | flops 600000000 | bytes 6000000 | tf_op jit(solution)/shard_map/square_products/pallas_call | solution.py:198
  49.3 2.4 %collective-permute-start.9 = (bf16[4,3,128,128]{3,2,1,0:T(8,128)(2,1)}, bf16[4,3,128,128]{3,2,1,0:T(8,128)(2,1)S(1)}, u32[]{:S(2)}, u32[]{:S(2)}) collective-permute-start(bf16[4,3,128,128]{3,2,1,0:T(8,128)(2,1)} %get-tuple-element.4.rest_0_), channel_id=1, source_target_pairs={{0,1},{1,0},{2,3},{3,2},{4,5},{5,4},{6,7},{7,6},{8,9},{9,8},{10,11... | collective-permute-start | bytes 1179656 | tf_op jit(solution)/shard_map/ppermute | solution.py:25
  51.7 1.9 %collective-permute-start.10 = (bf16[4,3,128,128]{3,2,1,0:T(8,128)(2,1)}, bf16[4,3,128,128]{3,2,1,0:T(8,128)(2,1)S(1)}, u32[]{:S(2)}, u32[]{:S(2)}) collective-permute-start(bf16[4,3,128,128]{3,2,1,0:T(8,128)(2,1)} %get-tuple-element.4.rest_0_), channel_id=1, source_target_pairs={{0,2},{1,3},{2,4},{3,5},{4,6},{5,7},{6,0},{7,1},{8,10},{9,11},{10,... | collective-permute-start | bytes 1179656 | tf_op jit(solution)/shard_map/ppermute | solution.py:25
  53.7 5.1 %collective-permute-start.15 = (bf16[4,3,128,128]{3,2,1,0:T(8,128)(2,1)}, bf16[4,3,128,128]{3,2,1,0:T(8,128)(2,1)S(1)}, u32[]{:S(2)}, u32[]{:S(2)}) collective-permute-start(bf16[4,3,128,128]{3,2,1,0:T(8,128)(2,1)} %get-tuple-element.4.rest_0_), channel_id=1, source_target_pairs={{0,6},{1,7},{2,0},{3,1},{4,2},{5,3},{6,4},{7,5},{8,14},{9,15},{10,... | collective-permute-start | bytes 1179656 | tf_op jit(solution)/shard_map/ppermute | solution.py:25
  58.8 2.1 %collective-permute-done.9.rest_1_ = bf16[4,3,128,128]{3,2,1,0:T(8,128)(2,1)S(1)} collective-permute-done((bf16[4,3,128,128]{3,2,1,0:T(8,128)(2,1)}, bf16[4,3,128,128]{3,2,1,0:T(8,128)(2,1)S(1)}, u32[]{:S(2)}, u32[]{:S(2)}) %collective-permute-start.9) | collective-permute-done | bytes 393248 | tf_op jit(solution)/shard_map/ppermute | solution.py:25
  60.9 1.9 %collective-permute-start.14 = (bf16[4,3,128,128]{3,2,1,0:T(8,128)(2,1)S(1)}, bf16[4,3,128,128]{3,2,1,0:T(8,128)(2,1)S(1)}, u32[]{:S(2)}, u32[]{:S(2)}) collective-permute-start(bf16[4,3,128,128]{3,2,1,0:T(8,128)(2,1)S(1)} %collective-permute-done.9.rest_1_), channel_id=1, source_target_pairs={{0,4},{1,5},{2,6},{3,7},{4,0},{5,1},{6,2},{7,3},{8,12},{9,13},{10,... | collective-permute-start | bytes 1179656 | tf_op jit(solution)/shard_map/ppermute | solution.py:25
  62.8 3.0 %collective-permute-start.13 = (bf16[4,3,128,128]{3,2,1,0:T(8,128)(2,1)S(1)}, bf16[4,3,128,128]{3,2,1,0:T(8,128)(2,1)S(1)}, u32[]{:S(2)}, u32[]{:S(2)}) collective-permute-start(bf16[4,3,128,128]{3,2,1,0:T(8,128)(2,1)S(1)} %collective-permute-done.9.rest_1_), channel_id=1, source_target_pairs={{0,6},{1,7},{2,0},{3,1},{4,2},{5,3},{6,4},{7,5},{8,14},{9,15},{10,... | collective-permute-start | bytes 1179656 | tf_op jit(solution)/shard_map/ppermute | solution.py:25
  65.8 11.0 %collective-permute-start.12 = (bf16[4,3,128,128]{3,2,1,0:T(8,128)(2,1)S(1)}, bf16[4,3,128,128]{3,2,1,0:T(8,128)(2,1)S(1)}, u32[]{:S(2)}, u32[]{:S(2)}) collective-permute-start(bf16[4,3,128,128]{3,2,1,0:T(8,128)(2,1)S(1)} %collective-permute-done.10.rest_2_), channel_id=1, source_target_pairs={{0,1},{1,0},{2,3},{3,2},{4,5},{5,4},{6,7},{7,6},{8,9},{9,8},{10,11... | collective-permute-start | bytes 1179656 | tf_op jit(solution)/shard_map/ppermute | solution.py:25
  76.9 1.9 %collective-permute-start.11 = (bf16[4,3,128,128]{3,2,1,0:T(8,128)(2,1)S(1)}, bf16[4,3,128,128]{3,2,1,0:T(8,128)(2,1)S(1)}, u32[]{:S(2)}, u32[]{:S(2)}) collective-permute-start(bf16[4,3,128,128]{3,2,1,0:T(8,128)(2,1)S(1)} %collective-permute-done.10.rest_2_), channel_id=1, source_target_pairs={{0,2},{1,3},{2,4},{3,5},{4,6},{5,7},{6,0},{7,1},{8,10},{9,11},{10,... | collective-permute-start | bytes 1179656 | tf_op jit(solution)/shard_map/ppermute | solution.py:25
  79.8 1.7 %cube_products.2.rest_5_ = f32[4,3,128,128]{3,2,1,0:T(8,128)S(1)} custom-call(s32[24,128]{1,0:T(8,128)S(1)} %pass_table.3.table, bf16[4,3,128,128]{3,2,1,0:T(8,128)(2,1)S(1)} %copy-done.3, bf16[4,3,128,128]{3,2,1,0:T(8,128)(2,1)S(1)} %collective-permute-done.9.rest_1_, bf16[4,3,128,128]{3,2,1,0:T(8,128)(2,1)S(1)} %collective-permute-done.10.rest_2_, ...), custom_call_target="tpu_custom_call" | custom-call | flops 8000000000 | bytes 6000000 | tf_op jit(solution)/shard_map/cube_products/pallas_call | solution.py:218
  82.6 5.1 %collective-permute-done.11.rest_0_ = bf16[4,3,128,128]{3,2,1,0:T(8,128)(2,1)S(1)} collective-permute-done((bf16[4,3,128,128]{3,2,1,0:T(8,128)(2,1)S(1)}, bf16[4,3,128,128]{3,2,1,0:T(8,128)(2,1)S(1)}, u32[]{:S(2)}, u32[]{:S(2)}) %collective-permute-start.11) | collective-permute-done | bytes 393248 | tf_op jit(solution)/shard_map/ppermute | solution.py:25
  87.8 2.5 %cube_products.3 = bf16[4,3,128,128]{3,2,1,0:T(8,128)(2,1)} custom-call(s32[24,128]{1,0:T(8,128)S(1)} %pass_table.3.table, bf16[4,3,128,128]{3,2,1,0:T(8,128)(2,1)S(1)} %collective-permute-done.11.rest_0_, bf16[4,3,128,128]{3,2,1,0:T(8,128)(2,1)S(1)} %collective-permute-done.12.rest_1_, bf16[4,3,128,128]{3,2,1,0:T(8,128)(2,1)S(1)} %collective-permute-done.13.rest_2_, ...), custom_call_target="tpu_custom_call" | custom-call | flops 600000000 | bytes 6000000 | tf_op jit(solution)/shard_map/cube_products/pallas_call | solution.py:218
  (23 shorter events, 6.1 us)
Async XLA Ops:
  1.7 18.4 %collective-permute-start.3 = (bf16[4,3,128,128]{3,2,1,0:T(8,128)(2,1)S(1)}, bf16[4,3,128,128]{3,2,1,0:T(8,128)(2,1)S(1)}, u32[]{:S(2)}, u32[]{:S(2)}) collective-permute-start(bf16[4,3,128,128]{3,2,1,0:T(8,128)(2,1)S(1)} %slice_bitcast_fusion.rest_0_), channel_id=1, source_target_pairs={{0,1},{1,0},{2,3},{3,2},{4,5},{5,4},{6,7},{7,6},{8,9},{9,8},{10,11... | collective-permute-start | bytes 1179656 | tf_op jit(solution)/shard_map/ppermute | solution.py:25
  5.1 17.0 %collective-permute-start.1 = (bf16[4,3,128,128]{3,2,1,0:T(8,128)(2,1)S(1)}, bf16[4,3,128,128]{3,2,1,0:T(8,128)(2,1)S(1)}, u32[]{:S(2)}, u32[]{:S(2)}) collective-permute-start(bf16[4,3,128,128]{3,2,1,0:T(8,128)(2,1)S(1)} %slice_bitcast_fusion.rest_0_), channel_id=1, source_target_pairs={{0,2},{1,3},{2,4},{3,5},{4,6},{5,7},{6,0},{7,1},{8,10},{9,11},{10,... | collective-permute-start | bytes 1179656 | tf_op jit(solution)/shard_map/ppermute | solution.py:25
  8.6 17.4 %collective-permute-start = (bf16[4,3,128,128]{3,2,1,0:T(8,128)(2,1)S(1)}, bf16[4,3,128,128]{3,2,1,0:T(8,128)(2,1)S(1)}, u32[]{:S(2)}, u32[]{:S(2)}) collective-permute-start(bf16[4,3,128,128]{3,2,1,0:T(8,128)(2,1)S(1)} %slice_bitcast_fusion.rest_0_), channel_id=1, source_target_pairs={{0,6},{1,7},{2,0},{3,1},{4,2},{5,3},{6,4},{7,5},{8,14},{9,15},{10,... | collective-permute-start | bytes 1179656 | tf_op jit(solution)/shard_map/ppermute | solution.py:25
  12.1 31.9 %collective-permute-start.8 = (bf16[48,128,128]{2,1,0:T(8,128)(2,1)}, bf16[48,128,128]{2,1,0:T(8,128)(2,1)S(1)}, u32[]{:S(2)}, u32[]{:S(2)}) collective-permute-start(bf16[48,128,128]{2,1,0:T(8,128)(2,1)} %bitcast.9), channel_id=1, source_target_pairs={{0,8},{8,0},{16,24},{24,16},{32,40},{40,32},{48,56},{56,48},{64,72... | collective-permute-start | bytes 4718600 | tf_op jit(solution)/shard_map/ppermute | solution.py:235
  14.1 30.0 %collective-permute-start.7 = (bf16[48,128,128]{2,1,0:T(8,128)(2,1)}, bf16[48,128,128]{2,1,0:T(8,128)(2,1)S(1)}, u32[]{:S(2)}, u32[]{:S(2)}) collective-permute-start(bf16[48,128,128]{2,1,0:T(8,128)(2,1)} %bitcast.10), channel_id=1, source_target_pairs={{8,16},{16,8},{24,32},{32,24},{40,48},{48,40},{56,64},{64,56},{72,... | collective-permute-start | bytes 4718600 | tf_op jit(solution)/shard_map/ppermute | solution.py:235
  20.1 10.8 %collective-permute-start.5 = (bf16[4,3,128,128]{3,2,1,0:T(8,128)(2,1)S(1)}, bf16[4,3,128,128]{3,2,1,0:T(8,128)(2,1)S(1)}, u32[]{:S(2)}, u32[]{:S(2)}) collective-permute-start(bf16[4,3,128,128]{3,2,1,0:T(8,128)(2,1)S(1)} %collective-permute-done.3.rest_0_.rest_1_), channel_id=1, source_target_pairs={{0,6},{1,7},{2,0},{3,1},{4,2},{5,3},{6,4},{7,5},{8,14},{9,15},{10,... | collective-permute-start | bytes 1179656 | tf_op jit(solution)/shard_map/ppermute | solution.py:25
  22.0 15.2 %collective-permute-start.4 = (bf16[4,3,128,128]{3,2,1,0:T(8,128)(2,1)S(1)}, bf16[4,3,128,128]{3,2,1,0:T(8,128)(2,1)S(1)}, u32[]{:S(2)}, u32[]{:S(2)}) collective-permute-start(bf16[4,3,128,128]{3,2,1,0:T(8,128)(2,1)S(1)} %collective-permute-done.3.rest_0_.rest_1_), channel_id=1, source_target_pairs={{0,2},{1,3},{2,4},{3,5},{4,6},{5,7},{6,0},{7,1},{8,10},{9,11},{10,... | collective-permute-start | bytes 1179656 | tf_op jit(solution)/shard_map/ppermute | solution.py:25
  26.0 18.0 %collective-permute-start.2 = (bf16[4,3,128,128]{3,2,1,0:T(8,128)(2,1)S(1)}, bf16[4,3,128,128]{3,2,1,0:T(8,128)(2,1)S(1)}, u32[]{:S(2)}, u32[]{:S(2)}) collective-permute-start(bf16[4,3,128,128]{3,2,1,0:T(8,128)(2,1)S(1)} %collective-permute-done.1.rest_1_.rest_2_), channel_id=1, source_target_pairs={{0,2},{1,3},{2,4},{3,5},{4,6},{5,7},{6,0},{7,1},{8,10},{9,11},{10,... | collective-permute-start | bytes 1179656 | tf_op jit(solution)/shard_map/ppermute | solution.py:25
  27.9 0.9 copy-start.1
  28.8 0.7 copy-start.2
  30.9 13.1 %collective-permute-start.6 = (bf16[4,3,128,128]{3,2,1,0:T(8,128)(2,1)S(1)}, bf16[4,3,128,128]{3,2,1,0:T(8,128)(2,1)S(1)}, u32[]{:S(2)}, u32[]{:S(2)}) collective-permute-start(bf16[4,3,128,128]{3,2,1,0:T(8,128)(2,1)S(1)} %collective-permute-done.5.rest_5_.rest_6_), channel_id=1, source_target_pairs={{0,6},{1,7},{2,0},{3,1},{4,2},{5,3},{6,4},{7,5},{8,14},{9,15},{10,... | collective-permute-start | bytes 1179656 | tf_op jit(solution)/shard_map/ppermute | solution.py:25
  44.0 1.4 %copy-start = (bf16[16,3,128,128]{3,2,1,0:T(8,128)(2,1)S(1)}, bf16[16,3,128,128]{3,2,1,0:T(8,128)(2,1)}, u32[]{:S(2)}) copy-start(bf16[16,3,128,128]{3,2,1,0:T(8,128)(2,1)} %param.3) | copy-start | bytes 4718596
  49.3 11.6 %collective-permute-start.9 = (bf16[4,3,128,128]{3,2,1,0:T(8,128)(2,1)}, bf16[4,3,128,128]{3,2,1,0:T(8,128)(2,1)S(1)}, u32[]{:S(2)}, u32[]{:S(2)}) collective-permute-start(bf16[4,3,128,128]{3,2,1,0:T(8,128)(2,1)} %get-tuple-element.4.rest_0_), channel_id=1, source_target_pairs={{0,1},{1,0},{2,3},{3,2},{4,5},{5,4},{6,7},{7,6},{8,9},{9,8},{10,11... | collective-permute-start | bytes 1179656 | tf_op jit(solution)/shard_map/ppermute | solution.py:25
  51.7 14.1 %collective-permute-start.10 = (bf16[4,3,128,128]{3,2,1,0:T(8,128)(2,1)}, bf16[4,3,128,128]{3,2,1,0:T(8,128)(2,1)S(1)}, u32[]{:S(2)}, u32[]{:S(2)}) collective-permute-start(bf16[4,3,128,128]{3,2,1,0:T(8,128)(2,1)} %get-tuple-element.4.rest_0_), channel_id=1, source_target_pairs={{0,2},{1,3},{2,4},{3,5},{4,6},{5,7},{6,0},{7,1},{8,10},{9,11},{10,... | collective-permute-start | bytes 1179656 | tf_op jit(solution)/shard_map/ppermute | solution.py:25
  53.7 25.1 %collective-permute-start.15 = (bf16[4,3,128,128]{3,2,1,0:T(8,128)(2,1)}, bf16[4,3,128,128]{3,2,1,0:T(8,128)(2,1)S(1)}, u32[]{:S(2)}, u32[]{:S(2)}) collective-permute-start(bf16[4,3,128,128]{3,2,1,0:T(8,128)(2,1)} %get-tuple-element.4.rest_0_), channel_id=1, source_target_pairs={{0,6},{1,7},{2,0},{3,1},{4,2},{5,3},{6,4},{7,5},{8,14},{9,15},{10,... | collective-permute-start | bytes 1179656 | tf_op jit(solution)/shard_map/ppermute | solution.py:25
  60.9 26.8 %collective-permute-start.14 = (bf16[4,3,128,128]{3,2,1,0:T(8,128)(2,1)S(1)}, bf16[4,3,128,128]{3,2,1,0:T(8,128)(2,1)S(1)}, u32[]{:S(2)}, u32[]{:S(2)}) collective-permute-start(bf16[4,3,128,128]{3,2,1,0:T(8,128)(2,1)S(1)} %collective-permute-done.9.rest_1_), channel_id=1, source_target_pairs={{0,4},{1,5},{2,6},{3,7},{4,0},{5,1},{6,2},{7,3},{8,12},{9,13},{10,... | collective-permute-start | bytes 1179656 | tf_op jit(solution)/shard_map/ppermute | solution.py:25
  62.8 24.9 %collective-permute-start.13 = (bf16[4,3,128,128]{3,2,1,0:T(8,128)(2,1)S(1)}, bf16[4,3,128,128]{3,2,1,0:T(8,128)(2,1)S(1)}, u32[]{:S(2)}, u32[]{:S(2)}) collective-permute-start(bf16[4,3,128,128]{3,2,1,0:T(8,128)(2,1)S(1)} %collective-permute-done.9.rest_1_), channel_id=1, source_target_pairs={{0,6},{1,7},{2,0},{3,1},{4,2},{5,3},{6,4},{7,5},{8,14},{9,15},{10,... | collective-permute-start | bytes 1179656 | tf_op jit(solution)/shard_map/ppermute | solution.py:25
  65.8 16.8 %collective-permute-start.12 = (bf16[4,3,128,128]{3,2,1,0:T(8,128)(2,1)S(1)}, bf16[4,3,128,128]{3,2,1,0:T(8,128)(2,1)S(1)}, u32[]{:S(2)}, u32[]{:S(2)}) collective-permute-start(bf16[4,3,128,128]{3,2,1,0:T(8,128)(2,1)S(1)} %collective-permute-done.10.rest_2_), channel_id=1, source_target_pairs={{0,1},{1,0},{2,3},{3,2},{4,5},{5,4},{6,7},{7,6},{8,9},{9,8},{10,11... | collective-permute-start | bytes 1179656 | tf_op jit(solution)/shard_map/ppermute | solution.py:25
  76.9 10.9 %collective-permute-start.11 = (bf16[4,3,128,128]{3,2,1,0:T(8,128)(2,1)S(1)}, bf16[4,3,128,128]{3,2,1,0:T(8,128)(2,1)S(1)}, u32[]{:S(2)}, u32[]{:S(2)}) collective-permute-start(bf16[4,3,128,128]{3,2,1,0:T(8,128)(2,1)S(1)} %collective-permute-done.10.rest_2_), channel_id=1, source_target_pairs={{0,2},{1,3},{2,4},{3,5},{4,6},{5,7},{6,0},{7,1},{8,10},{9,11},{10,... | collective-permute-start | bytes 1179656 | tf_op jit(solution)/shard_map/ppermute | solution.py:25
  78.8 1.0 %copy-start.3 = (bf16[4,3,128,128]{3,2,1,0:T(8,128)(2,1)S(1)}, bf16[4,3,128,128]{3,2,1,0:T(8,128)(2,1)}, u32[]{:S(2)}) copy-start(bf16[4,3,128,128]{3,2,1,0:T(8,128)(2,1)} %get-tuple-element.4.rest_0_) | copy-start | bytes 1179652

commit v8 on v7

--- a/solution.py
+++ b/solution.py
@@ -124,7 +124,7 @@
 COST = pl.CostEstimate(flops=600_000_000, bytes_accessed=6_000_000, transcendentals=0)
 
 
-def add_products(stage, sources, window, slots, table, lefts, ext, start, out_ref):
+def add_products(stage, sources, window, slots, table, lefts, ext, start, out_ref, before=None):
     capacity = len(lefts) * slots
     size = out_ref.shape[2]
     pair = 2
@@ -136,6 +136,8 @@
         source = lax.rem(y_at + (dy + Y), Y) * 2 + lax.rem(x_at + dx, 2)
         entry += [source * slots + s for s in range(slots)]
     for g in range(window):
+        if g == 1 and before is not None:
+            before()
         total = [None if start is None else start[g, q] for q in range(slots)]
         for e in range(0, capacity, pair):
             near = range(e, min(e + pair, capacity))
@@ -172,14 +174,19 @@
         copies = [pltpu.make_async_copy(a, b, sem.at[i]) for i, (a, b) in enumerate(copies)]
         for copy in copies:
             copy.start()
-        for copy in copies:
+        for copy in copies[:2]:
             copy.wait()
+
+    def wait_above():
+        pltpu.make_async_copy(
+            chip.at[pl.ds(0, tail)], ext.at[pl.ds(2 * rows, tail)], sem.at[2]
+        ).wait()
 
     for s in range(slots):
         ext[ext.shape[0] - slots + s] = jnp.zeros(ext.shape[1:], ext.dtype)
     pl.when(even)(lambda: lay_out(next_chip, chip))
     pl.when(jnp.logical_not(even))(lambda: lay_out(chip, next_chip))
-    add_products(0, SOURCES, window, slots, table, lefts, ext, None, out_ref)
+    add_products(0, SOURCES, window, slots, table, lefts, ext, None, out_ref, wait_above)
 
 
 def next_kernel(sources, window, slots, table, *rest):

time: 90.9 us -> 91.1 us (level)
  no operation moved by 1% of the time
where the time goes in v8:
time: 91.1 us; the launch traced here: 90.4 us
  starting transfers between devices  58.4 us (64%)
  waiting for transfers between devices  17.2 us (19%)
  Pallas kernels  8.94 us (10%)
  local copies, waits for them, and re-layouts  5.01 us (5%)
    ppermute x14, starting transfers between devices, moved(): return lax.ppermute(a, 'narrow', pairs)  50.4 us
    ppermute x14, waiting for transfers between devices, moved(): return lax.ppermute(a, 'narrow', pairs)  17.2 us
    ppermute x2, starting transfers between devices, swapped(): return lax.ppermute(x, axis, pairs)  7.94 us
    pallas_call x2, Pallas kernels, multiply(): pl.pallas_call(functools.partial(next_kernel, sources, window, slots), ou...  4.21 us
    unnamed x8, local copies, waits for them, and re-layouts  3.98 us
    pallas_call x1, Pallas kernels, multiply_first(): pl.pallas_call(functools.partial(first_kernel, window, slots), out_shape=...  3.98 us
  transfers between devices with their start and end apart: 16, of which 6 were waited for; matrix products, arithmetic and copies ran while one was open for 0% of the time, Pallas kernels for 3%

profile of v8, /device:TPU:32, one launch (start us, length us, event | category | flops | bytes accessed | tf_op | source)
XLA Modules:
  0.0 90.4 jit_solution(603158502763111079)
XLA Ops:
  1.7 3.4 %collective-permute-start.3 = (bf16[4,3,128,128]{3,2,1,0:T(8,128)(2,1)S(1)}, bf16[4,3,128,128]{3,2,1,0:T(8,128)(2,1)S(1)}, u32[]{:S(2)}, u32[]{:S(2)}) collective-permute-start(bf16[4,3,128,128]{3,2,1,0:T(8,128)(2,1)S(1)} %slice_bitcast_fusion.rest_0_), channel_id=1, source_target_pairs={{0,1},{1,0},{2,3},{3,2},{4,5},{5,4},{6,7},{7,6},{8,9},{9,8},{10,11... | collective-permute-start | bytes 1179656 | tf_op jit(solution)/shard_map/ppermute | solution.py:25
  5.1 3.5 %collective-permute-start.1 = (bf16[4,3,128,128]{3,2,1,0:T(8,128)(2,1)S(1)}, bf16[4,3,128,128]{3,2,1,0:T(8,128)(2,1)S(1)}, u32[]{:S(2)}, u32[]{:S(2)}) collective-permute-start(bf16[4,3,128,128]{3,2,1,0:T(8,128)(2,1)S(1)} %slice_bitcast_fusion.rest_0_), channel_id=1, source_target_pairs={{0,2},{1,3},{2,4},{3,5},{4,6},{5,7},{6,0},{7,1},{8,10},{9,11},{10,... | collective-permute-start | bytes 1179656 | tf_op jit(solution)/shard_map/ppermute | solution.py:25
  8.6 3.6 %collective-permute-start = (bf16[4,3,128,128]{3,2,1,0:T(8,128)(2,1)S(1)}, bf16[4,3,128,128]{3,2,1,0:T(8,128)(2,1)S(1)}, u32[]{:S(2)}, u32[]{:S(2)}) collective-permute-start(bf16[4,3,128,128]{3,2,1,0:T(8,128)(2,1)S(1)} %slice_bitcast_fusion.rest_0_), channel_id=1, source_target_pairs={{0,6},{1,7},{2,0},{3,1},{4,2},{5,3},{6,4},{7,5},{8,14},{9,15},{10,... | collective-permute-start | bytes 1179656 | tf_op jit(solution)/shard_map/ppermute | solution.py:25
  12.1 1.9 %collective-permute-start.8 = (bf16[48,128,128]{2,1,0:T(8,128)(2,1)}, bf16[48,128,128]{2,1,0:T(8,128)(2,1)S(1)}, u32[]{:S(2)}, u32[]{:S(2)}) collective-permute-start(bf16[48,128,128]{2,1,0:T(8,128)(2,1)} %bitcast.9), channel_id=1, source_target_pairs={{0,8},{8,0},{16,24},{24,16},{32,40},{40,32},{48,56},{56,48},{64,72... | collective-permute-start | bytes 4718600 | tf_op jit(solution)/shard_map/ppermute | solution.py:242
  14.1 6.0 %collective-permute-start.7 = (bf16[48,128,128]{2,1,0:T(8,128)(2,1)}, bf16[48,128,128]{2,1,0:T(8,128)(2,1)S(1)}, u32[]{:S(2)}, u32[]{:S(2)}) collective-permute-start(bf16[48,128,128]{2,1,0:T(8,128)(2,1)} %bitcast.10), channel_id=1, source_target_pairs={{8,16},{16,8},{24,32},{32,24},{40,48},{48,40},{56,64},{64,56},{72,... | collective-permute-start | bytes 4718600 | tf_op jit(solution)/shard_map/ppermute | solution.py:242
  20.1 1.9 %collective-permute-start.5 = (bf16[4,3,128,128]{3,2,1,0:T(8,128)(2,1)S(1)}, bf16[4,3,128,128]{3,2,1,0:T(8,128)(2,1)S(1)}, u32[]{:S(2)}, u32[]{:S(2)}) collective-permute-start(bf16[4,3,128,128]{3,2,1,0:T(8,128)(2,1)S(1)} %collective-permute-done.3.rest_0_.rest_1_), channel_id=1, source_target_pairs={{0,6},{1,7},{2,0},{3,1},{4,2},{5,3},{6,4},{7,5},{8,14},{9,15},{10,... | collective-permute-start | bytes 1179656 | tf_op jit(solution)/shard_map/ppermute | solution.py:25
  22.0 3.9 %collective-permute-start.4 = (bf16[4,3,128,128]{3,2,1,0:T(8,128)(2,1)S(1)}, bf16[4,3,128,128]{3,2,1,0:T(8,128)(2,1)S(1)}, u32[]{:S(2)}, u32[]{:S(2)}) collective-permute-start(bf16[4,3,128,128]{3,2,1,0:T(8,128)(2,1)S(1)} %collective-permute-done.3.rest_0_.rest_1_), channel_id=1, source_target_pairs={{0,2},{1,3},{2,4},{3,5},{4,6},{5,7},{6,0},{7,1},{8,10},{9,11},{10,... | collective-permute-start | bytes 1179656 | tf_op jit(solution)/shard_map/ppermute | solution.py:25
  26.0 1.9 %collective-permute-start.2 = (bf16[4,3,128,128]{3,2,1,0:T(8,128)(2,1)S(1)}, bf16[4,3,128,128]{3,2,1,0:T(8,128)(2,1)S(1)}, u32[]{:S(2)}, u32[]{:S(2)}) collective-permute-start(bf16[4,3,128,128]{3,2,1,0:T(8,128)(2,1)S(1)} %collective-permute-done.1.rest_1_.rest_2_), channel_id=1, source_target_pairs={{0,2},{1,3},{2,4},{3,5},{4,6},{5,7},{6,0},{7,1},{8,10},{9,11},{10,... | collective-permute-start | bytes 1179656 | tf_op jit(solution)/shard_map/ppermute | solution.py:25
  30.9 4.9 %collective-permute-start.6 = (bf16[4,3,128,128]{3,2,1,0:T(8,128)(2,1)S(1)}, bf16[4,3,128,128]{3,2,1,0:T(8,128)(2,1)S(1)}, u32[]{:S(2)}, u32[]{:S(2)}) collective-permute-start(bf16[4,3,128,128]{3,2,1,0:T(8,128)(2,1)S(1)} %collective-permute-done.5.rest_5_.rest_6_), channel_id=1, source_target_pairs={{0,6},{1,7},{2,0},{3,1},{4,2},{5,3},{6,4},{7,5},{8,14},{9,15},{10,... | collective-permute-start | bytes 1179656 | tf_op jit(solution)/shard_map/ppermute | solution.py:25
  35.9 1.3 %collective-permute-done.4.rest_2_.rest_4_.rest_5_ = bf16[4,3,128,128]{3,2,1,0:T(8,128)(2,1)S(1)} collective-permute-done((bf16[4,3,128,128]{3,2,1,0:T(8,128)(2,1)S(1)}, bf16[4,3,128,128]{3,2,1,0:T(8,128)(2,1)S(1)}, u32[]{:S(2)}, u32[]{:S(2)}) %collective-permute-start.4) | collective-permute-done | bytes 393248 | tf_op jit(solution)/shard_map/ppermute | solution.py:25
  37.2 6.8 %collective-permute-done.2.rest_1_.rest_3_.rest_4_ = bf16[4,3,128,128]{3,2,1,0:T(8,128)(2,1)S(1)} collective-permute-done((bf16[4,3,128,128]{3,2,1,0:T(8,128)(2,1)S(1)}, bf16[4,3,128,128]{3,2,1,0:T(8,128)(2,1)S(1)}, u32[]{:S(2)}, u32[]{:S(2)}) %collective-permute-start.2) | collective-permute-done | bytes 393248 | tf_op jit(solution)/shard_map/ppermute | solution.py:25
  44.1 1.4 %copy-done = bf16[16,3,128,128]{3,2,1,0:T(8,128)(2,1)S(1)} copy-done((bf16[16,3,128,128]{3,2,1,0:T(8,128)(2,1)S(1)}, bf16[16,3,128,128]{3,2,1,0:T(8,128)(2,1)}, u32[]{:S(2)}) %copy-start) | copy-done | bytes 1572888
  45.4 4.0 %square_products.1 = (bf16[4,3,128,128]{3,2,1,0:T(8,128)(2,1)}, bf16[135,128,128]{2,1,0:T(8,128)(2,1)S(1)}) custom-call(s32[24,128]{1,0:T(8,128)S(1)} %pass_table.3.table, bf16[4,3,128,128]{3,2,1,0:T(8,128)(2,1)S(1)} %slice_bitcast_fusion.rest_0_, bf16[4,3,128,128]{3,2,1,0:T(8,128)(2,1)S(1)} %collective-permute-done.3.rest_0_.rest_1_, ...), custom_call_target="tpu_custom_call" | custom-call | flops 600000000 | bytes 6000000 | tf_op jit(solution)/shard_map/square_products/pallas_call | solution.py:205
  49.4 2.4 %collective-permute-start.9 = (bf16[4,3,128,128]{3,2,1,0:T(8,128)(2,1)}, bf16[4,3,128,128]{3,2,1,0:T(8,128)(2,1)S(1)}, u32[]{:S(2)}, u32[]{:S(2)}) collective-permute-start(bf16[4,3,128,128]{3,2,1,0:T(8,128)(2,1)} %get-tuple-element.4.rest_0_), channel_id=1, source_target_pairs={{0,1},{1,0},{2,3},{3,2},{4,5},{5,4},{6,7},{7,6},{8,9},{9,8},{10,11... | collective-permute-start | bytes 1179656 | tf_op jit(solution)/shard_map/ppermute | solution.py:25
  51.9 1.9 %collective-permute-start.10 = (bf16[4,3,128,128]{3,2,1,0:T(8,128)(2,1)}, bf16[4,3,128,128]{3,2,1,0:T(8,128)(2,1)S(1)}, u32[]{:S(2)}, u32[]{:S(2)}) collective-permute-start(bf16[4,3,128,128]{3,2,1,0:T(8,128)(2,1)} %get-tuple-element.4.rest_0_), channel_id=1, source_target_pairs={{0,2},{1,3},{2,4},{3,5},{4,6},{5,7},{6,0},{7,1},{8,10},{9,11},{10,... | collective-permute-start | bytes 1179656 | tf_op jit(solution)/shard_map/ppermute | solution.py:25
  53.8 5.1 %collective-permute-start.15 = (bf16[4,3,128,128]{3,2,1,0:T(8,128)(2,1)}, bf16[4,3,128,128]{3,2,1,0:T(8,128)(2,1)S(1)}, u32[]{:S(2)}, u32[]{:S(2)}) collective-permute-start(bf16[4,3,128,128]{3,2,1,0:T(8,128)(2,1)} %get-tuple-element.4.rest_0_), channel_id=1, source_target_pairs={{0,6},{1,7},{2,0},{3,1},{4,2},{5,3},{6,4},{7,5},{8,14},{9,15},{10,... | collective-permute-start | bytes 1179656 | tf_op jit(solution)/shard_map/ppermute | solution.py:25
  58.9 2.1 %collective-permute-done.9.rest_1_ = bf16[4,3,128,128]{3,2,1,0:T(8,128)(2,1)S(1)} collective-permute-done((bf16[4,3,128,128]{3,2,1,0:T(8,128)(2,1)}, bf16[4,3,128,128]{3,2,1,0:T(8,128)(2,1)S(1)}, u32[]{:S(2)}, u32[]{:S(2)}) %collective-permute-start.9) | collective-permute-done | bytes 393248 | tf_op jit(solution)/shard_map/ppermute | solution.py:25
  61.1 1.9 %collective-permute-start.14 = (bf16[4,3,128,128]{3,2,1,0:T(8,128)(2,1)S(1)}, bf16[4,3,128,128]{3,2,1,0:T(8,128)(2,1)S(1)}, u32[]{:S(2)}, u32[]{:S(2)}) collective-permute-start(bf16[4,3,128,128]{3,2,1,0:T(8,128)(2,1)S(1)} %collective-permute-done.9.rest_1_), channel_id=1, source_target_pairs={{0,4},{1,5},{2,6},{3,7},{4,0},{5,1},{6,2},{7,3},{8,12},{9,13},{10,... | collective-permute-start | bytes 1179656 | tf_op jit(solution)/shard_map/ppermute | solution.py:25
  63.0 3.0 %collective-permute-start.13 = (bf16[4,3,128,128]{3,2,1,0:T(8,128)(2,1)S(1)}, bf16[4,3,128,128]{3,2,1,0:T(8,128)(2,1)S(1)}, u32[]{:S(2)}, u32[]{:S(2)}) collective-permute-start(bf16[4,3,128,128]{3,2,1,0:T(8,128)(2,1)S(1)} %collective-permute-done.9.rest_1_), channel_id=1, source_target_pairs={{0,6},{1,7},{2,0},{3,1},{4,2},{5,3},{6,4},{7,5},{8,14},{9,15},{10,... | collective-permute-start | bytes 1179656 | tf_op jit(solution)/shard_map/ppermute | solution.py:25
  66.0 11.0 %collective-permute-start.12 = (bf16[4,3,128,128]{3,2,1,0:T(8,128)(2,1)S(1)}, bf16[4,3,128,128]{3,2,1,0:T(8,128)(2,1)S(1)}, u32[]{:S(2)}, u32[]{:S(2)}) collective-permute-start(bf16[4,3,128,128]{3,2,1,0:T(8,128)(2,1)S(1)} %collective-permute-done.10.rest_2_), channel_id=1, source_target_pairs={{0,1},{1,0},{2,3},{3,2},{4,5},{5,4},{6,7},{7,6},{8,9},{9,8},{10,11... | collective-permute-start | bytes 1179656 | tf_op jit(solution)/shard_map/ppermute | solution.py:25
  77.0 1.9 %collective-permute-start.11 = (bf16[4,3,128,128]{3,2,1,0:T(8,128)(2,1)S(1)}, bf16[4,3,128,128]{3,2,1,0:T(8,128)(2,1)S(1)}, u32[]{:S(2)}, u32[]{:S(2)}) collective-permute-start(bf16[4,3,128,128]{3,2,1,0:T(8,128)(2,1)S(1)} %collective-permute-done.10.rest_2_), channel_id=1, source_target_pairs={{0,2},{1,3},{2,4},{3,5},{4,6},{5,7},{6,0},{7,1},{8,10},{9,11},{10,... | collective-permute-start | bytes 1179656 | tf_op jit(solution)/shard_map/ppermute | solution.py:25
  79.9 1.7 %cube_products.2.rest_5_ = f32[4,3,128,128]{3,2,1,0:T(8,128)S(1)} custom-call(s32[24,128]{1,0:T(8,128)S(1)} %pass_table.3.table, bf16[4,3,128,128]{3,2,1,0:T(8,128)(2,1)S(1)} %copy-done.3, bf16[4,3,128,128]{3,2,1,0:T(8,128)(2,1)S(1)} %collective-permute-done.9.rest_1_, bf16[4,3,128,128]{3,2,1,0:T(8,128)(2,1)S(1)} %collective-permute-done.10.rest_2_, ...), custom_call_target="tpu_custom_call" | custom-call | flops 8000000000 | bytes 6000000 | tf_op jit(solution)/shard_map/cube_products/pallas_call | solution.py:225
  82.7 5.1 %collective-permute-done.11.rest_0_ = bf16[4,3,128,128]{3,2,1,0:T(8,128)(2,1)S(1)} collective-permute-done((bf16[4,3,128,128]{3,2,1,0:T(8,128)(2,1)S(1)}, bf16[4,3,128,128]{3,2,1,0:T(8,128)(2,1)S(1)}, u32[]{:S(2)}, u32[]{:S(2)}) %collective-permute-start.11) | collective-permute-done | bytes 393248 | tf_op jit(solution)/shard_map/ppermute | solution.py:25
  87.9 2.5 %cube_products.3 = bf16[4,3,128,128]{3,2,1,0:T(8,128)(2,1)} custom-call(s32[24,128]{1,0:T(8,128)S(1)} %pass_table.3.table, bf16[4,3,128,128]{3,2,1,0:T(8,128)(2,1)S(1)} %collective-permute-done.11.rest_0_, bf16[4,3,128,128]{3,2,1,0:T(8,128)(2,1)S(1)} %collective-permute-done.12.rest_1_, bf16[4,3,128,128]{3,2,1,0:T(8,128)(2,1)S(1)} %collective-permute-done.13.rest_2_, ...), custom_call_target="tpu_custom_call" | custom-call | flops 600000000 | bytes 6000000 | tf_op jit(solution)/shard_map/cube_products/pallas_call | solution.py:225
  (23 shorter events, 6.1 us)
Async XLA Ops:
  1.7 18.4 %collective-permute-start.3 = (bf16[4,3,128,128]{3,2,1,0:T(8,128)(2,1)S(1)}, bf16[4,3,128,128]{3,2,1,0:T(8,128)(2,1)S(1)}, u32[]{:S(2)}, u32[]{:S(2)}) collective-permute-start(bf16[4,3,128,128]{3,2,1,0:T(8,128)(2,1)S(1)} %slice_bitcast_fusion.rest_0_), channel_id=1, source_target_pairs={{0,1},{1,0},{2,3},{3,2},{4,5},{5,4},{6,7},{7,6},{8,9},{9,8},{10,11... | collective-permute-start | bytes 1179656 | tf_op jit(solution)/shard_map/ppermute | solution.py:25
  5.1 17.0 %collective-permute-start.1 = (bf16[4,3,128,128]{3,2,1,0:T(8,128)(2,1)S(1)}, bf16[4,3,128,128]{3,2,1,0:T(8,128)(2,1)S(1)}, u32[]{:S(2)}, u32[]{:S(2)}) collective-permute-start(bf16[4,3,128,128]{3,2,1,0:T(8,128)(2,1)S(1)} %slice_bitcast_fusion.rest_0_), channel_id=1, source_target_pairs={{0,2},{1,3},{2,4},{3,5},{4,6},{5,7},{6,0},{7,1},{8,10},{9,11},{10,... | collective-permute-start | bytes 1179656 | tf_op jit(solution)/shard_map/ppermute | solution.py:25
  8.6 17.4 %collective-permute-start = (bf16[4,3,128,128]{3,2,1,0:T(8,128)(2,1)S(1)}, bf16[4,3,128,128]{3,2,1,0:T(8,128)(2,1)S(1)}, u32[]{:S(2)}, u32[]{:S(2)}) collective-permute-start(bf16[4,3,128,128]{3,2,1,0:T(8,128)(2,1)S(1)} %slice_bitcast_fusion.rest_0_), channel_id=1, source_target_pairs={{0,6},{1,7},{2,0},{3,1},{4,2},{5,3},{6,4},{7,5},{8,14},{9,15},{10,... | collective-permute-start | bytes 1179656 | tf_op jit(solution)/shard_map/ppermute | solution.py:25
  12.1 31.9 %collective-permute-start.8 = (bf16[48,128,128]{2,1,0:T(8,128)(2,1)}, bf16[48,128,128]{2,1,0:T(8,128)(2,1)S(1)}, u32[]{:S(2)}, u32[]{:S(2)}) collective-permute-start(bf16[48,128,128]{2,1,0:T(8,128)(2,1)} %bitcast.9), channel_id=1, source_target_pairs={{0,8},{8,0},{16,24},{24,16},{32,40},{40,32},{48,56},{56,48},{64,72... | collective-permute-start | bytes 4718600 | tf_op jit(solution)/shard_map/ppermute | solution.py:242
  14.1 30.0 %collective-permute-start.7 = (bf16[48,128,128]{2,1,0:T(8,128)(2,1)}, bf16[48,128,128]{2,1,0:T(8,128)(2,1)S(1)}, u32[]{:S(2)}, u32[]{:S(2)}) collective-permute-start(bf16[48,128,128]{2,1,0:T(8,128)(2,1)} %bitcast.10), channel_id=1, source_target_pairs={{8,16},{16,8},{24,32},{32,24},{40,48},{48,40},{56,64},{64,56},{72,... | collective-permute-start | bytes 4718600 | tf_op jit(solution)/shard_map/ppermute | solution.py:242
  20.1 10.8 %collective-permute-start.5 = (bf16[4,3,128,128]{3,2,1,0:T(8,128)(2,1)S(1)}, bf16[4,3,128,128]{3,2,1,0:T(8,128)(2,1)S(1)}, u32[]{:S(2)}, u32[]{:S(2)}) collective-permute-start(bf16[4,3,128,128]{3,2,1,0:T(8,128)(2,1)S(1)} %collective-permute-done.3.rest_0_.rest_1_), channel_id=1, source_target_pairs={{0,6},{1,7},{2,0},{3,1},{4,2},{5,3},{6,4},{7,5},{8,14},{9,15},{10,... | collective-permute-start | bytes 1179656 | tf_op jit(solution)/shard_map/ppermute | solution.py:25
  22.0 15.2 %collective-permute-start.4 = (bf16[4,3,128,128]{3,2,1,0:T(8,128)(2,1)S(1)}, bf16[4,3,128,128]{3,2,1,0:T(8,128)(2,1)S(1)}, u32[]{:S(2)}, u32[]{:S(2)}) collective-permute-start(bf16[4,3,128,128]{3,2,1,0:T(8,128)(2,1)S(1)} %collective-permute-done.3.rest_0_.rest_1_), channel_id=1, source_target_pairs={{0,2},{1,3},{2,4},{3,5},{4,6},{5,7},{6,0},{7,1},{8,10},{9,11},{10,... | collective-permute-start | bytes 1179656 | tf_op jit(solution)/shard_map/ppermute | solution.py:25
  26.0 18.0 %collective-permute-start.2 = (bf16[4,3,128,128]{3,2,1,0:T(8,128)(2,1)S(1)}, bf16[4,3,128,128]{3,2,1,0:T(8,128)(2,1)S(1)}, u32[]{:S(2)}, u32[]{:S(2)}) collective-permute-start(bf16[4,3,128,128]{3,2,1,0:T(8,128)(2,1)S(1)} %collective-permute-done.1.rest_1_.rest_2_), channel_id=1, source_target_pairs={{0,2},{1,3},{2,4},{3,5},{4,6},{5,7},{6,0},{7,1},{8,10},{9,11},{10,... | collective-permute-start | bytes 1179656 | tf_op jit(solution)/shard_map/ppermute | solution.py:25
  27.9 0.9 copy-start.1
  28.8 0.7 copy-start.2
  30.9 13.1 %collective-permute-start.6 = (bf16[4,3,128,128]{3,2,1,0:T(8,128)(2,1)S(1)}, bf16[4,3,128,128]{3,2,1,0:T(8,128)(2,1)S(1)}, u32[]{:S(2)}, u32[]{:S(2)}) collective-permute-start(bf16[4,3,128,128]{3,2,1,0:T(8,128)(2,1)S(1)} %collective-permute-done.5.rest_5_.rest_6_), channel_id=1, source_target_pairs={{0,6},{1,7},{2,0},{3,1},{4,2},{5,3},{6,4},{7,5},{8,14},{9,15},{10,... | collective-permute-start | bytes 1179656 | tf_op jit(solution)/shard_map/ppermute | solution.py:25
  44.0 1.4 %copy-start = (bf16[16,3,128,128]{3,2,1,0:T(8,128)(2,1)S(1)}, bf16[16,3,128,128]{3,2,1,0:T(8,128)(2,1)}, u32[]{:S(2)}) copy-start(bf16[16,3,128,128]{3,2,1,0:T(8,128)(2,1)} %param.3) | copy-start | bytes 4718596
  49.4 11.6 %collective-permute-start.9 = (bf16[4,3,128,128]{3,2,1,0:T(8,128)(2,1)}, bf16[4,3,128,128]{3,2,1,0:T(8,128)(2,1)S(1)}, u32[]{:S(2)}, u32[]{:S(2)}) collective-permute-start(bf16[4,3,128,128]{3,2,1,0:T(8,128)(2,1)} %get-tuple-element.4.rest_0_), channel_id=1, source_target_pairs={{0,1},{1,0},{2,3},{3,2},{4,5},{5,4},{6,7},{7,6},{8,9},{9,8},{10,11... | collective-permute-start | bytes 1179656 | tf_op jit(solution)/shard_map/ppermute | solution.py:25
  51.9 14.1 %collective-permute-start.10 = (bf16[4,3,128,128]{3,2,1,0:T(8,128)(2,1)}, bf16[4,3,128,128]{3,2,1,0:T(8,128)(2,1)S(1)}, u32[]{:S(2)}, u32[]{:S(2)}) collective-permute-start(bf16[4,3,128,128]{3,2,1,0:T(8,128)(2,1)} %get-tuple-element.4.rest_0_), channel_id=1, source_target_pairs={{0,2},{1,3},{2,4},{3,5},{4,6},{5,7},{6,0},{7,1},{8,10},{9,11},{10,... | collective-permute-start | bytes 1179656 | tf_op jit(solution)/shard_map/ppermute | solution.py:25
  53.8 25.1 %collective-permute-start.15 = (bf16[4,3,128,128]{3,2,1,0:T(8,128)(2,1)}, bf16[4,3,128,128]{3,2,1,0:T(8,128)(2,1)S(1)}, u32[]{:S(2)}, u32[]{:S(2)}) collective-permute-start(bf16[4,3,128,128]{3,2,1,0:T(8,128)(2,1)} %get-tuple-element.4.rest_0_), channel_id=1, source_target_pairs={{0,6},{1,7},{2,0},{3,1},{4,2},{5,3},{6,4},{7,5},{8,14},{9,15},{10,... | collective-permute-start | bytes 1179656 | tf_op jit(solution)/shard_map/ppermute | solution.py:25
  61.1 26.8 %collective-permute-start.14 = (bf16[4,3,128,128]{3,2,1,0:T(8,128)(2,1)S(1)}, bf16[4,3,128,128]{3,2,1,0:T(8,128)(2,1)S(1)}, u32[]{:S(2)}, u32[]{:S(2)}) collective-permute-start(bf16[4,3,128,128]{3,2,1,0:T(8,128)(2,1)S(1)} %collective-permute-done.9.rest_1_), channel_id=1, source_target_pairs={{0,4},{1,5},{2,6},{3,7},{4,0},{5,1},{6,2},{7,3},{8,12},{9,13},{10,... | collective-permute-start | bytes 1179656 | tf_op jit(solution)/shard_map/ppermute | solution.py:25
  63.0 24.9 %collective-permute-start.13 = (bf16[4,3,128,128]{3,2,1,0:T(8,128)(2,1)S(1)}, bf16[4,3,128,128]{3,2,1,0:T(8,128)(2,1)S(1)}, u32[]{:S(2)}, u32[]{:S(2)}) collective-permute-start(bf16[4,3,128,128]{3,2,1,0:T(8,128)(2,1)S(1)} %collective-permute-done.9.rest_1_), channel_id=1, source_target_pairs={{0,6},{1,7},{2,0},{3,1},{4,2},{5,3},{6,4},{7,5},{8,14},{9,15},{10,... | collective-permute-start | bytes 1179656 | tf_op jit(solution)/shard_map/ppermute | solution.py:25
  66.0 16.8 %collective-permute-start.12 = (bf16[4,3,128,128]{3,2,1,0:T(8,128)(2,1)S(1)}, bf16[4,3,128,128]{3,2,1,0:T(8,128)(2,1)S(1)}, u32[]{:S(2)}, u32[]{:S(2)}) collective-permute-start(bf16[4,3,128,128]{3,2,1,0:T(8,128)(2,1)S(1)} %collective-permute-done.10.rest_2_), channel_id=1, source_target_pairs={{0,1},{1,0},{2,3},{3,2},{4,5},{5,4},{6,7},{7,6},{8,9},{9,8},{10,11... | collective-permute-start | bytes 1179656 | tf_op jit(solution)/shard_map/ppermute | solution.py:25
  77.0 10.9 %collective-permute-start.11 = (bf16[4,3,128,128]{3,2,1,0:T(8,128)(2,1)S(1)}, bf16[4,3,128,128]{3,2,1,0:T(8,128)(2,1)S(1)}, u32[]{:S(2)}, u32[]{:S(2)}) collective-permute-start(bf16[4,3,128,128]{3,2,1,0:T(8,128)(2,1)S(1)} %collective-permute-done.10.rest_2_), channel_id=1, source_target_pairs={{0,2},{1,3},{2,4},{3,5},{4,6},{5,7},{6,0},{7,1},{8,10},{9,11},{10,... | collective-permute-start | bytes 1179656 | tf_op jit(solution)/shard_map/ppermute | solution.py:25
  78.9 1.0 %copy-start.3 = (bf16[4,3,128,128]{3,2,1,0:T(8,128)(2,1)S(1)}, bf16[4,3,128,128]{3,2,1,0:T(8,128)(2,1)}, u32[]{:S(2)}) copy-start(bf16[4,3,128,128]{3,2,1,0:T(8,128)(2,1)} %get-tuple-element.4.rest_0_) | copy-start | bytes 1179652
